TPU v7x, 32 devices: a whole 2x2x4 slice. The times are simulated.
32 devices in a mesh: query: 2 (over core), lib: 16 (over z, y, x).
Axes of the slice: x: 2, y: 2, z: 4, core: 2. Of those that a mesh axis runs over, the one named last changes fastest.
Arguments:
- queries: bfloat16 [1024, 2048], P(('query', 'lib')), may hold values from -64 to 64
- query_bucket: int32 [1024], P(('query', 'lib')), may hold values from 0 to 31, as said below
- library: bfloat16 [49152, 2048], P(('lib', 'query')), may hold values from -64 to 64
- library_time: bfloat16 [49152], P(('lib', 'query')), may hold values from 0 to 2
- library_bucket: int32 [49152], P(('lib', 'query')), may hold values from 0 to 31, as said below
Outputs:
- expected_spectra: bfloat16 [1024, 2048], P(('query', 'lib'))
- expected_time: float32 [1024], P(('query', 'lib'))
- log_evidence: float32 [1024], P(('query', 'lib'))
Inputs may be any that keep to these rules, and one draw needn't show every extreme that they name: `query_bucket`: library entries whose bucket differs from a query's by at most one are that query's candidates; the queries held by the devices at index i of lib lie in buckets 2 i and 2 i + 1. `library_bucket`: the library entries of every device hold each of the 32 buckets exactly 3072 // 64 times.
All inputs are finite; a program needn't handle non-finite values.
Results may differ from a plain program's by a relative error of at most 0.003.
Values may be sent and summed in bfloat16 or wider, within the bound.
No kernel may reach another device: no remote copies, remote signals or barrier semaphores. Data moves between devices by JAX's collectives and lax.ppermute only.
A program may use at most 128 MiB of HBM per device.

v0:
```python
import jax
import jax.numpy as jnp
from jax import lax
from jax.sharding import PartitionSpec as P

SHARPNESS = 448


def entry_scale(spectra_rows):
    return lax.rsqrt(jnp.mean(jnp.square(spectra_rows.astype(jnp.float32)), axis=1) + 1e-06)


def scaled_scores(query_block, query_scale, block_bucket, entries, entry_bucket):
    products = lax.dot_general(
        query_block, entries, (((1,), (1,)), ((), ())), preferred_element_type=jnp.float32
    )
    inside = jnp.abs(block_bucket[:, None] - entry_bucket[None, :]) <= 1
    return jnp.where(
        inside, products * query_scale[:, None] * entry_scale(entries)[None, :], -jnp.inf
    )


def finish(spectra_sum, totals, time_sum, own_maxima):
    expected = (spectra_sum / totals[:, None]).astype(jnp.bfloat16)
    return (expected, time_sum / totals, own_maxima + jnp.log(totals))


def per_device(queries, query_bucket, library, library_time, library_bucket):
    own_rows = queries.shape[0]
    bin_count = queries.shape[1]
    query_block, block_bucket = (
        lax.all_gather(queries, "lib", axis=0, tiled=True),
        lax.all_gather(query_bucket, "lib", axis=0, tiled=True),
    )
    query_scale = entry_scale(query_block) * (SHARPNESS / bin_count)
    entries, entry_time, entry_bucket = (
        lax.all_gather(library, "query", axis=0, tiled=True),
        lax.all_gather(library_time, "query", axis=0, tiled=True),
        lax.all_gather(library_bucket, "query", axis=0, tiled=True),
    )
    scores = scaled_scores(query_block, query_scale, block_bucket, entries, entry_bucket)
    maxima = lax.pmax(jnp.max(scores, axis=1), "lib")
    weights = jnp.exp(scores - maxima[:, None]).astype(jnp.bfloat16)
    total_part = jnp.sum(weights.astype(jnp.float32), axis=1)
    spectra_part = jnp.dot(weights, entries, preferred_element_type=jnp.float32)
    time_part = jnp.dot(weights, entry_time, preferred_element_type=jnp.float32)
    first_row = lax.axis_index("lib") * own_rows
    spectra_sum, totals, time_sum = (
        lax.psum_scatter(spectra_part, "lib", scatter_dimension=0, tiled=True),
        lax.psum_scatter(total_part, "lib", scatter_dimension=0, tiled=True),
        lax.psum_scatter(time_part, "lib", scatter_dimension=0, tiled=True),
    )
    own_maxima = lax.dynamic_slice_in_dim(maxima, first_row, own_rows)
    return finish(spectra_sum, totals, time_sum, own_maxima)


def solution(mesh):
    placed = (
        P(("query", "lib"), None),
        P(("query", "lib")),
        P(("lib", "query"), None),
        P(("lib", "query")),
        P(("lib", "query")),
    )
    return jax.shard_map(
        per_device,
        mesh=mesh,
        in_specs=placed,
        out_specs=(P(("query", "lib"), None), P(("query", "lib")), P(("query", "lib"))),
        check_vma=False,
    )
```

profile of v0, /device:TPU:0, one launch (start us, length us, event | category | flops | bytes accessed | tf_op | source)
XLA Modules:
  0.0 276.4 jit_solution(10963943871342219335)
XLA Ops:
  7.2 0.0 copy-start.3
  7.2 0.0 copy-start.1
  7.2 0.0 copy-start.4
  7.2 0.0 all-gather.5.cloned.1.call-start
  7.2 0.7 all-gather.5.cloned.1.call-update
  7.9 0.0 all-gather.7.cloned.1.call-start
  8.0 0.7 all-gather.7.cloned.1.call-update
  8.7 0.0 reduce-scatter.2.cloned.1.call-start
  8.7 0.0 copy-done.1
  8.8 0.0 copy-done.3
  8.8 0.6 fusion
  10.0 0.0 copy-done.4
  10.1 0.2 dynamic-update-slice
  10.3 16.2 %all-reduce = s32[512]{0:T(512)S(1)} all-reduce(s32[512]{0:T(512)S(1)} %dynamic-update-slice), channel_id=1, replica_groups=mesh['query'=2,'lib'=16] {'lib'}, use_global_device_ids=true, to_apply=%add | all-reduce | flops 512 | bytes 4096
  26.5 1.8 all-gather
  28.3 45.9 %all-gather.5.cloned.1.call-done = bf16[512,2048]{1,0:T(8,128)(2,1)} async-done(((bf16[32,2048]{1,0:T(8,128)(2,1)}), bf16[512,2048]{1,0:T(8,128)(2,1)}) %all-gather.5.cloned.1.call-update) | async-done | bytes 2097168 | tf_op jit(solution)/shard_map/all_gather | solution.py:32
  74.2 2.1 multiply_reduce_fusion.1
  76.3 23.1 %all-gather.7.cloned.1.call-done = bf16[3072,2048]{1,0:T(8,128)(2,1)} async-done(((bf16[1536,2048]{1,0:T(8,128)(2,1)}), bf16[3072,2048]{1,0:T(8,128)(2,1)}) %all-gather.7.cloned.1.call-update) | async-done | bytes 12582928 | tf_op jit(solution)/shard_map/all_gather | solution.py:37
  99.4 7.1 %multiply_reduce_fusion = f32[3072]{0:T(1024)S(1)} fusion(bf16[3072,2048]{1,0:T(8,128)(2,1)} %all-gather.7.cloned.1.call-done), kind=kLoop, calls=%fused_computation | loop fusion | flops 18871296 | bytes 12595200 | tf_op jit(solution)/shard_map/reduce_sum | solution.py:10
  106.5 12.1 %fusion.1 = (f32[512]{0:T(512)S(1)}, f32[512,3072]{1,0:T(8,128)}) fusion(f32[3072]{0:T(1024)S(1)} %add_rsqrt_fusion, f32[512]{0:T(512)S(1)} %rsqrt_multiply_fusion, bf16[512,2048]{1,0:T(8,128)(2,1)S(1)} %copy-done, bf16[3072,2048]{1,0:T(8,128)(2,1)} %all-gather.7.cloned.1.call-done, s32[3072]{0:T(1024)S(1)} %bitcast.13, s32[512]{0:T(512)S(1)} %all-reduce), kind=kOutput, calls=%fused_computation.12 | convolution fusion | flops 6453460480 | bytes 21002240 | tf_op jit(solution)/shard_map/dot_general | solution.py:14
  118.6 41.9 %pmax.7 = f32[512]{0:T(512)S(1)} all-reduce(f32[512]{0:T(512)S(1)} %get-tuple-element.11), channel_id=1, replica_groups=mesh['query'=2,'lib'=16] {'lib'}, use_global_device_ids=true, to_apply=%region_3.4 | all-reduce | flops 512 | bytes 4096 | tf_op jit(solution)/shard_map/pmax | solution.py:42
  160.5 3.8 %convert_reduce_fusion = (f32[512]{0:T(512)S(1)}, bf16[512,3072]{1,0:T(8,128)(2,1)S(1)}) fusion(f32[512,3072]{1,0:T(8,128)} %get-tuple-element.12, f32[512]{0:T(512)S(1)} %pmax.7), kind=kLoop, calls=%fused_computation.1 | loop fusion | flops 6290944 | bytes 9441280 | tf_op jit(solution)/shard_map/reduce_sum | solution.py:44
  164.4 10.9 %fusion.2 = f32[512,2048]{1,0:T(8,128)} fusion(bf16[512,3072]{1,0:T(8,128)(2,1)S(1)} %get-tuple-element.8, bf16[3072,2048]{1,0:T(8,128)(2,1)} %all-gather.7.cloned.1.call-done), kind=kOutput, calls=%fused_computation.13 | convolution fusion | flops 6442450944 | bytes 19922944 | tf_op jit(solution)/shard_map/dot_general | solution.py:45
  175.3 0.0 reduce-scatter.2.cloned.1.call-update
  175.4 0.0 copy-done.2
  176.0 1.8 all-gather.1
  177.8 0.9 fusion.3
  178.8 36.9 %all-reduce.3 = (f32[512]{0:T(512)S(1)}, f32[512]{0:T(512)S(1)}) all-reduce(f32[512]{0:T(512)S(1)} %get-tuple-element.7, f32[512]{0:T(512)S(1)} %bitcast.12), channel_id=3, replica_groups=mesh['query'=2,'lib'=16] {'lib'}, use_global_device_ids=true, to_apply=%region_6.7.clone | all-reduce | flops 1024 | bytes 8192
  215.7 0.6 log_add_fusion
  216.3 0.6 dynamic-slice_divide_fusion
  216.8 51.3 %reduce-scatter.2.cloned.1.call-done = f32[32,2048]{1,0:T(8,128)} async-done(((f32[512,2048]{1,0:T(8,128)}), f32[32,2048]{1,0:T(8,128)}) %reduce-scatter.2.cloned.1.call-update) | async-done | bytes 262160 | tf_op jit(solution)/shard_map/reduce_scatter | solution.py:49
  268.2 1.7 divide_convert_fusion
  (8 shorter events, 0.0 us)
Async XLA Ops:
  7.2 1.6 copy-start.3
  7.2 1.6 copy-start.1
  7.2 2.9 %copy-start.4 = (s32[32]{0:T(128)S(1)}, s32[32]{0:T(128)}, u32[]{:S(2)}) copy-start(s32[32]{0:T(128)} %param.6) | copy-start | bytes 388
  7.2 67.0 %all-gather.5.cloned.1.call-start = ((), (), s32[]{:S(2)}) async-start(), calls=%async_computation.1 | async-start | bytes 2228224 | tf_op jit(solution)/shard_map/all_gather | solution.py:32
  7.9 91.5 %all-gather.7.cloned.1.call-start = ((), (), s32[]{:S(2)}) async-start(), calls=%async_computation.2 | async-start | bytes 18874368 | tf_op jit(solution)/shard_map/all_gather | solution.py:37
  8.7 259.5 %reduce-scatter.2.cloned.1.call-start = ((), (), s32[]{:S(2)}) async-start(), calls=%async_computation.3 | async-start | bytes 4456448 | tf_op jit(solution)/shard_map/reduce_scatter | solution.py:49
  76.3 30.2 %copy-start = (bf16[512,2048]{1,0:T(8,128)(2,1)S(1)}, bf16[512,2048]{1,0:T(8,128)(2,1)}, u32[]{:S(2)}) copy-start(bf16[512,2048]{1,0:T(8,128)(2,1)} %all-gather.5.cloned.1.call-done) | copy-start | bytes 6291460
  164.4 11.0 %copy-start.2 = (bf16[1536]{0:T(1024)(128)(2,1)S(1)}, bf16[1536]{0:T(1024)(128)(2,1)}, u32[]{:S(2)}) copy-start(bf16[1536]{0:T(1024)(128)(2,1)} %param.8) | copy-start | bytes 9220
Sparse Core Ops, SparseCore 0:
  10.8 63.3 all-gather.4
  75.8 23.5 all-gather.6
  175.5 92.6 reduce-scatter.1
where the time goes:
time: 277 us; the launch traced here: 276 us
  waiting for transfers between devices  122 us (44%)
  blocking collectives  98.7 us (36%)
  matrix products  23.9 us (9%)
  other arithmetic  15.9 us (6%)
  between operations  15.2 us (5%)
    unnamed x2, blocking collectives  53.1 us
    reduce_scatter x1, waiting for transfers between devices, per_device(): lax.psum_scatter(spectra_part, 'lib', scatter_dimension=0, tiled=True)  51.3 us
    all_gather x1, waiting for transfers between devices, per_device(): lax.all_gather(queries, 'lib', axis=0, tiled=True)  45.9 us
    pmax x1, blocking collectives, per_device(): maxima = lax.pmax(jnp.max(scores, axis=1), 'lib')  41.9 us
    all_gather x1, waiting for transfers between devices, per_device(): lax.all_gather(library, 'query', axis=0, tiled=True)  23.1 us
    dot_general x1, matrix products, scaled_scores(): lax.dot_general(query_block, entries, (((1,), (1,)), ((), ())), preferred...  12.1 us
    dot_general x1, matrix products, per_device(): spectra_part = jnp.dot(weights, entries, preferred_element_type=jnp.float32)  10.9 us
    reduce_sum x2, other arithmetic, entry_scale(): jnp.mean(jnp.square(spectra_rows.astype(jnp.float32)), axis=1) + 1e-06  9.16 us
  transfers between devices with their start and end apart: 3, of which 3 were waited for; matrix products, arithmetic and copies ran while one was open for 2% of the time, Pallas kernels for 0%

commit v1 on v0

v1 whole, which is shorter than its diff:
```python
import functools
import math

import jax
import jax.numpy as jnp
from jax import lax
from jax.experimental import pallas as pl
from jax.experimental.pallas import tpu as pltpu
from jax.sharding import PartitionSpec as P

SHARPNESS = 448
EPSILON = 1e-06
LANES = 128
LOG2E = math.log2(math.e)
LN2 = math.log(2.0)
FRACTION_BITS = 14
SUM_BITS = 16
LOW_BITS = 15
MASKED = -1e30
NT = (((1,), (1,)), ((), ()))
MIB = 1 << 20


def sort_kernel(per_bucket, chunk, bucket_ref, time_ref, library_ref, sorted_ref, aux_ref):
    count, bins = library_ref.shape
    buckets = count // per_bucket
    before = (
        lax.broadcasted_iota(jnp.int32, (LANES, LANES), 0)
        < lax.broadcasted_iota(jnp.int32, (LANES, LANES), 1)
    ).astype(jnp.bfloat16)
    bucket_ids = lax.broadcasted_iota(jnp.int32, (buckets, LANES), 0)
    seen = (per_bucket * lax.broadcasted_iota(jnp.int32, (buckets, 1), 0)).astype(jnp.float32)
    places = []
    for at in range(0, count, LANES):
        member = bucket_ref[:, at : at + LANES] == bucket_ids
        member32 = member.astype(jnp.float32)
        earlier = jnp.dot(
            member32.astype(jnp.bfloat16), before, preferred_element_type=jnp.float32
        )
        places.append(jnp.sum(member32 * (earlier + seen), axis=0, keepdims=True))
        seen = seen + jnp.sum(member32, axis=1, keepdims=True)
    place = jnp.concatenate(places, axis=1).astype(jnp.int32)
    time_rows = jnp.broadcast_to(time_ref[...], (8, count)).astype(jnp.bfloat16)
    for at in range(0, count, chunk):
        rows = at + lax.broadcasted_iota(jnp.int32, (chunk, count), 0)
        chosen = (rows == place).astype(jnp.float32).astype(jnp.bfloat16)
        entries = jnp.dot(chosen, library_ref[...], preferred_element_type=jnp.float32)
        sorted_ref[at : at + chunk, :] = entries.astype(jnp.bfloat16)
        times = lax.dot_general(time_rows, chosen, NT, preferred_element_type=jnp.float32)
        mean = jnp.sum(entries * entries, axis=1, keepdims=True) / bins
        scale = jnp.broadcast_to(lax.rsqrt(mean + EPSILON), (chunk, LANES)).T[:8]
        bucket = ((at + lax.broadcasted_iota(jnp.int32, (8, chunk), 1)) // per_bucket).astype(
            jnp.float32
        )
        which = lax.broadcasted_iota(jnp.int32, (8, chunk), 0)
        aux_ref[:, at : at + chunk] = jnp.where(
            which == 0, scale, jnp.where(which == 1, times, bucket)
        )


def sort_library(library, library_time, library_bucket, per_bucket):
    count, bins = library.shape
    chunk = min(256, count)
    return pl.pallas_call(
        functools.partial(sort_kernel, per_bucket, chunk),
        out_shape=(
            jax.ShapeDtypeStruct((count, bins), jnp.bfloat16),
            jax.ShapeDtypeStruct((8, count), jnp.float32),
        ),
        compiler_params=pltpu.CompilerParams(vmem_limit_bytes=48 * MIB),
        cost_estimate=pl.CostEstimate(
            flops=2 * count * count * bins, bytes_accessed=4 * count * bins, transcendentals=0
        ),
        name="sort_library",
    )(library_bucket.reshape(1, count), library_time.astype(jnp.float32).reshape(1, count), library)


def encode(out, rows, vector, k, total, time_sum):
    bins = vector.shape[1]
    largest = jnp.maximum(jnp.max(jnp.abs(vector), axis=1, keepdims=True), 1e-30)
    e = jnp.ceil(jnp.log2(largest))
    coded = jnp.floor(vector * jnp.exp2(FRACTION_BITS - e) + 0.5).astype(jnp.int32)
    out[rows, :bins] = coded.astype(jnp.int16)
    lane = lax.broadcasted_iota(jnp.int32, (vector.shape[0], LANES), 1)
    total = (total * (1 << SUM_BITS) + 0.5).astype(jnp.int32)
    time_sum = (time_sum * (1 << SUM_BITS) + 0.5).astype(jnp.int32)
    low = (1 << LOW_BITS) - 1
    stats = jnp.zeros((vector.shape[0], LANES), jnp.int32)
    for at, value in enumerate(
        (k.astype(jnp.int32), e.astype(jnp.int32), total >> LOW_BITS, total & low, time_sum >> LOW_BITS, time_sum & low)
    ):
        stats = jnp.where(lane == at, value, stats)
    out[rows, bins:] = stats.astype(jnp.int16)


def merged(parts):
    bins = parts[0].shape[1] - LANES
    stats = [p[:, bins:].astype(jnp.int32).astype(jnp.float32) for p in parts]
    ks = [s[:, 0:1] for s in stats]
    k = functools.reduce(jnp.maximum, ks)
    high = float(1 << LOW_BITS)
    unit = 1.0 / (1 << SUM_BITS)
    vector = total = time_sum = 0.0
    for part, s, own in zip(parts, stats, ks):
        shift = jnp.exp2(own - k)
        total = total + (s[:, 2:3] * high + s[:, 3:4]) * (shift * unit)
        time_sum = time_sum + (s[:, 4:5] * high + s[:, 5:6]) * (shift * unit)
        factor = jnp.exp2(own - k + s[:, 1:2] - FRACTION_BITS)
        vector = vector + part[:, :bins].astype(jnp.int32).astype(jnp.float32) * factor
    return vector, k, total, time_sum


def merge_kernel(pieces, *refs):
    *parts, = refs[: len(refs) - pieces]
    outs = refs[len(refs) - pieces :]
    rows = parts[0].shape[0] // pieces
    for at, out in enumerate(outs):
        own = [p[at * rows : (at + 1) * rows, :] for p in parts]
        encode(out, slice(None), *merged(own))


def merge(parts, pieces):
    rows, width = parts[0].shape
    out = jax.ShapeDtypeStruct((rows // pieces, width), jnp.int16)
    return pl.pallas_call(
        functools.partial(merge_kernel, pieces),
        out_shape=(out,) * pieces,
        compiler_params=pltpu.CompilerParams(vmem_limit_bytes=32 * MIB),
        cost_estimate=pl.CostEstimate(
            flops=8 * rows * width * len(parts), bytes_accessed=2 * rows * width * (len(parts) + 1), transcendentals=0
        ),
        name="merge",
    )(*parts)


def finish_kernel(*refs):
    *parts, spectra_ref, time_ref, evidence_ref = refs
    vector, k, total, time_sum = merged([p[...] for p in parts])
    spectra_ref[...] = (vector / total).astype(jnp.bfloat16)
    shape = (total.shape[0], LANES)
    time_ref[...] = jnp.broadcast_to(time_sum / total, shape).T[:1]
    evidence_ref[...] = jnp.broadcast_to(k * LN2 + jnp.log(total), shape).T[:1]


def finish(parts):
    rows, width = parts[0].shape
    spectra, time, evidence = pl.pallas_call(
        finish_kernel,
        out_shape=(
            jax.ShapeDtypeStruct((rows, width - LANES), jnp.bfloat16),
            jax.ShapeDtypeStruct((1, rows), jnp.float32),
            jax.ShapeDtypeStruct((1, rows), jnp.float32),
        ),
        compiler_params=pltpu.CompilerParams(vmem_limit_bytes=32 * MIB),
        name="finish",
    )(*parts)
    return spectra, time.reshape(rows), evidence.reshape(rows)


def match_kernel(window, per_bucket, shards, base_ref, *refs):
    queries, refs = refs[:4], refs[4:]
    libraries, refs = refs[:shards], refs[shards:]
    auxes, refs = refs[:shards], refs[shards:]
    outs, refs = refs[:4], refs[4:]
    held, stacked, arrived = refs
    step = pl.program_id(0)
    steps = pl.num_programs(0)
    rows, width = queries[0].shape
    bins = width - LANES
    count = libraries[0].shape[0]

    def first_row(at):
        quad = base_ref[0] ^ at
        start = (quad * 8 - 1) * per_bucket // LANES * LANES
        return pl.multiple_of(jnp.clip(start, 0, count - window), LANES)

    def copies(at, slot):
        start = first_row(at)
        return [
            pltpu.make_async_copy(
                library.at[pl.ds(start, window), :],
                held.at[slot, pl.ds(s * window, window), :],
                arrived.at[slot, s],
            )
            for s, library in enumerate(libraries)
        ]

    @pl.when(step == 0)
    def _():
        for c in copies(0, 0):
            c.start()

    slot = lax.rem(step, 2)

    @pl.when(step + 1 < steps)
    def _():
        for c in copies(step + 1, 1 - slot):
            c.start()

    for v, q in enumerate(queries):
        stacked[v * rows : (v + 1) * rows, :] = q[...]
    mine = stacked[:, :bins]
    mine32 = mine.astype(jnp.float32)
    mean = jnp.sum(mine32 * mine32, axis=1, keepdims=True) / bins
    query_scale = lax.rsqrt(mean + EPSILON) * (SHARPNESS / bins)
    query_bucket = stacked[:, bins:].astype(jnp.float32)[:, 0:1]
    start = first_row(step)
    aux = jnp.concatenate([a[:, pl.ds(start, window)] for a in auxes], axis=1)

    for c in copies(step, slot):
        c.wait()
    entries = held.at[slot]
    products = lax.dot_general(mine, entries[...], NT, preferred_element_type=jnp.float32)
    scores = products * query_scale * aux[0:1] * LOG2E
    inside = jnp.abs(query_bucket - aux[2:3]) <= 1.0
    scores = jnp.where(inside, scores, MASKED)
    k = jnp.ceil(jnp.max(scores, axis=1, keepdims=True))
    weights = jnp.exp2(scores - k)
    total = jnp.sum(weights, axis=1, keepdims=True)
    time_sum = jnp.sum(weights * aux[1:2], axis=1, keepdims=True)
    upper = weights.astype(jnp.bfloat16)
    lower = (weights - upper.astype(jnp.float32)).astype(jnp.bfloat16)
    both = jnp.concatenate([upper, lower], axis=0)
    sums = jnp.dot(both, entries[...], preferred_element_type=jnp.float32)
    vector = sums[: 4 * rows] + sums[4 * rows :]
    for v, out in enumerate(outs):
        part = slice(v * rows, (v + 1) * rows)
        encode(out, slice(None), vector[part], k[part], total[part], time_sum[part])


def match(base, queries, libraries, auxes, per_bucket, steps):
    rows, width = queries[0].shape
    rows //= steps
    bins = width - LANES
    count = libraries[0].shape[0]
    shards = len(libraries)
    starts = [max(0, (8 * q - 1) * per_bucket // LANES * LANES) for q in range(steps)]
    ends = [min(count, (8 * q + 9) * per_bucket) for q in range(steps)]
    window = min(count, max(-(-(e - s) // LANES) * LANES for s, e in zip(starts, ends)))
    block = pl.BlockSpec((rows, width), lambda q, base: (q, 0))
    whole = pl.BlockSpec((8, count), lambda q, base: (0, 0))
    work = 4 * rows * shards * window * bins
    return pl.pallas_call(
        functools.partial(match_kernel, window, per_bucket, shards),
        out_shape=(jax.ShapeDtypeStruct(queries[0].shape, jnp.int16),) * 4,
        grid_spec=pltpu.PrefetchScalarGridSpec(
            num_scalar_prefetch=1,
            grid=(steps,),
            in_specs=[block] * 4 + [pl.BlockSpec(memory_space=pl.ANY)] * shards + [whole] * shards,
            out_specs=[block] * 4,
            scratch_shapes=[
                pltpu.VMEM((2, shards * window, bins), jnp.bfloat16),
                pltpu.VMEM((4 * rows, width), jnp.bfloat16),
                pltpu.SemaphoreType.DMA((2, shards)),
            ],
        ),
        compiler_params=pltpu.CompilerParams(vmem_limit_bytes=48 * MIB),
        cost_estimate=pl.CostEstimate(
            flops=steps * 6 * work, bytes_accessed=steps * 2 * shards * window * bins, transcendentals=0
        ),
        name="match",
    )(base, *queries, *libraries, *auxes)


def per_device(shards, places, queries, query_bucket, library, library_time, library_bucket):
    own_rows, bins = queries.shape
    per_bucket = library.shape[0] // (2 * places)
    far = places // 4

    def both_axes(first, second):
        return [
            (c * places + i, c * places + (i ^ (second if c % 2 else first)))
            for c in range(shards)
            for i in range(places)
        ]

    def send(value, first, second):
        return lax.ppermute(value, ("query", "lib"), both_axes(first, second))

    def swap(value, distance):
        return lax.ppermute(value, "query", [(c, c ^ distance) for c in range(shards)])

    bucket_columns = jnp.broadcast_to(query_bucket.astype(jnp.bfloat16)[:, None], (own_rows, LANES))
    own = jnp.concatenate([queries, bucket_columns], axis=1)
    gathered = [own] + [send(own, 4 * z, 4 * z) for z in range(1, far)]
    entries, aux = sort_library(library, library_time, library_bucket, per_bucket)
    libraries = [entries] + [swap(entries, d) for d in range(1, shards)]
    auxes = [aux] + [swap(aux, d) for d in range(1, shards)]
    near = jnp.concatenate(gathered, axis=0)
    second = send(near, 2, 1)
    first = send(near, 1, 2)
    corner = send(second, 1, 2)

    base = (lax.axis_index("lib") // 4).astype(jnp.int32).reshape(1)
    part_near, part_second, part_first, part_corner = match(
        base, (near, second, first, corner), libraries, auxes, per_bucket, far
    )
    from_corner = send(part_corner, 1, 2)
    from_first = send(part_first, 1, 2)
    (part_second,) = merge([part_second, from_corner], 1)
    from_second = send(part_second, 2, 1)
    parts = merge([part_near, from_first, from_second], far)
    arrived = [parts[0]] + [send(parts[z], 4 * z, 4 * z) for z in range(1, far)]
    return finish(arrived)


def solution(mesh):
    placed = (
        P(("query", "lib"), None),
        P(("query", "lib")),
        P(("lib", "query"), None),
        P(("lib", "query")),
        P(("lib", "query")),
    )
    return jax.shard_map(
        functools.partial(per_device, mesh.shape["query"], mesh.shape["lib"]),
        mesh=mesh,
        in_specs=placed,
        out_specs=(P(("query", "lib"), None), P(("query", "lib")), P(("query", "lib"))),
        check_vma=False,
    )
```

time: 277 us -> 120 us (0.43)
  blocking collectives: 98.7 us -> 0 us
  waiting for transfers between devices: 122 us -> 59.4 us
  Pallas kernels: 0 us -> 40.4 us
  matrix products: 23.9 us -> 0 us
  starting transfers between devices: 0.11 us -> 17.5 us
  other arithmetic: 15.9 us -> 0.06 us
  between operations: 15.2 us -> 0.69 us
    all_gather x2 -> x0, waiting for transfers between devices: 69 us -> none  [the longest x1 45.9 us: per_device(): lax.all_gather(queries, 'lib', axis=0, tiled=True)]
    ppermute x0 -> x14, waiting for transfers between devices: none -> 59.4 us  [the longest x12 58.1 us: send(): return lax.ppermute(value, ('query', 'lib'), both_axes(first, second))]
    unnamed x2 -> x0, blocking collectives: 53.1 us -> none
    reduce_scatter x1 -> x0, waiting for transfers between devices: 51.3 us -> none  [per_device(): lax.psum_scatter(spectra_part, 'lib', scatter_dimension=0, tiled=True)]
    pmax x1 -> x0, blocking collectives: 41.9 us -> none  [per_device(): maxima = lax.pmax(jnp.max(scores, axis=1), 'lib')]
    pallas_call x0 -> x5, Pallas kernels: none -> 40.4 us  [the longest x1 20.8 us: match(): pl.pallas_call(functools.partial(match_kernel, window, per_bucket, shards...]
    dot_general x3 -> x0, matrix products: 23.9 us -> none  [the longest x1 12.1 us: scaled_scores(): lax.dot_general(query_block, entries, (((1,), (1,)), ((), ())), preferred...]
    ppermute x0 -> x14, starting transfers between devices: none -> 17.5 us  [the longest x12 17 us: send(): return lax.ppermute(value, ('query', 'lib'), both_axes(first, second))]
  transfers between devices with their start and end apart: 3 -> 14, of which waited for: 3 -> 9; matrix products, arithmetic and copies ran while one was open for 2% -> 0% of each run, Pallas kernels for 0% -> 1%
where the time goes in v1:
time: 120 us
  waiting for transfers between devices  59.4 us (50%)
  Pallas kernels  40.4 us (34%)
  starting transfers between devices  17.5 us (15%)
  local copies, waits for them, and re-layouts  1.48 us (1%)
    ppermute x12, waiting for transfers between devices, send(): return lax.ppermute(value, ('query', 'lib'), both_axes(first, second))  58.1 us
    pallas_call x1, Pallas kernels, match(): pl.pallas_call(functools.partial(match_kernel, window, per_bucket, shards...  20.8 us
    ppermute x12, starting transfers between devices, send(): return lax.ppermute(value, ('query', 'lib'), both_axes(first, second))  17 us
    pallas_call x1, Pallas kernels, sort_library(): pl.pallas_call(functools.partial(sort_kernel, per_bucket, chunk), out_sha...  16.7 us
  transfers between devices with their start and end apart: 14, of which 9 were waited for; matrix products, arithmetic and copies ran while one was open for 0% of the time, Pallas kernels for 1%

profile of v1, /device:TPU:0, one launch (start us, length us, event | category | flops | bytes accessed | tf_op | source)
XLA Modules:
  0.0 119.5 jit_solution(10405107652736550003)
XLA Ops:
  0.6 0.7 reshape.31.time_ref
  1.3 0.7 reshape.25.bucket_ref
  2.0 16.7 %sort_library.1 = (bf16[1536,2048]{1,0:T(8,128)(2,1)}, f32[8,1536]{1,0:T(8,128)S(1)}) custom-call(s32[1,1536]{1,0:T(1,128)S(1)} %reshape.25.bucket_ref, f32[1,1536]{1,0:T(1,128)S(1)} %reshape.31.time_ref, bf16[1536,2048]{1,0:T(8,128)(2,1)} %library_ref.1), custom_call_target="tpu_custom_call" | custom-call | flops 9663676416 | bytes 12582912 | tf_op jit(solution)/shard_map/sort_library/pallas_call | solution.py:64
  18.7 0.5 collective-permute-start.6
  19.2 0.1 broadcast_in_dim.2
  19.3 4.7 %collective-permute-start.2 = (bf16[32,2176]{1,0:T(8,128)(2,1)S(1)}, bf16[32,2176]{1,0:T(8,128)(2,1)S(1)}, u32[]{:S(2)}, u32[]{:S(2)}) collective-permute-start(bf16[32,2176]{1,0:T(8,128)(2,1)S(1)} %pad_maximum_fusion.1), channel_id=1, source_target_pairs={{0,12},{1,13},{2,14},{3,15},{4,8},{5,9},{6,10},{7,11},{8,4},{9,5},... | collective-permute-start | bytes 417800 | tf_op jit(solution)/shard_map/ppermute | solution.py:278
  24.0 0.6 collective-permute-start
  24.6 4.0 %collective-permute-done.2 = bf16[32,2176]{1,0:T(8,128)(2,1)S(1)} collective-permute-done((bf16[32,2176]{1,0:T(8,128)(2,1)S(1)}, bf16[32,2176]{1,0:T(8,128)(2,1)S(1)}, u32[]{:S(2)}, u32[]{:S(2)}) %collective-permute-start.2) | collective-permute-done | bytes 139296 | tf_op jit(solution)/shard_map/ppermute | solution.py:278
  28.6 7.8 %collective-permute-done.1 = bf16[32,2176]{1,0:T(8,128)(2,1)S(1)} collective-permute-done((bf16[32,2176]{1,0:T(8,128)(2,1)S(1)}, bf16[32,2176]{1,0:T(8,128)(2,1)S(1)}, u32[]{:S(2)}, u32[]{:S(2)}) %collective-permute-start.1) | collective-permute-done | bytes 139296 | tf_op jit(solution)/shard_map/ppermute | solution.py:278
  36.4 0.0 collective-permute-done
  36.5 1.6 %collective-permute-start.3 = (bf16[128,2176]{1,0:T(8,128)(2,1)S(1)}, bf16[128,2176]{1,0:T(8,128)(2,1)S(1)}, u32[]{:S(2)}, u32[]{:S(2)}) collective-permute-start(bf16[128,2176]{1,0:T(8,128)(2,1)S(1)} %pad_maximum_fusion.refs_0_), channel_id=1, source_target_pairs={{0,2},{1,3},{2,0},{3,1},{4,6},{5,7},{6,4},{7,5},{8,10},{9,11},{10,... | collective-permute-start | bytes 1671176 | tf_op jit(solution)/shard_map/ppermute | solution.py:278
  38.1 1.5 %collective-permute-start.4 = (bf16[128,2176]{1,0:T(8,128)(2,1)S(1)}, bf16[128,2176]{1,0:T(8,128)(2,1)S(1)}, u32[]{:S(2)}, u32[]{:S(2)}) collective-permute-start(bf16[128,2176]{1,0:T(8,128)(2,1)S(1)} %pad_maximum_fusion.refs_0_), channel_id=1, source_target_pairs={{0,1},{1,0},{2,3},{3,2},{4,5},{5,4},{6,7},{7,6},{8,9},{9,8},{10,11... | collective-permute-start | bytes 1671176 | tf_op jit(solution)/shard_map/ppermute | solution.py:278
  39.5 12.5 %collective-permute-done.3.refs_1_ = bf16[128,2176]{1,0:T(8,128)(2,1)S(1)} collective-permute-done((bf16[128,2176]{1,0:T(8,128)(2,1)S(1)}, bf16[128,2176]{1,0:T(8,128)(2,1)S(1)}, u32[]{:S(2)}, u32[]{:S(2)}) %collective-permute-start.3) | collective-permute-done | bytes 557088 | tf_op jit(solution)/shard_map/ppermute | solution.py:278
  52.0 0.5 collective-permute-start.5
  52.5 0.0 collective-permute-start.7
  52.5 1.2 %collective-permute-done.7.refs_7_ = f32[8,1536]{1,0:T(8,128)S(1)} collective-permute-done((f32[8,1536]{1,0:T(8,128)S(1)}, f32[8,1536]{1,0:T(8,128)S(1)}, u32[]{:S(2)}, u32[]{:S(2)}) %collective-permute-start.7) | collective-permute-done | bytes 49184 | tf_op jit(solution)/shard_map/ppermute | solution.py:281
  53.8 0.0 collective-permute-done.4.refs_2_
  53.8 7.8 %collective-permute-done.5.refs_3_ = bf16[128,2176]{1,0:T(8,128)(2,1)S(1)} collective-permute-done((bf16[128,2176]{1,0:T(8,128)(2,1)S(1)}, bf16[128,2176]{1,0:T(8,128)(2,1)S(1)}, u32[]{:S(2)}, u32[]{:S(2)}) %collective-permute-start.5) | collective-permute-done | bytes 557088 | tf_op jit(solution)/shard_map/ppermute | solution.py:278
  61.6 20.8 %match.1 = (s16[128,2176]{1,0:T(8,128)(2,1)S(1)}, s16[128,2176]{1,0:T(8,128)(2,1)S(1)}, s16[128,2176]{1,0:T(8,128)(2,1)S(1)}, s16[128,2176]{1,0:T(8,128)(2,1)S(1)}) custom-call(s32[1]{0:T(128)} %bitcast.base_ref, bf16[128,2176]{1,0:T(8,128)(2,1)S(1)} %pad_maximum_fusion.refs_0_, bf16[128,2176]{1,0:T(8,128)(2,1)S(1)} %collective-permute-done.3.refs_1_, ...), custom_call_target="tpu_custom_call" | custom-call | flops 8053063680 | bytes 20971520 | tf_op jit(solution)/shard_map/match/pallas_call | solution.py:243
  82.4 0.6 collective-permute-start.9
  83.0 1.5 %collective-permute-start.8 = (s16[128,2176]{1,0:T(8,128)(2,1)S(1)}, s16[128,2176]{1,0:T(8,128)(2,1)S(1)}, u32[]{:S(2)}, u32[]{:S(2)}) collective-permute-start(s16[128,2176]{1,0:T(8,128)(2,1)S(1)} %get-tuple-element.19), channel_id=1, source_target_pairs={{0,1},{1,0},{2,3},{3,2},{4,5},{5,4},{6,7},{7,6},{8,9},{9,8},{10,11... | collective-permute-start | bytes 1671176 | tf_op jit(solution)/shard_map/ppermute | solution.py:278
  84.5 8.4 %collective-permute-done.9.refs_1_ = s16[128,2176]{1,0:T(8,128)(2,1)S(1)} collective-permute-done((s16[128,2176]{1,0:T(8,128)(2,1)S(1)}, s16[128,2176]{1,0:T(8,128)(2,1)S(1)}, u32[]{:S(2)}, u32[]{:S(2)}) %collective-permute-start.9) | collective-permute-done | bytes 557088 | tf_op jit(solution)/shard_map/ppermute | solution.py:278
  92.9 0.7 merge.2
  93.6 1.6 %collective-permute-start.10 = (s16[128,2176]{1,0:T(8,128)(2,1)S(1)}, s16[128,2176]{1,0:T(8,128)(2,1)S(1)}, u32[]{:S(2)}, u32[]{:S(2)}) collective-permute-start(s16[128,2176]{1,0:T(8,128)(2,1)S(1)} %merge.2), channel_id=1, source_target_pairs={{0,2},{1,3},{2,0},{3,1},{4,6},{5,7},{6,4},{7,5},{8,10},{9,11},{10,... | collective-permute-start | bytes 1671176 | tf_op jit(solution)/shard_map/ppermute | solution.py:278
  95.2 8.7 %collective-permute-done.8.refs_1_ = s16[128,2176]{1,0:T(8,128)(2,1)S(1)} collective-permute-done((s16[128,2176]{1,0:T(8,128)(2,1)S(1)}, s16[128,2176]{1,0:T(8,128)(2,1)S(1)}, u32[]{:S(2)}, u32[]{:S(2)}) %collective-permute-start.8) | collective-permute-done | bytes 557088 | tf_op jit(solution)/shard_map/ppermute | solution.py:278
  103.9 1.3 %merge.3 = (s16[32,2176]{1,0:T(8,128)(2,1)S(1)}, s16[32,2176]{1,0:T(8,128)(2,1)S(1)}, s16[32,2176]{1,0:T(8,128)(2,1)S(1)}, s16[32,2176]{1,0:T(8,128)(2,1)S(1)}) custom-call(s16[128,2176]{1,0:T(8,128)(2,1)S(1)} %get-tuple-element.18.refs_0_, s16[128,2176]{1,0:T(8,128)(2,1)S(1)} %collective-permute-done.8.refs_1_, ...), custom_call_target="tpu_custom_call" | custom-call | flops 6684672 | bytes 2228224 | tf_op jit(solution)/shard_map/merge/pallas_call | solution.py:125
  105.2 0.1 collective-permute-start.11
  105.3 3.0 %collective-permute-start.12 = (s16[32,2176]{1,0:T(8,128)(2,1)S(1)}, s16[32,2176]{1,0:T(8,128)(2,1)S(1)}, u32[]{:S(2)}, u32[]{:S(2)}) collective-permute-start(s16[32,2176]{1,0:T(8,128)(2,1)S(1)} %get-tuple-element.24), channel_id=1, source_target_pairs={{0,8},{1,9},{2,10},{3,11},{4,12},{5,13},{6,14},{7,15},{8,0},{9,1},... | collective-permute-start | bytes 417800 | tf_op jit(solution)/shard_map/ppermute | solution.py:278
  108.3 1.3 %collective-permute-start.13 = (s16[32,2176]{1,0:T(8,128)(2,1)S(1)}, s16[32,2176]{1,0:T(8,128)(2,1)S(1)}, u32[]{:S(2)}, u32[]{:S(2)}) collective-permute-start(s16[32,2176]{1,0:T(8,128)(2,1)S(1)} %get-tuple-element.25), channel_id=1, source_target_pairs={{0,12},{1,13},{2,14},{3,15},{4,8},{5,9},{6,10},{7,11},{8,4},{9,5},... | collective-permute-start | bytes 417800 | tf_op jit(solution)/shard_map/ppermute | solution.py:278
  109.7 2.4 %collective-permute-done.11.refs_1_ = s16[32,2176]{1,0:T(8,128)(2,1)S(1)} collective-permute-done((s16[32,2176]{1,0:T(8,128)(2,1)S(1)}, s16[32,2176]{1,0:T(8,128)(2,1)S(1)}, u32[]{:S(2)}, u32[]{:S(2)}) %collective-permute-start.11) | collective-permute-done | bytes 139296 | tf_op jit(solution)/shard_map/ppermute | solution.py:278
  112.0 6.5 %collective-permute-done.12.refs_2_ = s16[32,2176]{1,0:T(8,128)(2,1)S(1)} collective-permute-done((s16[32,2176]{1,0:T(8,128)(2,1)S(1)}, s16[32,2176]{1,0:T(8,128)(2,1)S(1)}, u32[]{:S(2)}, u32[]{:S(2)}) %collective-permute-start.12) | collective-permute-done | bytes 139296 | tf_op jit(solution)/shard_map/ppermute | solution.py:278
  118.5 1.0 finish.1
  (11 shorter events, 0.1 us)
Async XLA Ops:
  2.0 17.2 %copy-start.1 = (s32[32]{0:T(128)S(1)}, s32[32]{0:T(128)}, u32[]{:S(2)}) copy-start(s32[32]{0:T(128)} %param.6) | copy-start | bytes 388
  2.0 17.3 %copy-start = (bf16[32,2048]{1,0:T(8,128)(2,1)S(1)}, bf16[32,2048]{1,0:T(8,128)(2,1)}, u32[]{:S(2)}) copy-start(bf16[32,2048]{1,0:T(8,128)(2,1)} %param.5) | copy-start | bytes 393220
  18.7 42.8 %collective-permute-start.6 = (bf16[1536,2048]{1,0:T(8,128)(2,1)}, bf16[1536,2048]{1,0:T(8,128)(2,1)}, u32[]{:S(2)}, u32[]{:S(2)}) collective-permute-start(bf16[1536,2048]{1,0:T(8,128)(2,1)} %get-tuple-element.16.refs_4_), channel_id=1, source_target_pairs={{0,16},{16,0},{1,17},{17,1},{2,18},{18,2},{3,19},{19,3},{4,20},{20... | collective-permute-start | bytes 18874376 | tf_op jit(solution)/shard_map/ppermute | solution.py:281
  19.3 9.3 %collective-permute-start.2 = (bf16[32,2176]{1,0:T(8,128)(2,1)S(1)}, bf16[32,2176]{1,0:T(8,128)(2,1)S(1)}, u32[]{:S(2)}, u32[]{:S(2)}) collective-permute-start(bf16[32,2176]{1,0:T(8,128)(2,1)S(1)} %pad_maximum_fusion.1), channel_id=1, source_target_pairs={{0,12},{1,13},{2,14},{3,15},{4,8},{5,9},{6,10},{7,11},{8,4},{9,5},... | collective-permute-start | bytes 417800 | tf_op jit(solution)/shard_map/ppermute | solution.py:278
  24.0 12.4 %collective-permute-start.1 = (bf16[32,2176]{1,0:T(8,128)(2,1)S(1)}, bf16[32,2176]{1,0:T(8,128)(2,1)S(1)}, u32[]{:S(2)}, u32[]{:S(2)}) collective-permute-start(bf16[32,2176]{1,0:T(8,128)(2,1)S(1)} %pad_maximum_fusion.1), channel_id=1, source_target_pairs={{0,8},{1,9},{2,10},{3,11},{4,12},{5,13},{6,14},{7,15},{8,0},{9,1},... | collective-permute-start | bytes 417800 | tf_op jit(solution)/shard_map/ppermute | solution.py:278
  24.0 12.4 %collective-permute-start = (bf16[32,2176]{1,0:T(8,128)(2,1)S(1)}, bf16[32,2176]{1,0:T(8,128)(2,1)S(1)}, u32[]{:S(2)}, u32[]{:S(2)}) collective-permute-start(bf16[32,2176]{1,0:T(8,128)(2,1)S(1)} %pad_maximum_fusion.1), channel_id=1, source_target_pairs={{0,4},{1,5},{2,6},{3,7},{4,0},{5,1},{6,2},{7,3},{8,12},{9,13},{10,... | collective-permute-start | bytes 417800 | tf_op jit(solution)/shard_map/ppermute | solution.py:278
  36.5 15.6 %collective-permute-start.3 = (bf16[128,2176]{1,0:T(8,128)(2,1)S(1)}, bf16[128,2176]{1,0:T(8,128)(2,1)S(1)}, u32[]{:S(2)}, u32[]{:S(2)}) collective-permute-start(bf16[128,2176]{1,0:T(8,128)(2,1)S(1)} %pad_maximum_fusion.refs_0_), channel_id=1, source_target_pairs={{0,2},{1,3},{2,0},{3,1},{4,6},{5,7},{6,4},{7,5},{8,10},{9,11},{10,... | collective-permute-start | bytes 1671176 | tf_op jit(solution)/shard_map/ppermute | solution.py:278
  38.1 15.7 %collective-permute-start.4 = (bf16[128,2176]{1,0:T(8,128)(2,1)S(1)}, bf16[128,2176]{1,0:T(8,128)(2,1)S(1)}, u32[]{:S(2)}, u32[]{:S(2)}) collective-permute-start(bf16[128,2176]{1,0:T(8,128)(2,1)S(1)} %pad_maximum_fusion.refs_0_), channel_id=1, source_target_pairs={{0,1},{1,0},{2,3},{3,2},{4,5},{5,4},{6,7},{7,6},{8,9},{9,8},{10,11... | collective-permute-start | bytes 1671176 | tf_op jit(solution)/shard_map/ppermute | solution.py:278
  52.0 9.5 %collective-permute-start.5 = (bf16[128,2176]{1,0:T(8,128)(2,1)S(1)}, bf16[128,2176]{1,0:T(8,128)(2,1)S(1)}, u32[]{:S(2)}, u32[]{:S(2)}) collective-permute-start(bf16[128,2176]{1,0:T(8,128)(2,1)S(1)} %collective-permute-done.3.refs_1_), channel_id=1, source_target_pairs={{0,1},{1,0},{2,3},{3,2},{4,5},{5,4},{6,7},{7,6},{8,9},{9,8},{10,11... | collective-permute-start | bytes 1671176 | tf_op jit(solution)/shard_map/ppermute | solution.py:278
  52.5 1.2 %collective-permute-start.7 = (f32[8,1536]{1,0:T(8,128)S(1)}, f32[8,1536]{1,0:T(8,128)S(1)}, u32[]{:S(2)}, u32[]{:S(2)}) collective-permute-start(f32[8,1536]{1,0:T(8,128)S(1)} %get-tuple-element.17.refs_6_), channel_id=1, source_target_pairs={{0,16},{16,0},{1,17},{17,1},{2,18},{18,2},{3,19},{19,3},{4,20},{20... | collective-permute-start | bytes 147464 | tf_op jit(solution)/shard_map/ppermute | solution.py:281
  82.4 10.5 %collective-permute-start.9 = (s16[128,2176]{1,0:T(8,128)(2,1)S(1)}, s16[128,2176]{1,0:T(8,128)(2,1)S(1)}, u32[]{:S(2)}, u32[]{:S(2)}) collective-permute-start(s16[128,2176]{1,0:T(8,128)(2,1)S(1)} %get-tuple-element.21), channel_id=1, source_target_pairs={{0,1},{1,0},{2,3},{3,2},{4,5},{5,4},{6,7},{7,6},{8,9},{9,8},{10,11... | collective-permute-start | bytes 1671176 | tf_op jit(solution)/shard_map/ppermute | solution.py:278
  83.0 21.0 %collective-permute-start.8 = (s16[128,2176]{1,0:T(8,128)(2,1)S(1)}, s16[128,2176]{1,0:T(8,128)(2,1)S(1)}, u32[]{:S(2)}, u32[]{:S(2)}) collective-permute-start(s16[128,2176]{1,0:T(8,128)(2,1)S(1)} %get-tuple-element.19), channel_id=1, source_target_pairs={{0,1},{1,0},{2,3},{3,2},{4,5},{5,4},{6,7},{7,6},{8,9},{9,8},{10,11... | collective-permute-start | bytes 1671176 | tf_op jit(solution)/shard_map/ppermute | solution.py:278
  93.6 10.3 %collective-permute-start.10 = (s16[128,2176]{1,0:T(8,128)(2,1)S(1)}, s16[128,2176]{1,0:T(8,128)(2,1)S(1)}, u32[]{:S(2)}, u32[]{:S(2)}) collective-permute-start(s16[128,2176]{1,0:T(8,128)(2,1)S(1)} %merge.2), channel_id=1, source_target_pairs={{0,2},{1,3},{2,0},{3,1},{4,6},{5,7},{6,4},{7,5},{8,10},{9,11},{10,... | collective-permute-start | bytes 1671176 | tf_op jit(solution)/shard_map/ppermute | solution.py:278
  105.2 6.8 %collective-permute-start.11 = (s16[32,2176]{1,0:T(8,128)(2,1)S(1)}, s16[32,2176]{1,0:T(8,128)(2,1)S(1)}, u32[]{:S(2)}, u32[]{:S(2)}) collective-permute-start(s16[32,2176]{1,0:T(8,128)(2,1)S(1)} %get-tuple-element.23), channel_id=1, source_target_pairs={{0,4},{1,5},{2,6},{3,7},{4,0},{5,1},{6,2},{7,3},{8,12},{9,13},{10,... | collective-permute-start | bytes 417800 | tf_op jit(solution)/shard_map/ppermute | solution.py:278
  105.3 13.3 %collective-permute-start.12 = (s16[32,2176]{1,0:T(8,128)(2,1)S(1)}, s16[32,2176]{1,0:T(8,128)(2,1)S(1)}, u32[]{:S(2)}, u32[]{:S(2)}) collective-permute-start(s16[32,2176]{1,0:T(8,128)(2,1)S(1)} %get-tuple-element.24), channel_id=1, source_target_pairs={{0,8},{1,9},{2,10},{3,11},{4,12},{5,13},{6,14},{7,15},{8,0},{9,1},... | collective-permute-start | bytes 417800 | tf_op jit(solution)/shard_map/ppermute | solution.py:278
  108.3 10.2 %collective-permute-start.13 = (s16[32,2176]{1,0:T(8,128)(2,1)S(1)}, s16[32,2176]{1,0:T(8,128)(2,1)S(1)}, u32[]{:S(2)}, u32[]{:S(2)}) collective-permute-start(s16[32,2176]{1,0:T(8,128)(2,1)S(1)} %get-tuple-element.25), channel_id=1, source_target_pairs={{0,12},{1,13},{2,14},{3,15},{4,8},{5,9},{6,10},{7,11},{8,4},{9,5},... | collective-permute-start | bytes 417800 | tf_op jit(solution)/shard_map/ppermute | solution.py:278

commit v2 on v0

v2 whole, which is shorter than its diff:
```python
import functools
import math

import jax
import jax.numpy as jnp
from jax import lax
from jax.experimental import pallas as pl
from jax.experimental.pallas import tpu as pltpu
from jax.sharding import PartitionSpec as P

SHARPNESS = 448
EPSILON = 1e-06
LANES = 128
LOG2E = math.log2(math.e)
LN2 = math.log(2.0)
FRACTION_BITS = 14
SUM_BITS = 16
LOW_BITS = 15
MASKED = -1e30
OUTSIDE = 1e6
UNIT = 16
LARGEST = 8
SORT_MIB, MATCH_MIB, MERGE_MIB = 20, 20, 4
NT = (((1,), (1,)), ((), ()))
MIB = 1 << 20


def split3(value):
    pieces = []
    for _ in range(3):
        piece = value.astype(jnp.bfloat16)
        pieces.append(piece)
        value = value - piece.astype(jnp.float32)
    return pieces


def sort_kernel(buckets, bucket_ref, time_ref, library_ref, sorted_ref, first_ref):
    count, bins = library_ref.shape

    def earlier(n):
        order = [lax.broadcasted_iota(jnp.int32, (n, n), d) for d in range(2)]
        return (order[0] < order[1]).astype(jnp.float32).astype(jnp.bfloat16)

    member = (
        bucket_ref[...] == lax.broadcasted_iota(jnp.int32, (buckets, count), 0)
    ).astype(jnp.float32)
    member16 = member.astype(jnp.bfloat16)
    before = jnp.dot(member16, earlier(count), preferred_element_type=jnp.float32)
    lower = lax.dot_general(
        earlier(buckets), member16, (((0,), (0,)), ((), ())), preferred_element_type=jnp.float32
    )
    first = jnp.sum(lower, axis=1, keepdims=True)
    place = jnp.sum(member * (before + first), axis=0, keepdims=True).astype(jnp.int32)
    first_ref[...] = jnp.broadcast_to(first, (buckets, LANES)).astype(jnp.int32)
    chosen = (
        (lax.broadcasted_iota(jnp.int32, (count, count), 0) == place)
        .astype(jnp.float32)
        .astype(jnp.bfloat16)
    )

    entries = library_ref[...]
    wide = entries.astype(jnp.float32)
    scale = lax.rsqrt(jnp.sum(wide * wide, axis=1, keepdims=True) / bins + EPSILON)
    which = lax.broadcasted_iota(jnp.int32, (LANES, count), 0)
    facts = jnp.where(which == 0, time_ref[...], jnp.where(which == 1, bucket_ref[...].astype(jnp.float32), 0.0)).T
    lane = lax.broadcasted_iota(jnp.int32, (count, LANES), 1)
    for at, piece in enumerate(split3(scale)):
        facts = jnp.where(lane == 2 + at, piece.astype(jnp.float32), facts)
    sorted_ref[:, :bins] = jnp.dot(chosen, entries, preferred_element_type=jnp.float32).astype(
        jnp.bfloat16
    )
    sorted_ref[:, bins:] = jnp.dot(
        chosen, facts.astype(jnp.bfloat16), preferred_element_type=jnp.float32
    ).astype(jnp.bfloat16)


def sort_library(blocks, buckets, library, library_time, library_bucket):
    total, bins = library.shape
    count = total // blocks
    row = pl.BlockSpec((1, count), lambda n: (0, n))
    return pl.pallas_call(
        functools.partial(sort_kernel, buckets),
        out_shape=(
            jax.ShapeDtypeStruct((total, bins + LANES), jnp.bfloat16),
            jax.ShapeDtypeStruct((blocks * buckets, LANES), jnp.int32),
        ),
        grid=(blocks,),
        in_specs=[row, row, pl.BlockSpec((count, bins), lambda n: (n, 0))],
        out_specs=[
            pl.BlockSpec((count, bins + LANES), lambda n: (n, 0)),
            pl.BlockSpec((buckets, LANES), lambda n: (n, 0)),
        ],
        compiler_params=pltpu.CompilerParams(vmem_limit_bytes=SORT_MIB * MIB),
        cost_estimate=pl.CostEstimate(flops=5 * count * total * bins, bytes_accessed=(4 * total * bins) // 1, transcendentals=0),
        name="sort_library",
    )(library_bucket, library_time, library)


def encode(out, rows, vector, k, total, time_sum):
    bins = vector.shape[1]
    largest = jnp.maximum(jnp.max(jnp.abs(vector), axis=1, keepdims=True), 1e-30)
    e = jnp.ceil(jnp.log2(largest))
    coded = jnp.floor(vector * jnp.exp2(FRACTION_BITS - e) + 0.5).astype(jnp.int32)
    out[rows, :bins] = coded.astype(jnp.int16)
    lane = lax.broadcasted_iota(jnp.int32, (vector.shape[0], LANES), 1)
    total = (total * (1 << SUM_BITS) + 0.5).astype(jnp.int32)
    time_sum = (time_sum * (1 << SUM_BITS) + 0.5).astype(jnp.int32)
    low = (1 << LOW_BITS) - 1
    stats = jnp.zeros((vector.shape[0], LANES), jnp.int32)
    for at, value in enumerate(
        (k.astype(jnp.int32), e.astype(jnp.int32), total >> LOW_BITS, total & low, time_sum >> LOW_BITS, time_sum & low)
    ):
        stats = jnp.where(lane == at, value, stats)
    out[rows, bins:] = stats.astype(jnp.int16)


def merged(parts):
    bins = parts[0].shape[1] - LANES
    stats = [p[:, bins:].astype(jnp.int32).astype(jnp.float32) for p in parts]
    ks = [s[:, 0:1] for s in stats]
    k = functools.reduce(jnp.maximum, ks)
    high = float(1 << LOW_BITS)
    unit = 1.0 / (1 << SUM_BITS)
    vector = total = time_sum = 0.0
    for part, s, own in zip(parts, stats, ks):
        shift = jnp.exp2(own - k)
        total = total + (s[:, 2:3] * high + s[:, 3:4]) * (shift * unit)
        time_sum = time_sum + (s[:, 4:5] * high + s[:, 5:6]) * (shift * unit)
        factor = jnp.exp2(own - k + s[:, 1:2] - FRACTION_BITS)
        vector = vector + part[:, :bins].astype(jnp.int32).astype(jnp.float32) * factor
    return vector, k, total, time_sum


def merge_kernel(pieces, *refs):
    parts = refs[: len(refs) - pieces]
    outs = refs[len(refs) - pieces :]
    rows = parts[0].shape[0] // pieces
    for at, out in enumerate(outs):
        own = [p[at * rows : (at + 1) * rows, :] for p in parts]
        encode(out, slice(None), *merged(own))


def merge(parts, pieces):
    rows, width = parts[0].shape
    out = jax.ShapeDtypeStruct((rows // pieces, width), jnp.int16)
    return pl.pallas_call(
        functools.partial(merge_kernel, pieces),
        out_shape=(out,) * pieces,
        compiler_params=pltpu.CompilerParams(vmem_limit_bytes=MERGE_MIB * MIB),
        cost_estimate=pl.CostEstimate(flops=(8 * rows * width * len(parts)) // 1, bytes_accessed=(2 * rows * width * (len(parts) + 1)) // 1, transcendentals=0),
        name="merge",
    )(*parts)


def finish_kernel(*refs):
    *parts, spectra_ref, time_ref, evidence_ref = refs
    vector, k, total, time_sum = merged([p[...] for p in parts])
    spectra_ref[...] = (vector / total).astype(jnp.bfloat16)
    shape = (total.shape[0], LANES)
    time_ref[...] = jnp.broadcast_to(time_sum / total, shape).T[:1]
    evidence_ref[...] = jnp.broadcast_to(k * LN2 + jnp.log(total), shape).T[:1]


def finish(parts):
    rows, width = parts[0].shape
    spectra, time, evidence = pl.pallas_call(
        finish_kernel,
        out_shape=(
            jax.ShapeDtypeStruct((rows, width - LANES), jnp.bfloat16),
            jax.ShapeDtypeStruct((1, rows), jnp.float32),
            jax.ShapeDtypeStruct((1, rows), jnp.float32),
        ),
        compiler_params=pltpu.CompilerParams(vmem_limit_bytes=MERGE_MIB * MIB),
        name="finish",
    )(*parts)
    return spectra, time.reshape(rows), evidence.reshape(rows)


def window_kernel(shards, blocks, buckets, quad_ref, first_ref, *refs):
    libraries, refs, arrived = refs[:shards], refs[shards:-1], refs[-1]
    nears, seconds, helds, factses, parts = (refs[at :: 5] for at in range(5))
    count = libraries[0].shape[0] // blocks
    entries, width = helds[0].shape
    share = entries // shards

    def fetch(held, sem, library, begin, units, filled):
        def copy(size, done):
            pltpu.make_async_copy(
                library.at[pl.ds(pl.multiple_of((begin + done) * UNIT, UNIT), size * UNIT), :],
                held.at[pl.ds(pl.multiple_of((filled + done) * UNIT, UNIT), size * UNIT), :],
                sem,
            ).start()

        most = LARGEST
        while most * UNIT > count:
            most //= 2

        def large(i, carry):
            copy(most, i * most)
            return carry

        lax.fori_loop(0, units // most, large, 0)
        size = most // 2
        while size:

            @pl.when((units & size) != 0)
            def _(size=size):
                copy(size, units // (2 * size) * (2 * size))

            size //= 2

    filled = []
    for at, held in enumerate(helds):
        low = jnp.maximum(8 * quad_ref[at] - 1, 0)
        high = 8 * quad_ref[at] + 9
        for shard, library in enumerate(libraries):
            region, sem = held.at[shard * share : (shard + 1) * share, :], arrived.at[at, shard]
            there = jnp.int32(0)
            for n in range(blocks):
                row = (shard * blocks + n) * buckets
                start = first_ref[row + low]
                end = first_ref[row + jnp.minimum(high, buckets - 1)]
                end = jnp.where(high >= buckets, count, end)
                begin = start // UNIT
                units = (end + UNIT - 1) // UNIT - begin
                fetch(region, sem, library, n * (count // UNIT) + begin, units, there)
                there = there + units
            fetch(region, sem, library, 0, share // UNIT - there, there)
            filled.append(there)

    for at, held in enumerate(helds):
        queries = jnp.concatenate([nears[at][...], seconds[at][...]], axis=0)
        products, here = [], []
        for shard in range(shards):
            region = held.at[shard * share : (shard + 1) * share, :]
            pltpu.make_async_copy(region, region, arrived.at[at, shard]).wait()
            products.append(score(queries, region))
            row = lax.broadcasted_iota(jnp.int32, (1, share), 1)
            here.append(row - filled[at * shards + shard] * UNIT)
        columns = held[:, width - LANES :].astype(jnp.float32).T
        which = lax.broadcasted_iota(jnp.int32, (8, entries), 0)
        bucket = jnp.where(jnp.concatenate(here, axis=1) < 0, columns[1:2], OUTSIDE)
        scale = columns[2:3] + columns[3:4] + columns[4:5]
        facts = jnp.where(which == 0, columns[0:1], jnp.where(which == 1, bucket, scale))
        factses[at][...] = facts
        weigh(queries, jnp.concatenate(products, axis=1), facts, held, parts[at])


def rest_kernel(far_ref, held, facts_ref, part_ref):
    queries = far_ref[...]
    weigh(queries, score(queries, held), facts_ref[...], held, part_ref)


def score(queries, held):
    bins = queries.shape[1] - LANES
    return lax.dot_general(
        queries[:, :bins], held[:, :bins], NT, preferred_element_type=jnp.float32
    )


def weigh(queries, products, facts, held, part_ref):
    rows, width = queries.shape
    bins = width - LANES
    wide = queries[:, :bins].astype(jnp.float32)
    mean = jnp.sum(wide * wide, axis=1, keepdims=True) / bins
    query_scale = lax.rsqrt(mean + EPSILON) * (SHARPNESS / bins)
    query_bucket = queries[:, bins:].astype(jnp.float32)[:, 0:1]
    time, bucket, scale = facts[0:1], facts[1:2], facts[2:3]
    scores = products * query_scale * scale * LOG2E
    scores = jnp.where(jnp.abs(query_bucket - bucket) <= 1.0, scores, MASKED)
    k = jnp.ceil(jnp.max(scores, axis=1, keepdims=True))
    weights = jnp.exp2(scores - k)
    total = jnp.sum(weights, axis=1, keepdims=True)
    time_sum = jnp.sum(weights * time, axis=1, keepdims=True)
    upper = weights.astype(jnp.bfloat16)
    lower = (weights - upper.astype(jnp.float32)).astype(jnp.bfloat16)
    both = jnp.concatenate([upper, lower], axis=0)
    sums = jnp.dot(both, held[:, :bins], preferred_element_type=jnp.float32)
    encode(part_ref, slice(None), sums[:rows] + sums[rows:], k, total, time_sum)


def match_near(quad, firsts, near, second, libraries, per_bucket, blocks, buckets):
    quads = len(near)
    rows, width = near[0].shape
    bins = width - LANES
    shards = len(libraries)
    units = (10 * per_bucket + blocks * 2 * (UNIT - 1)) // UNIT
    entries = shards * (-(-units * UNIT // LANES) * LANES)
    vmem, smem = pl.BlockSpec(memory_space=pltpu.VMEM), pl.BlockSpec(memory_space=pltpu.SMEM)
    outs = (
        jax.ShapeDtypeStruct((entries, width), jnp.bfloat16),
        jax.ShapeDtypeStruct((8, entries), jnp.float32),
        jax.ShapeDtypeStruct((2 * rows, width), jnp.int16),
    )

    def kernel(quad_ref, first_ref, *refs):
        ins, rest = refs[: shards + 2 * quads], refs[shards + 2 * quads :]
        by_quad = []
        for at in range(quads):
            by_quad += ins[shards + 2 * at : shards + 2 * at + 2]
            by_quad += rest[3 * at : 3 * at + 3]
        window_kernel(shards, blocks, buckets, quad_ref, first_ref, *ins[:shards], *by_quad, rest[-1])

    results = pl.pallas_call(
        kernel,
        out_shape=outs * quads,
        in_specs=[smem, smem] + [pl.BlockSpec(memory_space=pl.ANY)] * shards + [vmem] * (2 * quads),
        out_specs=[vmem] * (3 * quads),
        scratch_shapes=[pltpu.SemaphoreType.DMA((quads, shards))],
        compiler_params=pltpu.CompilerParams(vmem_limit_bytes=MATCH_MIB * MIB),
        cost_estimate=pl.CostEstimate(
            flops=45 * quads * rows * entries * bins, bytes_accessed=2 * entries * width, transcendentals=0
        ),
        name="match_near",
    )(quad, firsts, *libraries, *[q for both in zip(near, second) for q in both])
    return [results[3 * at : 3 * at + 3] for at in range(quads)]


def match_far(far, held, facts):
    rows, width = far.shape
    return pl.pallas_call(
        rest_kernel,
        out_shape=jax.ShapeDtypeStruct((rows, width), jnp.int16),
        compiler_params=pltpu.CompilerParams(vmem_limit_bytes=MATCH_MIB * MIB),
        cost_estimate=pl.CostEstimate(flops=15 * rows * held.shape[0] * width, bytes_accessed=(2 * held.size) // 1, transcendentals=0),
        name="match_far",
    )(far, held, facts)


def per_device(shards, places, queries, query_bucket, library, library_time, library_bucket):
    own_rows, bins = queries.shape
    per_bucket = library.shape[0] // (2 * places)
    layers = places // 4
    quads = layers // shards
    buckets = 2 * places
    core = lax.axis_index("query")
    layer = lax.axis_index("lib") // 4

    def send(value, first, second):
        pairs = [
            (c * places + i, c * places + (i ^ (second if c % 2 else first)))
            for c in range(shards)
            for i in range(places)
        ]
        return lax.ppermute(value, ("query", "lib"), pairs)

    def layer_pairs(stream, distance):
        for s in range(shards):
            for i in range(places):
                worker, at = divmod(i // 4, quads)
                yield (s ^ distance) * places + i, worker * places + ((at ^ stream) + quads * s) * 4 + i % 4

    def spread(value, stream):
        return lax.ppermute(value, ("query", "lib"), list(layer_pairs(stream, 0)))

    def collect(value, stream, distance):
        return lax.ppermute(value, ("query", "lib"), [(b, a) for a, b in layer_pairs(stream, distance)])

    def swap(value, distance):
        return lax.ppermute(value, "query", [(c, c ^ distance) for c in range(shards)])

    blocks = 3
    rows = jnp.concatenate([queries] + [swap(queries, d) for d in range(1, shards)], axis=0)
    row_bucket = jnp.concatenate([query_bucket] + [swap(query_bucket, d) for d in range(1, shards)])
    bucket_columns = jnp.broadcast_to(row_bucket.astype(jnp.bfloat16)[:, None], (shards * own_rows, LANES))
    own = jnp.concatenate([rows, bucket_columns], axis=1)

    tie = lax.optimization_barrier
    near = [spread(own, at) for at in range(quads)]
    bucket_row = library_bucket.reshape(1, -1)
    time_row = library_time.astype(jnp.float32).reshape(1, -1)
    entries, firsts = sort_library(blocks, buckets, library, time_row, bucket_row)
    entries, firsts, near = tie((entries, firsts, near))
    libraries = [entries] + [swap(entries, d) for d in range(1, shards)]
    firsts = firsts[:, 0]
    firsts = jnp.concatenate([firsts] + [swap(firsts, d) for d in range(1, shards)])
    second = [send(n, 2, 1) for n in near]
    second, near = tie((second, near))
    wide = [jnp.concatenate(both, axis=0) for both in zip(near, second)]

    far = [send(w, 1, 2) for w in wide]
    quad = jnp.stack([core * quads + (at ^ (layer % quads)) for at in range(quads)]).astype(jnp.int32)
    matched = match_near(quad, firsts, near, second, libraries, per_bucket, blocks, buckets)
    far, matched = tie((far, matched))
    from_far = []
    for at, (held, facts, _) in enumerate(matched):
        from_far.append(send(match_far(far[at], held, facts), 1, 2))
    returned = []
    for at, (_, _, near_sums) in enumerate(matched):
        near_sums, second_sums = merge([near_sums, from_far[at]], 2)
        pieces = merge([near_sums, send(second_sums, 2, 1)], shards)
        returned += [collect(piece, at, d) for d, piece in enumerate(pieces)]
    return finish(returned)


def solution(mesh):
    placed = (
        P(("query", "lib"), None),
        P(("query", "lib")),
        P(("lib", "query"), None),
        P(("lib", "query")),
        P(("lib", "query")),
    )
    return jax.shard_map(
        functools.partial(per_device, mesh.shape["query"], mesh.shape["lib"]),
        mesh=mesh,
        in_specs=placed,
        out_specs=(P(("query", "lib"), None), P(("query", "lib")), P(("query", "lib"))),
        check_vma=False,
    )
```

time: 277 us -> 93.1 us (0.34)
  blocking collectives: 98.7 us -> 0 us
  waiting for transfers between devices: 122 us -> 25.9 us
  Pallas kernels: 0 us -> 30 us
  starting transfers between devices: 0.11 us -> 29.9 us
  matrix products: 23.9 us -> 0 us
  between operations: 15.2 us -> 0.76 us
  other arithmetic: 15.9 us -> 1.91 us
  local copies, waits for them, and re-layouts: 0.87 us -> 4.35 us
    all_gather x2 -> x0, waiting for transfers between devices: 69 us -> none  [the longest x1 45.9 us: per_device(): lax.all_gather(queries, 'lib', axis=0, tiled=True)]
    unnamed x2 -> x0, blocking collectives: 53.1 us -> none
    reduce_scatter x1 -> x0, waiting for transfers between devices: 51.3 us -> none  [per_device(): lax.psum_scatter(spectra_part, 'lib', scatter_dimension=0, tiled=True)]
    pmax x1 -> x0, blocking collectives: 41.9 us -> none  [per_device(): maxima = lax.pmax(jnp.max(scores, axis=1), 'lib')]
    pallas_call x0 -> x9, Pallas kernels: none -> 30 us  [the longest x1 11.5 us: match_near(): pl.pallas_call(kernel, out_shape=outs * quads, in_specs=[smem, smem] + [p...]
    ppermute x0 -> x18, starting transfers between devices: none -> 29.9 us  [the longest x4 12.5 us: collect(): lax.ppermute(value, ('query', 'lib'), [(b, a) for a, b in layer_pairs(str...]
    ppermute x0 -> x18, waiting for transfers between devices: none -> 25.9 us  [the longest x8 12.4 us: send(): return lax.ppermute(value, ('query', 'lib'), pairs)]
    dot_general x3 -> x0, matrix products: 23.9 us -> none  [the longest x1 12.1 us: scaled_scores(): lax.dot_general(query_block, entries, (((1,), (1,)), ((), ())), preferred...]
  transfers between devices with their start and end apart: 3 -> 18, of which waited for: 3 -> 5; matrix products, arithmetic and copies ran while one was open for 2% -> 3% of each run, Pallas kernels for 0% -> 27%
where the time goes in v2:
time: 93.1 us; the launch traced here: 92.8 us
  Pallas kernels  30 us (32%)
  starting transfers between devices  29.9 us (32%)
  waiting for transfers between devices  25.9 us (28%)
  local copies, waits for them, and re-layouts  4.35 us (5%)
  other arithmetic  1.91 us (2%)
    ppermute x4, starting transfers between devices, collect(): lax.ppermute(value, ('query', 'lib'), [(b, a) for a, b in layer_pairs(str...  12.5 us
    ppermute x8, waiting for transfers between devices, send(): return lax.ppermute(value, ('query', 'lib'), pairs)  12.4 us
    pallas_call x1, Pallas kernels, match_near(): pl.pallas_call(kernel, out_shape=outs * quads, in_specs=[smem, smem] + [p...  11.5 us
    ppermute x8, starting transfers between devices, send(): return lax.ppermute(value, ('query', 'lib'), pairs)  9.51 us
    pallas_call x2, Pallas kernels, match_far(): pl.pallas_call(rest_kernel, out_shape=jax.ShapeDtypeStruct((rows, width),...  8.79 us
    ppermute x4, waiting for transfers between devices, swap(): lax.ppermute(value, 'query', [(c, c ^ distance) for c in range(shards)])  8.06 us
    pallas_call x1, Pallas kernels, sort_library(): pl.pallas_call(functools.partial(sort_kernel, buckets), out_shape=(jax.Sh...  6.51 us
    ppermute x4, waiting for transfers between devices, collect(): lax.ppermute(value, ('query', 'lib'), [(b, a) for a, b in layer_pairs(str...  5.42 us
  transfers between devices with their start and end apart: 18, of which 5 were waited for; matrix products, arithmetic and copies ran while one was open for 3% of the time, Pallas kernels for 27%

profile of v2, /device:TPU:0, one launch (start us, length us, event | category | flops | bytes accessed | tf_op | source)
XLA Modules:
  0.0 92.8 jit_solution(571740680933870662)
XLA Ops:
  0.6 0.5 collective-permute-start
  1.2 0.7 convert.7
  1.9 0.7 reshape.35.bucket_ref
  2.6 0.7 reshape.41.time_ref
  3.4 0.9 %pad_maximum_fusion.2 = bf16[64,2176]{1,0:T(8,128)(2,1)S(1)} fusion(bf16[64,128]{1,0:T(8,128)(2,1)S(1)} %broadcast_in_dim.2, bf16[32,2048]{1,0:T(8,128)(2,1)S(1)} %collective-permute-done, bf16[32,2048]{1,0:T(8,128)(2,1)} %param.5), kind=kLoop, calls=%fused_computation.2 | loop fusion | flops 835584 | bytes 557056 | tf_op jit(solution)/shard_map/concatenate | solution.py:366
  4.4 0.7 collective-permute-start.2
  5.1 3.1 %collective-permute-start.3 = (bf16[64,2176]{1,0:T(8,128)(2,1)S(1)}, bf16[64,2176]{1,0:T(8,128)(2,1)S(1)}, u32[]{:S(2)}, u32[]{:S(2)}) collective-permute-start(bf16[64,2176]{1,0:T(8,128)(2,1)S(1)} %pad_maximum_fusion.2), channel_id=1, source_target_pairs={{0,4},{1,5},{2,6},{3,7},{4,0},{5,1},{6,2},{7,3},{8,20},{9,21},{10,... | collective-permute-start | bytes 835592 | tf_op jit(solution)/shard_map/ppermute | solution.py:354
  8.1 2.8 %copy-done = bf16[1536,2048]{1,0:T(8,128)(2,1)S(1)} copy-done((bf16[1536,2048]{1,0:T(8,128)(2,1)S(1)}, bf16[1536,2048]{1,0:T(8,128)(2,1)}, u32[]{:S(2)}) %copy-start) | copy-done | bytes 6291480
  10.9 6.5 %sort_library.1 = (bf16[1536,2176]{1,0:T(8,128)(2,1)}, s32[96,128]{1,0:T(8,128)S(1)}) custom-call(s32[1,1536]{1,0:T(1,128)S(1)} %reshape.35.bucket_ref, f32[1,1536]{1,0:T(1,128)S(1)} %reshape.41.time_ref, bf16[1536,2048]{1,0:T(8,128)(2,1)S(1)} %copy-done), custom_call_target="tpu_custom_call" | custom-call | flops 8053063680 | bytes 12582912 | tf_op jit(solution)/shard_map/sort_library/pallas_call | solution.py:81
  17.4 3.4 %collective-permute-start.9 = (bf16[1536,2176]{1,0:T(8,128)(2,1)}, bf16[1536,2176]{1,0:T(8,128)(2,1)}, u32[]{:S(2)}, u32[]{:S(2)}) collective-permute-start(bf16[1536,2176]{1,0:T(8,128)(2,1)} %get-tuple-element.47.refs_0_), channel_id=1, source_target_pairs={{0,16},{16,0},{1,17},{17,1},{2,18},{18,2},{3,19},{19,3},{4,20},{20... | collective-permute-start | bytes 20054024 | tf_op jit(solution)/shard_map/ppermute | solution.py:360
  20.8 1.5 %collective-permute-start.4 = (bf16[64,2176]{1,0:T(8,128)(2,1)S(1)}, bf16[64,2176]{1,0:T(8,128)(2,1)S(1)}, u32[]{:S(2)}, u32[]{:S(2)}) collective-permute-start(bf16[64,2176]{1,0:T(8,128)(2,1)S(1)} %collective-permute-done.2.refs_2_), channel_id=1, source_target_pairs={{0,2},{1,3},{2,0},{3,1},{4,6},{5,7},{6,4},{7,5},{8,10},{9,11},{10,... | collective-permute-start | bytes 835592 | tf_op jit(solution)/shard_map/ppermute | solution.py:345
  23.1 8.1 %collective-permute-done.8 = s32[96]{0:T(128)S(1)} collective-permute-done((s32[96]{0:T(128)S(1)}, s32[96]{0:T(128)S(1)}, u32[]{:S(2)}, u32[]{:S(2)}) %collective-permute-start.8) | collective-permute-done | bytes 416 | tf_op jit(solution)/shard_map/ppermute | solution.py:360
  31.3 1.6 %collective-permute-start.7 = (bf16[128,2176]{1,0:T(8,128)(2,1)S(1)}, bf16[128,2176]{1,0:T(8,128)(2,1)S(1)}, u32[]{:S(2)}, u32[]{:S(2)}) collective-permute-start(bf16[128,2176]{1,0:T(8,128)(2,1)S(1)} %pad_maximum_fusion.1), channel_id=1, source_target_pairs={{0,1},{1,0},{2,3},{3,2},{4,5},{5,4},{6,7},{7,6},{8,9},{9,8},{10,11... | collective-permute-start | bytes 1671176 | tf_op jit(solution)/shard_map/ppermute | solution.py:345
  32.9 0.6 collective-permute-start.6
  33.5 11.5 %match_near.1 = (bf16[1280,2176]{1,0:T(8,128)(2,1)S(1)}, f32[8,1280]{1,0:T(8,128)S(1)}, s16[128,2176]{1,0:T(8,128)(2,1)S(1)}, bf16[1280,2176]{1,0:T(8,128)(2,1)S...) custom-call(s32[2]{0:T(128)S(1)} %pad_add_fusion.1.quad_ref, s32[192]{0:T(256)S(1)} %pad_add_fusion.first_ref, ...), custom_call_target="tpu_custom_call" | custom-call | flops 15099494400 | bytes 5570560 | tf_op jit(solution)/shard_map/match_near/pallas_call | solution.py:304
  45.1 1.8 %collective-permute-done.6.far_ref = bf16[128,2176]{1,0:T(8,128)(2,1)S(1)} collective-permute-done((bf16[128,2176]{1,0:T(8,128)(2,1)S(1)}, bf16[128,2176]{1,0:T(8,128)(2,1)S(1)}, u32[]{:S(2)}, u32[]{:S(2)}) %collective-permute-start.6) | collective-permute-done | bytes 557088 | tf_op jit(solution)/shard_map/ppermute | solution.py:345
  46.9 4.4 %match_far.3 = s16[128,2176]{1,0:T(8,128)(2,1)S(1)} custom-call(bf16[128,2176]{1,0:T(8,128)(2,1)S(1)} %collective-permute-done.7.far_ref, bf16[1280,2176]{1,0:T(8,128)(2,1)S(1)} %get-tuple-element.64.held, f32[8,1280]{1,0:T(8,128)S(1)} %get-tuple-element.65.facts_ref), custom_call_target="tpu_custom_call" | custom-call | flops 5347737600 | bytes 5570560 | tf_op jit(solution)/shard_map/match_far/pallas_call | solution.py:321
  51.3 1.6 %collective-permute-start.14 = (s16[128,2176]{1,0:T(8,128)(2,1)S(1)}, s16[128,2176]{1,0:T(8,128)(2,1)S(1)}, u32[]{:S(2)}, u32[]{:S(2)}) collective-permute-start(s16[128,2176]{1,0:T(8,128)(2,1)S(1)} %match_far.3), channel_id=1, source_target_pairs={{0,1},{1,0},{2,3},{3,2},{4,5},{5,4},{6,7},{7,6},{8,9},{9,8},{10,11... | collective-permute-start | bytes 1671176 | tf_op jit(solution)/shard_map/ppermute | solution.py:345
  52.8 4.4 %match_far.2 = s16[128,2176]{1,0:T(8,128)(2,1)S(1)} custom-call(bf16[128,2176]{1,0:T(8,128)(2,1)S(1)} %collective-permute-done.6.far_ref, bf16[1280,2176]{1,0:T(8,128)(2,1)S(1)} %get-tuple-element.56.held, f32[8,1280]{1,0:T(8,128)S(1)} %get-tuple-element.57.facts_ref), custom_call_target="tpu_custom_call" | custom-call | flops 5347737600 | bytes 5570560 | tf_op jit(solution)/shard_map/match_far/pallas_call | solution.py:321
  57.2 0.6 collective-permute-start.10
  57.8 3.0 %collective-permute-done.14.refs_1_ = s16[128,2176]{1,0:T(8,128)(2,1)S(1)} collective-permute-done((s16[128,2176]{1,0:T(8,128)(2,1)S(1)}, s16[128,2176]{1,0:T(8,128)(2,1)S(1)}, u32[]{:S(2)}, u32[]{:S(2)}) %collective-permute-start.14) | collective-permute-done | bytes 557088 | tf_op jit(solution)/shard_map/ppermute | solution.py:345
  60.9 0.7 merge.6
  61.6 1.6 %collective-permute-start.15 = (s16[64,2176]{1,0:T(8,128)(2,1)S(1)}, s16[64,2176]{1,0:T(8,128)(2,1)S(1)}, u32[]{:S(2)}, u32[]{:S(2)}) collective-permute-start(s16[64,2176]{1,0:T(8,128)(2,1)S(1)} %get-tuple-element.67), channel_id=1, source_target_pairs={{0,2},{1,3},{2,0},{3,1},{4,6},{5,7},{6,4},{7,5},{8,10},{9,11},{10,... | collective-permute-start | bytes 835592 | tf_op jit(solution)/shard_map/ppermute | solution.py:345
  63.2 7.6 %collective-permute-done.10.refs_1_ = s16[128,2176]{1,0:T(8,128)(2,1)S(1)} collective-permute-done((s16[128,2176]{1,0:T(8,128)(2,1)S(1)}, s16[128,2176]{1,0:T(8,128)(2,1)S(1)}, u32[]{:S(2)}, u32[]{:S(2)}) %collective-permute-start.10) | collective-permute-done | bytes 557088 | tf_op jit(solution)/shard_map/ppermute | solution.py:345
  70.7 0.7 merge.4
  71.5 1.6 %collective-permute-start.11 = (s16[64,2176]{1,0:T(8,128)(2,1)S(1)}, s16[64,2176]{1,0:T(8,128)(2,1)S(1)}, u32[]{:S(2)}, u32[]{:S(2)}) collective-permute-start(s16[64,2176]{1,0:T(8,128)(2,1)S(1)} %get-tuple-element.59), channel_id=1, source_target_pairs={{0,2},{1,3},{2,0},{3,1},{4,6},{5,7},{6,4},{7,5},{8,10},{9,11},{10,... | collective-permute-start | bytes 835592 | tf_op jit(solution)/shard_map/ppermute | solution.py:345
  73.5 3.6 %collective-permute-start.16 = (s16[32,2176]{1,0:T(8,128)(2,1)S(1)}, s16[32,2176]{1,0:T(8,128)(2,1)S(1)}, u32[]{:S(2)}, u32[]{:S(2)}) collective-permute-start(s16[32,2176]{1,0:T(8,128)(2,1)S(1)} %get-tuple-element.68), channel_id=1, source_target_pairs={{4,0},{5,1},{6,2},{7,3},{0,4},{1,5},{2,6},{3,7},{20,8},{21,9},{22,... | collective-permute-start | bytes 417800 | tf_op jit(solution)/shard_map/ppermute | solution.py:357
  77.1 2.6 %collective-permute-start.17 = (s16[32,2176]{1,0:T(8,128)(2,1)S(1)}, s16[32,2176]{1,0:T(8,128)(2,1)S(1)}, u32[]{:S(2)}, u32[]{:S(2)}) collective-permute-start(s16[32,2176]{1,0:T(8,128)(2,1)S(1)} %get-tuple-element.69), channel_id=1, source_target_pairs={{4,16},{5,17},{6,18},{7,19},{0,20},{1,21},{2,22},{3,23},{20,24},{2... | collective-permute-start | bytes 417800 | tf_op jit(solution)/shard_map/ppermute | solution.py:357
  80.1 0.7 collective-permute-start.12
  80.8 5.7 %collective-permute-start.13 = (s16[32,2176]{1,0:T(8,128)(2,1)S(1)}, s16[32,2176]{1,0:T(8,128)(2,1)S(1)}, u32[]{:S(2)}, u32[]{:S(2)}) collective-permute-start(s16[32,2176]{1,0:T(8,128)(2,1)S(1)} %get-tuple-element.61), channel_id=1, source_target_pairs={{0,16},{1,17},{2,18},{3,19},{4,20},{5,21},{6,22},{7,23},{16,24},{1... | collective-permute-start | bytes 417800 | tf_op jit(solution)/shard_map/ppermute | solution.py:357
  86.5 5.4 %collective-permute-done.13.refs_1_ = s16[32,2176]{1,0:T(8,128)(2,1)S(1)} collective-permute-done((s16[32,2176]{1,0:T(8,128)(2,1)S(1)}, s16[32,2176]{1,0:T(8,128)(2,1)S(1)}, u32[]{:S(2)}, u32[]{:S(2)}) %collective-permute-start.13) | collective-permute-done | bytes 139296 | tf_op jit(solution)/shard_map/ppermute | solution.py:357
  91.9 0.9 %finish.1 = (bf16[32,2048]{1,0:T(8,128)(2,1)}, f32[1,32]{1,0:T(1,128)}, f32[1,32]{1,0:T(1,128)}) custom-call(s16[32,2176]{1,0:T(8,128)(2,1)S(1)} %collective-permute-done.12.refs_0_, s16[32,2176]{1,0:T(8,128)(2,1)S(1)} %collective-permute-done.13.refs_1_, s16[32,2176]{1,0:T(8,128)(2,1)S(1)} %collective-permute-done.16.refs_2_, ...), custom_call_target="tpu_custom_call" | custom-call | tf_op jit(solution)/shard_map/finish/pallas_call | solution.py:166
  (27 shorter events, 2.0 us)
Async XLA Ops:
  0.6 2.7 %collective-permute-start = (bf16[32,2048]{1,0:T(8,128)(2,1)}, bf16[32,2048]{1,0:T(8,128)(2,1)S(1)}, u32[]{:S(2)}, u32[]{:S(2)}) collective-permute-start(bf16[32,2048]{1,0:T(8,128)(2,1)} %param.5), channel_id=1, source_target_pairs={{0,16},{16,0},{1,17},{17,1},{2,18},{18,2},{3,19},{19,3},{4,20},{20... | collective-permute-start | bytes 393224 | tf_op jit(solution)/shard_map/ppermute | solution.py:360
  1.1 2.1 %collective-permute-start.1 = (s32[32]{0:T(128)}, s32[32]{0:T(128)S(1)}, u32[]{:S(2)}, u32[]{:S(2)}) collective-permute-start(s32[32]{0:T(128)} %param.6), channel_id=1, source_target_pairs={{0,16},{16,0},{1,17},{17,1},{2,18},{18,2},{3,19},{19,3},{4,20},{20... | collective-permute-start | bytes 392 | tf_op jit(solution)/shard_map/ppermute | solution.py:360
  4.4 13.1 %collective-permute-start.2 = (bf16[64,2176]{1,0:T(8,128)(2,1)S(1)}, bf16[64,2176]{1,0:T(8,128)(2,1)S(1)}, u32[]{:S(2)}, u32[]{:S(2)}) collective-permute-start(bf16[64,2176]{1,0:T(8,128)(2,1)S(1)} %pad_maximum_fusion.2), channel_id=1, source_target_pairs={{0,0},{1,1},{2,2},{3,3},{4,4},{5,5},{6,6},{7,7},{8,16},{9,17},{10,... | collective-permute-start | bytes 835592 | tf_op jit(solution)/shard_map/ppermute | solution.py:354
  5.1 12.4 %collective-permute-start.3 = (bf16[64,2176]{1,0:T(8,128)(2,1)S(1)}, bf16[64,2176]{1,0:T(8,128)(2,1)S(1)}, u32[]{:S(2)}, u32[]{:S(2)}) collective-permute-start(bf16[64,2176]{1,0:T(8,128)(2,1)S(1)} %pad_maximum_fusion.2), channel_id=1, source_target_pairs={{0,4},{1,5},{2,6},{3,7},{4,0},{5,1},{6,2},{7,3},{8,20},{9,21},{10,... | collective-permute-start | bytes 835592 | tf_op jit(solution)/shard_map/ppermute | solution.py:354
  8.1 2.8 %copy-start = (bf16[1536,2048]{1,0:T(8,128)(2,1)S(1)}, bf16[1536,2048]{1,0:T(8,128)(2,1)}, u32[]{:S(2)}) copy-start(bf16[1536,2048]{1,0:T(8,128)(2,1)} %library_ref.1) | copy-start | bytes 18874372
  17.4 16.1 %collective-permute-start.9 = (bf16[1536,2176]{1,0:T(8,128)(2,1)}, bf16[1536,2176]{1,0:T(8,128)(2,1)}, u32[]{:S(2)}, u32[]{:S(2)}) collective-permute-start(bf16[1536,2176]{1,0:T(8,128)(2,1)} %get-tuple-element.47.refs_0_), channel_id=1, source_target_pairs={{0,16},{16,0},{1,17},{17,1},{2,18},{18,2},{3,19},{19,3},{4,20},{20... | collective-permute-start | bytes 20054024 | tf_op jit(solution)/shard_map/ppermute | solution.py:360
  20.8 10.4 %collective-permute-start.4 = (bf16[64,2176]{1,0:T(8,128)(2,1)S(1)}, bf16[64,2176]{1,0:T(8,128)(2,1)S(1)}, u32[]{:S(2)}, u32[]{:S(2)}) collective-permute-start(bf16[64,2176]{1,0:T(8,128)(2,1)S(1)} %collective-permute-done.2.refs_2_), channel_id=1, source_target_pairs={{0,2},{1,3},{2,0},{3,1},{4,6},{5,7},{6,4},{7,5},{8,10},{9,11},{10,... | collective-permute-start | bytes 835592 | tf_op jit(solution)/shard_map/ppermute | solution.py:345
  22.3 8.9 %collective-permute-start.5 = (bf16[64,2176]{1,0:T(8,128)(2,1)S(1)}, bf16[64,2176]{1,0:T(8,128)(2,1)S(1)}, u32[]{:S(2)}, u32[]{:S(2)}) collective-permute-start(bf16[64,2176]{1,0:T(8,128)(2,1)S(1)} %collective-permute-done.3.refs_4_), channel_id=1, source_target_pairs={{0,2},{1,3},{2,0},{3,1},{4,6},{5,7},{6,4},{7,5},{8,10},{9,11},{10,... | collective-permute-start | bytes 835592 | tf_op jit(solution)/shard_map/ppermute | solution.py:345
  23.0 8.2 %collective-permute-start.8 = (s32[96]{0:T(128)S(1)}, s32[96]{0:T(128)S(1)}, u32[]{:S(2)}, u32[]{:S(2)}) collective-permute-start(s32[96]{0:T(128)S(1)} %slice_reduce_fusion), channel_id=1, source_target_pairs={{0,16},{16,0},{1,17},{17,1},{2,18},{18,2},{3,19},{19,3},{4,20},{20... | collective-permute-start | bytes 1160 | tf_op jit(solution)/shard_map/ppermute | solution.py:360
  31.3 13.8 %collective-permute-start.7 = (bf16[128,2176]{1,0:T(8,128)(2,1)S(1)}, bf16[128,2176]{1,0:T(8,128)(2,1)S(1)}, u32[]{:S(2)}, u32[]{:S(2)}) collective-permute-start(bf16[128,2176]{1,0:T(8,128)(2,1)S(1)} %pad_maximum_fusion.1), channel_id=1, source_target_pairs={{0,1},{1,0},{2,3},{3,2},{4,5},{5,4},{6,7},{7,6},{8,9},{9,8},{10,11... | collective-permute-start | bytes 1671176 | tf_op jit(solution)/shard_map/ppermute | solution.py:345
  32.9 14.0 %collective-permute-start.6 = (bf16[128,2176]{1,0:T(8,128)(2,1)S(1)}, bf16[128,2176]{1,0:T(8,128)(2,1)S(1)}, u32[]{:S(2)}, u32[]{:S(2)}) collective-permute-start(bf16[128,2176]{1,0:T(8,128)(2,1)S(1)} %pad_maximum_fusion), channel_id=1, source_target_pairs={{0,1},{1,0},{2,3},{3,2},{4,5},{5,4},{6,7},{7,6},{8,9},{9,8},{10,11... | collective-permute-start | bytes 1671176 | tf_op jit(solution)/shard_map/ppermute | solution.py:345
  51.3 9.6 %collective-permute-start.14 = (s16[128,2176]{1,0:T(8,128)(2,1)S(1)}, s16[128,2176]{1,0:T(8,128)(2,1)S(1)}, u32[]{:S(2)}, u32[]{:S(2)}) collective-permute-start(s16[128,2176]{1,0:T(8,128)(2,1)S(1)} %match_far.3), channel_id=1, source_target_pairs={{0,1},{1,0},{2,3},{3,2},{4,5},{5,4},{6,7},{7,6},{8,9},{9,8},{10,11... | collective-permute-start | bytes 1671176 | tf_op jit(solution)/shard_map/ppermute | solution.py:345
  57.2 13.5 %collective-permute-start.10 = (s16[128,2176]{1,0:T(8,128)(2,1)S(1)}, s16[128,2176]{1,0:T(8,128)(2,1)S(1)}, u32[]{:S(2)}, u32[]{:S(2)}) collective-permute-start(s16[128,2176]{1,0:T(8,128)(2,1)S(1)} %match_far.2), channel_id=1, source_target_pairs={{0,1},{1,0},{2,3},{3,2},{4,5},{5,4},{6,7},{7,6},{8,9},{9,8},{10,11... | collective-permute-start | bytes 1671176 | tf_op jit(solution)/shard_map/ppermute | solution.py:345
  61.6 11.4 %collective-permute-start.15 = (s16[64,2176]{1,0:T(8,128)(2,1)S(1)}, s16[64,2176]{1,0:T(8,128)(2,1)S(1)}, u32[]{:S(2)}, u32[]{:S(2)}) collective-permute-start(s16[64,2176]{1,0:T(8,128)(2,1)S(1)} %get-tuple-element.67), channel_id=1, source_target_pairs={{0,2},{1,3},{2,0},{3,1},{4,6},{5,7},{6,4},{7,5},{8,10},{9,11},{10,... | collective-permute-start | bytes 835592 | tf_op jit(solution)/shard_map/ppermute | solution.py:345
  71.5 8.2 %collective-permute-start.11 = (s16[64,2176]{1,0:T(8,128)(2,1)S(1)}, s16[64,2176]{1,0:T(8,128)(2,1)S(1)}, u32[]{:S(2)}, u32[]{:S(2)}) collective-permute-start(s16[64,2176]{1,0:T(8,128)(2,1)S(1)} %get-tuple-element.59), channel_id=1, source_target_pairs={{0,2},{1,3},{2,0},{3,1},{4,6},{5,7},{6,4},{7,5},{8,10},{9,11},{10,... | collective-permute-start | bytes 835592 | tf_op jit(solution)/shard_map/ppermute | solution.py:345
  73.5 13.0 %collective-permute-start.16 = (s16[32,2176]{1,0:T(8,128)(2,1)S(1)}, s16[32,2176]{1,0:T(8,128)(2,1)S(1)}, u32[]{:S(2)}, u32[]{:S(2)}) collective-permute-start(s16[32,2176]{1,0:T(8,128)(2,1)S(1)} %get-tuple-element.68), channel_id=1, source_target_pairs={{4,0},{5,1},{6,2},{7,3},{0,4},{1,5},{2,6},{3,7},{20,8},{21,9},{22,... | collective-permute-start | bytes 417800 | tf_op jit(solution)/shard_map/ppermute | solution.py:357
  77.1 9.4 %collective-permute-start.17 = (s16[32,2176]{1,0:T(8,128)(2,1)S(1)}, s16[32,2176]{1,0:T(8,128)(2,1)S(1)}, u32[]{:S(2)}, u32[]{:S(2)}) collective-permute-start(s16[32,2176]{1,0:T(8,128)(2,1)S(1)} %get-tuple-element.69), channel_id=1, source_target_pairs={{4,16},{5,17},{6,18},{7,19},{0,20},{1,21},{2,22},{3,23},{20,24},{2... | collective-permute-start | bytes 417800 | tf_op jit(solution)/shard_map/ppermute | solution.py:357
  80.1 6.3 %collective-permute-start.12 = (s16[32,2176]{1,0:T(8,128)(2,1)S(1)}, s16[32,2176]{1,0:T(8,128)(2,1)S(1)}, u32[]{:S(2)}, u32[]{:S(2)}) collective-permute-start(s16[32,2176]{1,0:T(8,128)(2,1)S(1)} %get-tuple-element.60), channel_id=1, source_target_pairs={{0,0},{1,1},{2,2},{3,3},{4,4},{5,5},{6,6},{7,7},{16,8},{17,9},{18,... | collective-permute-start | bytes 417800 | tf_op jit(solution)/shard_map/ppermute | solution.py:357
  80.8 11.1 %collective-permute-start.13 = (s16[32,2176]{1,0:T(8,128)(2,1)S(1)}, s16[32,2176]{1,0:T(8,128)(2,1)S(1)}, u32[]{:S(2)}, u32[]{:S(2)}) collective-permute-start(s16[32,2176]{1,0:T(8,128)(2,1)S(1)} %get-tuple-element.61), channel_id=1, source_target_pairs={{0,16},{1,17},{2,18},{3,19},{4,20},{5,21},{6,22},{7,23},{16,24},{1... | collective-permute-start | bytes 417800 | tf_op jit(solution)/shard_map/ppermute | solution.py:357

commit v3 on v2

--- a/solution.py
+++ b/solution.py
@@ -34,15 +34,24 @@
     return pieces
 
 
-def sort_kernel(buckets, bucket_ref, time_ref, library_ref, sorted_ref, first_ref):
+def sort_kernel(buckets, time_ref, bucket_ref, library_ref, sorted_ref, first_ref, facts_ref):
     count, bins = library_ref.shape
+    total = time_ref.shape[0]
+
+    @pl.when(pl.program_id(0) == 0)
+    def _():
+        facts_ref[0:1, :] = time_ref[...].astype(jnp.float32).reshape(1, total)
+        facts_ref[1:2, :] = bucket_ref[...].astype(jnp.float32).reshape(1, total)
+
 
     def earlier(n):
         order = [lax.broadcasted_iota(jnp.int32, (n, n), d) for d in range(2)]
         return (order[0] < order[1]).astype(jnp.float32).astype(jnp.bfloat16)
 
+    here = pl.ds(pl.multiple_of(pl.program_id(0) * count, LANES), count)
+    time, bucket = facts_ref[0:1, here], facts_ref[1:2, here]
     member = (
-        bucket_ref[...] == lax.broadcasted_iota(jnp.int32, (buckets, count), 0)
+        bucket == lax.broadcasted_iota(jnp.int32, (buckets, count), 0).astype(jnp.float32)
     ).astype(jnp.float32)
     member16 = member.astype(jnp.bfloat16)
     before = jnp.dot(member16, earlier(count), preferred_element_type=jnp.float32)
@@ -62,7 +71,7 @@
     wide = entries.astype(jnp.float32)
     scale = lax.rsqrt(jnp.sum(wide * wide, axis=1, keepdims=True) / bins + EPSILON)
     which = lax.broadcasted_iota(jnp.int32, (LANES, count), 0)
-    facts = jnp.where(which == 0, time_ref[...], jnp.where(which == 1, bucket_ref[...].astype(jnp.float32), 0.0)).T
+    facts = jnp.where(which == 0, time, jnp.where(which == 1, bucket, 0.0)).T
     lane = lax.broadcasted_iota(jnp.int32, (count, LANES), 1)
     for at, piece in enumerate(split3(scale)):
         facts = jnp.where(lane == 2 + at, piece.astype(jnp.float32), facts)
@@ -77,7 +86,6 @@
 def sort_library(blocks, buckets, library, library_time, library_bucket):
     total, bins = library.shape
     count = total // blocks
-    row = pl.BlockSpec((1, count), lambda n: (0, n))
     return pl.pallas_call(
         functools.partial(sort_kernel, buckets),
         out_shape=(
@@ -85,15 +93,20 @@
             jax.ShapeDtypeStruct((blocks * buckets, LANES), jnp.int32),
         ),
         grid=(blocks,),
-        in_specs=[row, row, pl.BlockSpec((count, bins), lambda n: (n, 0))],
+        in_specs=[
+            pl.BlockSpec((total,), lambda n: (0,)),
+            pl.BlockSpec((total,), lambda n: (0,)),
+            pl.BlockSpec((count, bins), lambda n: (n, 0)),
+        ],
         out_specs=[
             pl.BlockSpec((count, bins + LANES), lambda n: (n, 0)),
             pl.BlockSpec((buckets, LANES), lambda n: (n, 0)),
         ],
+        scratch_shapes=[pltpu.VMEM((8, total), jnp.float32)],
         compiler_params=pltpu.CompilerParams(vmem_limit_bytes=SORT_MIB * MIB),
-        cost_estimate=pl.CostEstimate(flops=5 * count * total * bins, bytes_accessed=(4 * total * bins) // 1, transcendentals=0),
+        cost_estimate=pl.CostEstimate(flops=5 * count * total * bins, bytes_accessed=4 * total * bins, transcendentals=0),
         name="sort_library",
-    )(library_bucket, library_time, library)
+    )(library_time, library_bucket, library)
 
 
 def encode(out, rows, vector, k, total, time_sum):
@@ -147,7 +160,7 @@
         functools.partial(merge_kernel, pieces),
         out_shape=(out,) * pieces,
         compiler_params=pltpu.CompilerParams(vmem_limit_bytes=MERGE_MIB * MIB),
-        cost_estimate=pl.CostEstimate(flops=(8 * rows * width * len(parts)) // 1, bytes_accessed=(2 * rows * width * (len(parts) + 1)) // 1, transcendentals=0),
+        cost_estimate=pl.CostEstimate(flops=8 * rows * width * len(parts), bytes_accessed=2 * rows * width * (len(parts) + 1), transcendentals=0),
         name="merge",
     )(*parts)
 
@@ -176,9 +189,33 @@
     return spectra, time.reshape(rows), evidence.reshape(rows)
 
 
+def pack_kernel(*refs):
+    *parts, out = refs
+    count = len(parts) // 2
+    rows, bins = parts[0].shape
+    for d in range(count):
+        at = slice(d * rows, (d + 1) * rows)
+        out[at, :bins] = parts[d][...]
+        bucket = parts[count + d][...].reshape(1, rows).astype(jnp.float32)
+        if rows < LANES:
+            bucket = jnp.concatenate([bucket, jnp.zeros((1, LANES - rows), jnp.float32)], axis=1)
+        columns = jnp.broadcast_to(bucket, (LANES, LANES)).T
+        out[at, bins:] = columns[:rows].astype(jnp.bfloat16)
+
+
+def pack(queries, buckets):
+    rows, bins = queries[0].shape
+    return pl.pallas_call(
+        pack_kernel,
+        out_shape=jax.ShapeDtypeStruct((len(queries) * rows, bins + LANES), jnp.bfloat16),
+        compiler_params=pltpu.CompilerParams(vmem_limit_bytes=MERGE_MIB * MIB),
+        name="pack",
+    )(*queries, *buckets)
+
+
 def window_kernel(shards, blocks, buckets, quad_ref, first_ref, *refs):
     libraries, refs, arrived = refs[:shards], refs[shards:-1], refs[-1]
-    nears, seconds, helds, factses, parts = (refs[at :: 5] for at in range(5))
+    nears, seconds, helds, factses, *parts = (refs[at :: 6] for at in range(6))
     count = libraries[0].shape[0] // blocks
     entries, width = helds[0].shape
     share = entries // shards
@@ -243,12 +280,12 @@
         scale = columns[2:3] + columns[3:4] + columns[4:5]
         facts = jnp.where(which == 0, columns[0:1], jnp.where(which == 1, bucket, scale))
         factses[at][...] = facts
-        weigh(queries, jnp.concatenate(products, axis=1), facts, held, parts[at])
-
-
-def rest_kernel(far_ref, held, facts_ref, part_ref):
+        weigh(queries, jnp.concatenate(products, axis=1), facts, held, [p[at] for p in parts])
+
+
+def rest_kernel(far_ref, held, facts_ref, *parts):
     queries = far_ref[...]
-    weigh(queries, score(queries, held), facts_ref[...], held, part_ref)
+    weigh(queries, score(queries, held), facts_ref[...], held, parts)
 
 
 def score(queries, held):
@@ -258,7 +295,7 @@
     )
 
 
-def weigh(queries, products, facts, held, part_ref):
+def weigh(queries, products, facts, held, parts):
     rows, width = queries.shape
     bins = width - LANES
     wide = queries[:, :bins].astype(jnp.float32)
@@ -276,7 +313,10 @@
     lower = (weights - upper.astype(jnp.float32)).astype(jnp.bfloat16)
     both = jnp.concatenate([upper, lower], axis=0)
     sums = jnp.dot(both, held[:, :bins], preferred_element_type=jnp.float32)
-    encode(part_ref, slice(None), sums[:rows] + sums[rows:], k, total, time_sum)
+    vector = sums[:rows] + sums[rows:]
+    for n, part in enumerate(parts):
+        at = slice(n * rows // len(parts), (n + 1) * rows // len(parts))
+        encode(part, slice(None), vector[at], k[at], total[at], time_sum[at])
 
 
 def match_near(quad, firsts, near, second, libraries, per_bucket, blocks, buckets):
@@ -290,7 +330,8 @@
     outs = (
         jax.ShapeDtypeStruct((entries, width), jnp.bfloat16),
         jax.ShapeDtypeStruct((8, entries), jnp.float32),
-        jax.ShapeDtypeStruct((2 * rows, width), jnp.int16),
+        jax.ShapeDtypeStruct((rows, width), jnp.int16),
+        jax.ShapeDtypeStruct((rows, width), jnp.int16),
     )
 
     def kernel(quad_ref, first_ref, *refs):
@@ -298,14 +339,14 @@
         by_quad = []
         for at in range(quads):
             by_quad += ins[shards + 2 * at : shards + 2 * at + 2]
-            by_quad += rest[3 * at : 3 * at + 3]
+            by_quad += rest[4 * at : 4 * at + 4]
         window_kernel(shards, blocks, buckets, quad_ref, first_ref, *ins[:shards], *by_quad, rest[-1])
 
     results = pl.pallas_call(
         kernel,
         out_shape=outs * quads,
         in_specs=[smem, smem] + [pl.BlockSpec(memory_space=pl.ANY)] * shards + [vmem] * (2 * quads),
-        out_specs=[vmem] * (3 * quads),
+        out_specs=[vmem] * (4 * quads),
         scratch_shapes=[pltpu.SemaphoreType.DMA((quads, shards))],
         compiler_params=pltpu.CompilerParams(vmem_limit_bytes=MATCH_MIB * MIB),
         cost_estimate=pl.CostEstimate(
@@ -313,16 +354,16 @@
         ),
         name="match_near",
     )(quad, firsts, *libraries, *[q for both in zip(near, second) for q in both])
-    return [results[3 * at : 3 * at + 3] for at in range(quads)]
+    return [results[4 * at : 4 * at + 4] for at in range(quads)]
 
 
 def match_far(far, held, facts):
     rows, width = far.shape
     return pl.pallas_call(
         rest_kernel,
-        out_shape=jax.ShapeDtypeStruct((rows, width), jnp.int16),
+        out_shape=(jax.ShapeDtypeStruct((rows // 2, width), jnp.int16),) * 2,
         compiler_params=pltpu.CompilerParams(vmem_limit_bytes=MATCH_MIB * MIB),
-        cost_estimate=pl.CostEstimate(flops=15 * rows * held.shape[0] * width, bytes_accessed=(2 * held.size) // 1, transcendentals=0),
+        cost_estimate=pl.CostEstimate(flops=15 * rows * held.shape[0] * width, bytes_accessed=2 * held.size, transcendentals=0),
         name="match_far",
     )(far, held, facts)
 
@@ -360,16 +401,14 @@
         return lax.ppermute(value, "query", [(c, c ^ distance) for c in range(shards)])
 
     blocks = 3
-    rows = jnp.concatenate([queries] + [swap(queries, d) for d in range(1, shards)], axis=0)
-    row_bucket = jnp.concatenate([query_bucket] + [swap(query_bucket, d) for d in range(1, shards)])
-    bucket_columns = jnp.broadcast_to(row_bucket.astype(jnp.bfloat16)[:, None], (shards * own_rows, LANES))
-    own = jnp.concatenate([rows, bucket_columns], axis=1)
+    own = pack(
+        [queries] + [swap(queries, d) for d in range(1, shards)],
+        [query_bucket] + [swap(query_bucket, d) for d in range(1, shards)],
+    )
 
     tie = lax.optimization_barrier
     near = [spread(own, at) for at in range(quads)]
-    bucket_row = library_bucket.reshape(1, -1)
-    time_row = library_time.astype(jnp.float32).reshape(1, -1)
-    entries, firsts = sort_library(blocks, buckets, library, time_row, bucket_row)
+    entries, firsts = sort_library(blocks, buckets, library, library_time, library_bucket)
     entries, firsts, near = tie((entries, firsts, near))
     libraries = [entries] + [swap(entries, d) for d in range(1, shards)]
     firsts = firsts[:, 0]
@@ -382,13 +421,18 @@
     quad = jnp.stack([core * quads + (at ^ (layer % quads)) for at in range(quads)]).astype(jnp.int32)
     matched = match_near(quad, firsts, near, second, libraries, per_bucket, blocks, buckets)
     far, matched = tie((far, matched))
-    from_far = []
-    for at, (held, facts, _) in enumerate(matched):
-        from_far.append(send(match_far(far[at], held, facts), 1, 2))
+    from_second = [send(second_sums, 2, 1) for _, _, _, second_sums in matched]
+    first_sums, from_corner = [], []
+    for at, (held, facts, _, _) in enumerate(matched):
+        if at == quads - 1:
+            far[at], from_second = tie((far[at], from_second))
+        sums, corner_sums = match_far(far[at], held, facts)
+        first_sums.append(sums)
+        from_corner.append(send(corner_sums, 2, 1))
     returned = []
-    for at, (_, _, near_sums) in enumerate(matched):
-        near_sums, second_sums = merge([near_sums, from_far[at]], 2)
-        pieces = merge([near_sums, send(second_sums, 2, 1)], shards)
+    for at, (_, _, near_sums, _) in enumerate(matched):
+        (sums,) = merge([first_sums[at], from_corner[at]], 1)
+        pieces = merge([near_sums, from_second[at], send(sums, 1, 2)], shards)
         returned += [collect(piece, at, d) for d, piece in enumerate(pieces)]
     return finish(returned)
 

time: 93.1 us -> 91.2 us (0.980)
  waiting for transfers between devices: 25.9 us -> 24.2 us
  other arithmetic: 1.91 us -> 0.24 us
  local copies, waits for them, and re-layouts: 4.35 us -> 5.83 us
    ppermute x8 -> x10, waiting for transfers between devices: 12.4 us -> 9.25 us  [send(): return lax.ppermute(value, ('query', 'lib'), pairs)]
    unnamed x2 -> x10, local copies, waits for them, and re-layouts: 2.78 us -> 5.73 us
    ppermute x4, starting transfers between devices: 12.5 us -> 10.2 us  [collect(): lax.ppermute(value, ('query', 'lib'), [(b, a) for a, b in layer_pairs(str...]
    ppermute x8 -> x10, starting transfers between devices: 9.51 us -> 11.4 us  [send(): return lax.ppermute(value, ('query', 'lib'), pairs)]
    reshape x2 -> x0, local copies, waits for them, and re-layouts: 1.39 us -> none  [the longest x1 0.7 us: per_device(): bucket_row = library_bucket.reshape(1, -1)]
    ppermute x4, waiting for transfers between devices: 8.06 us -> 9.24 us  [swap(): lax.ppermute(value, 'query', [(c, c ^ distance) for c in range(shards)])]
    concatenate x2 -> x0, other arithmetic: 1.01 us -> none  [the longest x1 0.93 us: per_device(): own = jnp.concatenate([rows, bucket_columns], axis=1)]
    pallas_call x2 -> x3, Pallas kernels: 8.79 us -> 8.84 us  [the longest x2 8.77 us: match_far(): pl.pallas_call(rest_kernel, out_shape=(jax.ShapeDtypeStruct((rows // 2, w...]
  transfers between devices with their start and end apart: 18 -> 20, of which waited for: 5 -> 7; matrix products, arithmetic and copies ran while one was open for 3% -> 0% of each run, Pallas kernels for 27% -> 32%
where the time goes in v3:
time: 91.2 us; the launch traced here: 90.1 us
  Pallas kernels  29.7 us (33%)
  starting transfers between devices  29.4 us (32%)
  waiting for transfers between devices  24.2 us (27%)
  local copies, waits for them, and re-layouts  5.83 us (6%)
    pallas_call x1, Pallas kernels, match_near(): pl.pallas_call(kernel, out_shape=outs * quads, in_specs=[smem, smem] + [p...  11.6 us
    ppermute x10, starting transfers between devices, send(): return lax.ppermute(value, ('query', 'lib'), pairs)  11.4 us
    ppermute x4, starting transfers between devices, collect(): lax.ppermute(value, ('query', 'lib'), [(b, a) for a, b in layer_pairs(str...  10.2 us
    ppermute x10, waiting for transfers between devices, send(): return lax.ppermute(value, ('query', 'lib'), pairs)  9.25 us
    ppermute x4, waiting for transfers between devices, swap(): lax.ppermute(value, 'query', [(c, c ^ distance) for c in range(shards)])  9.24 us
    pallas_call x2, Pallas kernels, match_far(): pl.pallas_call(rest_kernel, out_shape=(jax.ShapeDtypeStruct((rows // 2, w...  8.77 us
    pallas_call x1, Pallas kernels, sort_library(): pl.pallas_call(functools.partial(sort_kernel, buckets), out_shape=(jax.Sh...  6.6 us
    unnamed x10, local copies, waits for them, and re-layouts  5.73 us
  transfers between devices with their start and end apart: 20, of which 7 were waited for; matrix products, arithmetic and copies ran while one was open for 0% of the time, Pallas kernels for 32%

profile of v3, /device:TPU:0, one launch (start us, length us, event | category | flops | bytes accessed | tf_op | source)
XLA Modules:
  0.0 90.1 jit_solution(6729192920375124063)
XLA Ops:
  0.6 0.5 collective-permute-start
  1.2 1.2 %collective-permute-done.1.refs_3_ = s32[32]{0:T(128)S(1)} collective-permute-done((s32[32]{0:T(128)}, s32[32]{0:T(128)S(1)}, u32[]{:S(2)}, u32[]{:S(2)}) %collective-permute-start.1) | collective-permute-done | bytes 160 | tf_op jit(solution)/shard_map/ppermute | solution.py:401
  2.4 0.9 %copy-done = bf16[32,2048]{1,0:T(8,128)(2,1)S(1)} copy-done((bf16[32,2048]{1,0:T(8,128)(2,1)S(1)}, bf16[32,2048]{1,0:T(8,128)(2,1)}, u32[]{:S(2)}) %copy-start) | copy-done | bytes 131096
  3.3 0.7 copy-done.1
  4.0 0.7 collective-permute-start.2
  4.7 2.9 %collective-permute-start.3 = (bf16[64,2176]{1,0:T(8,128)(2,1)S(1)}, bf16[64,2176]{1,0:T(8,128)(2,1)S(1)}, u32[]{:S(2)}, u32[]{:S(2)}) collective-permute-start(bf16[64,2176]{1,0:T(8,128)(2,1)S(1)} %pack.1), channel_id=1, source_target_pairs={{0,4},{1,5},{2,6},{3,7},{4,0},{5,1},{6,2},{7,3},{8,20},{9,21},{10,... | collective-permute-start | bytes 835592 | tf_op jit(solution)/shard_map/ppermute | solution.py:395
  7.7 2.8 %copy-done.2 = bf16[1536,2048]{1,0:T(8,128)(2,1)S(1)} copy-done((bf16[1536,2048]{1,0:T(8,128)(2,1)S(1)}, bf16[1536,2048]{1,0:T(8,128)(2,1)}, u32[]{:S(2)}) %copy-start.2) | copy-done | bytes 6291480
  10.5 0.7 copy-done.3
  11.2 0.7 copy-done.4
  11.8 6.6 %sort_library.1 = (bf16[1536,2176]{1,0:T(8,128)(2,1)}, s32[96,128]{1,0:T(8,128)S(1)}) custom-call(bf16[1536]{0:T(1024)(128)(2,1)S(1)} %copy-done.4, s32[1536]{0:T(1024)S(1)} %copy-done.3, bf16[1536,2048]{1,0:T(8,128)(2,1)S(1)} %copy-done.2), custom_call_target="tpu_custom_call" | custom-call | flops 8053063680 | bytes 12582912 | tf_op jit(solution)/shard_map/sort_library/pallas_call | solution.py:89
  18.4 3.5 %collective-permute-start.9 = (bf16[1536,2176]{1,0:T(8,128)(2,1)}, bf16[1536,2176]{1,0:T(8,128)(2,1)}, u32[]{:S(2)}, u32[]{:S(2)}) collective-permute-start(bf16[1536,2176]{1,0:T(8,128)(2,1)} %get-tuple-element.54.refs_0_), channel_id=1, source_target_pairs={{0,16},{16,0},{1,17},{17,1},{2,18},{18,2},{3,19},{19,3},{4,20},{20... | collective-permute-start | bytes 20054024 | tf_op jit(solution)/shard_map/ppermute | solution.py:401
  22.0 1.5 %collective-permute-start.4 = (bf16[64,2176]{1,0:T(8,128)(2,1)S(1)}, bf16[64,2176]{1,0:T(8,128)(2,1)S(1)}, u32[]{:S(2)}, u32[]{:S(2)}) collective-permute-start(bf16[64,2176]{1,0:T(8,128)(2,1)S(1)} %collective-permute-done.2.refs_2_), channel_id=1, source_target_pairs={{0,2},{1,3},{2,0},{3,1},{4,6},{5,7},{6,4},{7,5},{8,10},{9,11},{10,... | collective-permute-start | bytes 835592 | tf_op jit(solution)/shard_map/ppermute | solution.py:386
  24.3 8.1 %collective-permute-done.8 = s32[96]{0:T(128)S(1)} collective-permute-done((s32[96]{0:T(128)S(1)}, s32[96]{0:T(128)S(1)}, u32[]{:S(2)}, u32[]{:S(2)}) %collective-permute-start.8) | collective-permute-done | bytes 416 | tf_op jit(solution)/shard_map/ppermute | solution.py:401
  32.4 1.6 %collective-permute-start.7 = (bf16[128,2176]{1,0:T(8,128)(2,1)S(1)}, bf16[128,2176]{1,0:T(8,128)(2,1)S(1)}, u32[]{:S(2)}, u32[]{:S(2)}) collective-permute-start(bf16[128,2176]{1,0:T(8,128)(2,1)S(1)} %pad_maximum_fusion.1), channel_id=1, source_target_pairs={{0,1},{1,0},{2,3},{3,2},{4,5},{5,4},{6,7},{7,6},{8,9},{9,8},{10,11... | collective-permute-start | bytes 1671176 | tf_op jit(solution)/shard_map/ppermute | solution.py:386
  34.0 0.6 collective-permute-start.6
  34.6 11.6 %match_near.1 = (bf16[1280,2176]{1,0:T(8,128)(2,1)S(1)}, f32[8,1280]{1,0:T(8,128)S(1)}, s16[64,2176]{1,0:T(8,128)(2,1)S(1)}, s16[64,2176]{1,0:T(8,128)(2,1)S(1)}...) custom-call(s32[2]{0:T(128)S(1)} %pad_add_fusion.1.quad_ref, ...), custom_call_target="tpu_custom_call" | custom-call | flops 15099494400 | bytes 5570560 | tf_op jit(solution)/shard_map/match_near/pallas_call | solution.py:345
  46.3 1.7 %collective-permute-done.6.far_ref = bf16[128,2176]{1,0:T(8,128)(2,1)S(1)} collective-permute-done((bf16[128,2176]{1,0:T(8,128)(2,1)S(1)}, bf16[128,2176]{1,0:T(8,128)(2,1)S(1)}, u32[]{:S(2)}, u32[]{:S(2)}) %collective-permute-start.6) | collective-permute-done | bytes 557088 | tf_op jit(solution)/shard_map/ppermute | solution.py:386
  48.0 1.5 %collective-permute-start.10 = (s16[64,2176]{1,0:T(8,128)(2,1)S(1)}, s16[64,2176]{1,0:T(8,128)(2,1)S(1)}, u32[]{:S(2)}, u32[]{:S(2)}) collective-permute-start(s16[64,2176]{1,0:T(8,128)(2,1)S(1)} %get-tuple-element.65), channel_id=1, source_target_pairs={{0,2},{1,3},{2,0},{3,1},{4,6},{5,7},{6,4},{7,5},{8,10},{9,11},{10,... | collective-permute-start | bytes 835592 | tf_op jit(solution)/shard_map/ppermute | solution.py:386
  50.0 4.4 %match_far.2 = (s16[64,2176]{1,0:T(8,128)(2,1)S(1)}, s16[64,2176]{1,0:T(8,128)(2,1)S(1)}) custom-call(bf16[128,2176]{1,0:T(8,128)(2,1)S(1)} %collective-permute-done.6.far_ref, bf16[1280,2176]{1,0:T(8,128)(2,1)S(1)} %get-tuple-element.69.held, f32[8,1280]{1,0:T(8,128)S(1)} %get-tuple-element.70.facts_ref), custom_call_target="tpu_custom_call" | custom-call | flops 5347737600 | bytes 5570560 | tf_op jit(solution)/shard_map/match_far/pallas_call | solution.py:362
  54.4 1.6 %collective-permute-start.12 = (s16[64,2176]{1,0:T(8,128)(2,1)S(1)}, s16[64,2176]{1,0:T(8,128)(2,1)S(1)}, u32[]{:S(2)}, u32[]{:S(2)}) collective-permute-start(s16[64,2176]{1,0:T(8,128)(2,1)S(1)} %get-tuple-element.72), channel_id=1, source_target_pairs={{0,2},{1,3},{2,0},{3,1},{4,6},{5,7},{6,4},{7,5},{8,10},{9,11},{10,... | collective-permute-start | bytes 835592 | tf_op jit(solution)/shard_map/ppermute | solution.py:386
  56.0 1.5 %collective-permute-done.11.refs_1_ = s16[64,2176]{1,0:T(8,128)(2,1)S(1)} collective-permute-done((s16[64,2176]{1,0:T(8,128)(2,1)S(1)}, s16[64,2176]{1,0:T(8,128)(2,1)S(1)}, u32[]{:S(2)}, u32[]{:S(2)}) %collective-permute-start.11) | collective-permute-done | bytes 278560 | tf_op jit(solution)/shard_map/ppermute | solution.py:386
  57.5 4.4 %match_far.3 = (s16[64,2176]{1,0:T(8,128)(2,1)S(1)}, s16[64,2176]{1,0:T(8,128)(2,1)S(1)}) custom-call(bf16[128,2176]{1,0:T(8,128)(2,1)S(1)} %collective-permute-done.7.far_ref, bf16[1280,2176]{1,0:T(8,128)(2,1)S(1)} %get-tuple-element.78.held, f32[8,1280]{1,0:T(8,128)S(1)} %get-tuple-element.79.facts_ref), custom_call_target="tpu_custom_call" | custom-call | flops 5347737600 | bytes 5570560 | tf_op jit(solution)/shard_map/match_far/pallas_call | solution.py:362
  61.9 1.6 %collective-permute-start.16 = (s16[64,2176]{1,0:T(8,128)(2,1)S(1)}, s16[64,2176]{1,0:T(8,128)(2,1)S(1)}, u32[]{:S(2)}, u32[]{:S(2)}) collective-permute-start(s16[64,2176]{1,0:T(8,128)(2,1)S(1)} %get-tuple-element.81), channel_id=1, source_target_pairs={{0,2},{1,3},{2,0},{3,1},{4,6},{5,7},{6,4},{7,5},{8,10},{9,11},{10,... | collective-permute-start | bytes 835592 | tf_op jit(solution)/shard_map/ppermute | solution.py:386
  63.9 1.6 %collective-permute-start.13 = (s16[64,2176]{1,0:T(8,128)(2,1)S(1)}, s16[64,2176]{1,0:T(8,128)(2,1)S(1)}, u32[]{:S(2)}, u32[]{:S(2)}) collective-permute-start(s16[64,2176]{1,0:T(8,128)(2,1)S(1)} %merge.4), channel_id=1, source_target_pairs={{0,1},{1,0},{2,3},{3,2},{4,5},{5,4},{6,7},{7,6},{8,9},{9,8},{10,11... | collective-permute-start | bytes 835592 | tf_op jit(solution)/shard_map/ppermute | solution.py:386
  65.5 6.0 %collective-permute-done.16.refs_1_ = s16[64,2176]{1,0:T(8,128)(2,1)S(1)} collective-permute-done((s16[64,2176]{1,0:T(8,128)(2,1)S(1)}, s16[64,2176]{1,0:T(8,128)(2,1)S(1)}, u32[]{:S(2)}, u32[]{:S(2)}) %collective-permute-start.16) | collective-permute-done | bytes 278560 | tf_op jit(solution)/shard_map/ppermute | solution.py:386
  72.8 0.7 collective-permute-start.14
  73.5 5.4 %collective-permute-start.15 = (s16[32,2176]{1,0:T(8,128)(2,1)S(1)}, s16[32,2176]{1,0:T(8,128)(2,1)S(1)}, u32[]{:S(2)}, u32[]{:S(2)}) collective-permute-start(s16[32,2176]{1,0:T(8,128)(2,1)S(1)} %get-tuple-element.74), channel_id=1, source_target_pairs={{0,16},{1,17},{2,18},{3,19},{4,20},{5,21},{6,22},{7,23},{16,24},{1... | collective-permute-start | bytes 417800 | tf_op jit(solution)/shard_map/ppermute | solution.py:398
  79.3 1.7 %collective-permute-start.18 = (s16[32,2176]{1,0:T(8,128)(2,1)S(1)}, s16[32,2176]{1,0:T(8,128)(2,1)S(1)}, u32[]{:S(2)}, u32[]{:S(2)}) collective-permute-start(s16[32,2176]{1,0:T(8,128)(2,1)S(1)} %get-tuple-element.82), channel_id=1, source_target_pairs={{4,0},{5,1},{6,2},{7,3},{0,4},{1,5},{2,6},{3,7},{20,8},{21,9},{22,... | collective-permute-start | bytes 417800 | tf_op jit(solution)/shard_map/ppermute | solution.py:398
  81.0 2.4 %collective-permute-start.19 = (s16[32,2176]{1,0:T(8,128)(2,1)S(1)}, s16[32,2176]{1,0:T(8,128)(2,1)S(1)}, u32[]{:S(2)}, u32[]{:S(2)}) collective-permute-start(s16[32,2176]{1,0:T(8,128)(2,1)S(1)} %get-tuple-element.83), channel_id=1, source_target_pairs={{4,16},{5,17},{6,18},{7,19},{0,20},{1,21},{2,22},{3,23},{20,24},{2... | collective-permute-start | bytes 417800 | tf_op jit(solution)/shard_map/ppermute | solution.py:398
  83.4 2.8 %collective-permute-done.15.refs_1_ = s16[32,2176]{1,0:T(8,128)(2,1)S(1)} collective-permute-done((s16[32,2176]{1,0:T(8,128)(2,1)S(1)}, s16[32,2176]{1,0:T(8,128)(2,1)S(1)}, u32[]{:S(2)}, u32[]{:S(2)}) %collective-permute-start.15) | collective-permute-done | bytes 139296 | tf_op jit(solution)/shard_map/ppermute | solution.py:398
  86.2 2.9 %collective-permute-done.18.refs_2_ = s16[32,2176]{1,0:T(8,128)(2,1)S(1)} collective-permute-done((s16[32,2176]{1,0:T(8,128)(2,1)S(1)}, s16[32,2176]{1,0:T(8,128)(2,1)S(1)}, u32[]{:S(2)}, u32[]{:S(2)}) %collective-permute-start.18) | collective-permute-done | bytes 139296 | tf_op jit(solution)/shard_map/ppermute | solution.py:398
  89.1 1.0 %finish.1 = (bf16[32,2048]{1,0:T(8,128)(2,1)}, f32[1,32]{1,0:T(1,128)}, f32[1,32]{1,0:T(1,128)}) custom-call(s16[32,2176]{1,0:T(8,128)(2,1)S(1)} %collective-permute-done.14.refs_0_, s16[32,2176]{1,0:T(8,128)(2,1)S(1)} %collective-permute-done.15.refs_1_, s16[32,2176]{1,0:T(8,128)(2,1)S(1)} %collective-permute-done.18.refs_2_, ...), custom_call_target="tpu_custom_call" | custom-call | tf_op jit(solution)/shard_map/finish/pallas_call | solution.py:179
  (33 shorter events, 3.8 us)
Async XLA Ops:
  0.6 1.8 %collective-permute-start = (bf16[32,2048]{1,0:T(8,128)(2,1)}, bf16[32,2048]{1,0:T(8,128)(2,1)S(1)}, u32[]{:S(2)}, u32[]{:S(2)}) collective-permute-start(bf16[32,2048]{1,0:T(8,128)(2,1)} %refs_0_.1), channel_id=1, source_target_pairs={{0,16},{16,0},{1,17},{17,1},{2,18},{18,2},{3,19},{19,3},{4,20},{20... | collective-permute-start | bytes 393224 | tf_op jit(solution)/shard_map/ppermute | solution.py:401
  1.1 1.3 %collective-permute-start.1 = (s32[32]{0:T(128)}, s32[32]{0:T(128)S(1)}, u32[]{:S(2)}, u32[]{:S(2)}) collective-permute-start(s32[32]{0:T(128)} %refs_2_.1), channel_id=1, source_target_pairs={{0,16},{16,0},{1,17},{17,1},{2,18},{18,2},{3,19},{19,3},{4,20},{20... | collective-permute-start | bytes 392 | tf_op jit(solution)/shard_map/ppermute | solution.py:401
  2.4 0.9 %copy-start = (bf16[32,2048]{1,0:T(8,128)(2,1)S(1)}, bf16[32,2048]{1,0:T(8,128)(2,1)}, u32[]{:S(2)}) copy-start(bf16[32,2048]{1,0:T(8,128)(2,1)} %refs_0_.1) | copy-start | bytes 393220
  3.3 0.7 copy-start.1
  4.0 14.4 %collective-permute-start.2 = (bf16[64,2176]{1,0:T(8,128)(2,1)S(1)}, bf16[64,2176]{1,0:T(8,128)(2,1)S(1)}, u32[]{:S(2)}, u32[]{:S(2)}) collective-permute-start(bf16[64,2176]{1,0:T(8,128)(2,1)S(1)} %pack.1), channel_id=1, source_target_pairs={{0,0},{1,1},{2,2},{3,3},{4,4},{5,5},{6,6},{7,7},{8,16},{9,17},{10,... | collective-permute-start | bytes 835592 | tf_op jit(solution)/shard_map/ppermute | solution.py:395
  4.7 13.7 %collective-permute-start.3 = (bf16[64,2176]{1,0:T(8,128)(2,1)S(1)}, bf16[64,2176]{1,0:T(8,128)(2,1)S(1)}, u32[]{:S(2)}, u32[]{:S(2)}) collective-permute-start(bf16[64,2176]{1,0:T(8,128)(2,1)S(1)} %pack.1), channel_id=1, source_target_pairs={{0,4},{1,5},{2,6},{3,7},{4,0},{5,1},{6,2},{7,3},{8,20},{9,21},{10,... | collective-permute-start | bytes 835592 | tf_op jit(solution)/shard_map/ppermute | solution.py:395
  7.7 2.8 %copy-start.2 = (bf16[1536,2048]{1,0:T(8,128)(2,1)S(1)}, bf16[1536,2048]{1,0:T(8,128)(2,1)}, u32[]{:S(2)}) copy-start(bf16[1536,2048]{1,0:T(8,128)(2,1)} %library_ref.1) | copy-start | bytes 18874372
  10.5 0.7 copy-start.3
  11.1 0.7 copy-start.4
  18.4 16.2 %collective-permute-start.9 = (bf16[1536,2176]{1,0:T(8,128)(2,1)}, bf16[1536,2176]{1,0:T(8,128)(2,1)}, u32[]{:S(2)}, u32[]{:S(2)}) collective-permute-start(bf16[1536,2176]{1,0:T(8,128)(2,1)} %get-tuple-element.54.refs_0_), channel_id=1, source_target_pairs={{0,16},{16,0},{1,17},{17,1},{2,18},{18,2},{3,19},{19,3},{4,20},{20... | collective-permute-start | bytes 20054024 | tf_op jit(solution)/shard_map/ppermute | solution.py:401
  22.0 10.4 %collective-permute-start.4 = (bf16[64,2176]{1,0:T(8,128)(2,1)S(1)}, bf16[64,2176]{1,0:T(8,128)(2,1)S(1)}, u32[]{:S(2)}, u32[]{:S(2)}) collective-permute-start(bf16[64,2176]{1,0:T(8,128)(2,1)S(1)} %collective-permute-done.2.refs_2_), channel_id=1, source_target_pairs={{0,2},{1,3},{2,0},{3,1},{4,6},{5,7},{6,4},{7,5},{8,10},{9,11},{10,... | collective-permute-start | bytes 835592 | tf_op jit(solution)/shard_map/ppermute | solution.py:386
  23.5 8.9 %collective-permute-start.5 = (bf16[64,2176]{1,0:T(8,128)(2,1)S(1)}, bf16[64,2176]{1,0:T(8,128)(2,1)S(1)}, u32[]{:S(2)}, u32[]{:S(2)}) collective-permute-start(bf16[64,2176]{1,0:T(8,128)(2,1)S(1)} %collective-permute-done.3.refs_4_), channel_id=1, source_target_pairs={{0,2},{1,3},{2,0},{3,1},{4,6},{5,7},{6,4},{7,5},{8,10},{9,11},{10,... | collective-permute-start | bytes 835592 | tf_op jit(solution)/shard_map/ppermute | solution.py:386
  24.1 8.2 %collective-permute-start.8 = (s32[96]{0:T(128)S(1)}, s32[96]{0:T(128)S(1)}, u32[]{:S(2)}, u32[]{:S(2)}) collective-permute-start(s32[96]{0:T(128)S(1)} %slice_reduce_fusion), channel_id=1, source_target_pairs={{0,16},{16,0},{1,17},{17,1},{2,18},{18,2},{3,19},{19,3},{4,20},{20... | collective-permute-start | bytes 1160 | tf_op jit(solution)/shard_map/ppermute | solution.py:401
  32.4 13.8 %collective-permute-start.7 = (bf16[128,2176]{1,0:T(8,128)(2,1)S(1)}, bf16[128,2176]{1,0:T(8,128)(2,1)S(1)}, u32[]{:S(2)}, u32[]{:S(2)}) collective-permute-start(bf16[128,2176]{1,0:T(8,128)(2,1)S(1)} %pad_maximum_fusion.1), channel_id=1, source_target_pairs={{0,1},{1,0},{2,3},{3,2},{4,5},{5,4},{6,7},{7,6},{8,9},{9,8},{10,11... | collective-permute-start | bytes 1671176 | tf_op jit(solution)/shard_map/ppermute | solution.py:386
  34.0 14.0 %collective-permute-start.6 = (bf16[128,2176]{1,0:T(8,128)(2,1)S(1)}, bf16[128,2176]{1,0:T(8,128)(2,1)S(1)}, u32[]{:S(2)}, u32[]{:S(2)}) collective-permute-start(bf16[128,2176]{1,0:T(8,128)(2,1)S(1)} %pad_maximum_fusion), channel_id=1, source_target_pairs={{0,1},{1,0},{2,3},{3,2},{4,5},{5,4},{6,7},{7,6},{8,9},{9,8},{10,11... | collective-permute-start | bytes 1671176 | tf_op jit(solution)/shard_map/ppermute | solution.py:386
  48.0 8.0 %collective-permute-start.10 = (s16[64,2176]{1,0:T(8,128)(2,1)S(1)}, s16[64,2176]{1,0:T(8,128)(2,1)S(1)}, u32[]{:S(2)}, u32[]{:S(2)}) collective-permute-start(s16[64,2176]{1,0:T(8,128)(2,1)S(1)} %get-tuple-element.65), channel_id=1, source_target_pairs={{0,2},{1,3},{2,0},{3,1},{4,6},{5,7},{6,4},{7,5},{8,10},{9,11},{10,... | collective-permute-start | bytes 835592 | tf_op jit(solution)/shard_map/ppermute | solution.py:386
  49.5 8.0 %collective-permute-start.11 = (s16[64,2176]{1,0:T(8,128)(2,1)S(1)}, s16[64,2176]{1,0:T(8,128)(2,1)S(1)}, u32[]{:S(2)}, u32[]{:S(2)}) collective-permute-start(s16[64,2176]{1,0:T(8,128)(2,1)S(1)} %get-tuple-element.66), channel_id=1, source_target_pairs={{0,2},{1,3},{2,0},{3,1},{4,6},{5,7},{6,4},{7,5},{8,10},{9,11},{10,... | collective-permute-start | bytes 835592 | tf_op jit(solution)/shard_map/ppermute | solution.py:386
  54.4 9.1 %collective-permute-start.12 = (s16[64,2176]{1,0:T(8,128)(2,1)S(1)}, s16[64,2176]{1,0:T(8,128)(2,1)S(1)}, u32[]{:S(2)}, u32[]{:S(2)}) collective-permute-start(s16[64,2176]{1,0:T(8,128)(2,1)S(1)} %get-tuple-element.72), channel_id=1, source_target_pairs={{0,2},{1,3},{2,0},{3,1},{4,6},{5,7},{6,4},{7,5},{8,10},{9,11},{10,... | collective-permute-start | bytes 835592 | tf_op jit(solution)/shard_map/ppermute | solution.py:386
  61.9 9.5 %collective-permute-start.16 = (s16[64,2176]{1,0:T(8,128)(2,1)S(1)}, s16[64,2176]{1,0:T(8,128)(2,1)S(1)}, u32[]{:S(2)}, u32[]{:S(2)}) collective-permute-start(s16[64,2176]{1,0:T(8,128)(2,1)S(1)} %get-tuple-element.81), channel_id=1, source_target_pairs={{0,2},{1,3},{2,0},{3,1},{4,6},{5,7},{6,4},{7,5},{8,10},{9,11},{10,... | collective-permute-start | bytes 835592 | tf_op jit(solution)/shard_map/ppermute | solution.py:386
  63.9 8.4 %collective-permute-start.13 = (s16[64,2176]{1,0:T(8,128)(2,1)S(1)}, s16[64,2176]{1,0:T(8,128)(2,1)S(1)}, u32[]{:S(2)}, u32[]{:S(2)}) collective-permute-start(s16[64,2176]{1,0:T(8,128)(2,1)S(1)} %merge.4), channel_id=1, source_target_pairs={{0,1},{1,0},{2,3},{3,2},{4,5},{5,4},{6,7},{7,6},{8,9},{9,8},{10,11... | collective-permute-start | bytes 835592 | tf_op jit(solution)/shard_map/ppermute | solution.py:386
  71.9 7.0 %collective-permute-start.17 = (s16[64,2176]{1,0:T(8,128)(2,1)S(1)}, s16[64,2176]{1,0:T(8,128)(2,1)S(1)}, u32[]{:S(2)}, u32[]{:S(2)}) collective-permute-start(s16[64,2176]{1,0:T(8,128)(2,1)S(1)} %merge.6), channel_id=1, source_target_pairs={{0,1},{1,0},{2,3},{3,2},{4,5},{5,4},{6,7},{7,6},{8,9},{9,8},{10,11... | collective-permute-start | bytes 835592 | tf_op jit(solution)/shard_map/ppermute | solution.py:386
  72.8 10.6 %collective-permute-start.14 = (s16[32,2176]{1,0:T(8,128)(2,1)S(1)}, s16[32,2176]{1,0:T(8,128)(2,1)S(1)}, u32[]{:S(2)}, u32[]{:S(2)}) collective-permute-start(s16[32,2176]{1,0:T(8,128)(2,1)S(1)} %get-tuple-element.73), channel_id=1, source_target_pairs={{0,0},{1,1},{2,2},{3,3},{4,4},{5,5},{6,6},{7,7},{16,8},{17,9},{18,... | collective-permute-start | bytes 417800 | tf_op jit(solution)/shard_map/ppermute | solution.py:398
  73.5 12.8 %collective-permute-start.15 = (s16[32,2176]{1,0:T(8,128)(2,1)S(1)}, s16[32,2176]{1,0:T(8,128)(2,1)S(1)}, u32[]{:S(2)}, u32[]{:S(2)}) collective-permute-start(s16[32,2176]{1,0:T(8,128)(2,1)S(1)} %get-tuple-element.74), channel_id=1, source_target_pairs={{0,16},{1,17},{2,18},{3,19},{4,20},{5,21},{6,22},{7,23},{16,24},{1... | collective-permute-start | bytes 417800 | tf_op jit(solution)/shard_map/ppermute | solution.py:398
  79.3 9.8 %collective-permute-start.18 = (s16[32,2176]{1,0:T(8,128)(2,1)S(1)}, s16[32,2176]{1,0:T(8,128)(2,1)S(1)}, u32[]{:S(2)}, u32[]{:S(2)}) collective-permute-start(s16[32,2176]{1,0:T(8,128)(2,1)S(1)} %get-tuple-element.82), channel_id=1, source_target_pairs={{4,0},{5,1},{6,2},{7,3},{0,4},{1,5},{2,6},{3,7},{20,8},{21,9},{22,... | collective-permute-start | bytes 417800 | tf_op jit(solution)/shard_map/ppermute | solution.py:398
  81.0 8.1 %collective-permute-start.19 = (s16[32,2176]{1,0:T(8,128)(2,1)S(1)}, s16[32,2176]{1,0:T(8,128)(2,1)S(1)}, u32[]{:S(2)}, u32[]{:S(2)}) collective-permute-start(s16[32,2176]{1,0:T(8,128)(2,1)S(1)} %get-tuple-element.83), channel_id=1, source_target_pairs={{4,16},{5,17},{6,18},{7,19},{0,20},{1,21},{2,22},{3,23},{20,24},{2... | collective-permute-start | bytes 417800 | tf_op jit(solution)/shard_map/ppermute | solution.py:398

commit v4 on v3

--- a/solution.py
+++ b/solution.py
@@ -420,17 +420,17 @@
     far = [send(w, 1, 2) for w in wide]
     quad = jnp.stack([core * quads + (at ^ (layer % quads)) for at in range(quads)]).astype(jnp.int32)
     matched = match_near(quad, firsts, near, second, libraries, per_bucket, blocks, buckets)
+    from_second = [send(second_sums, 2, 1) for _, _, _, second_sums in matched]
     far, matched = tie((far, matched))
-    from_second = [send(second_sums, 2, 1) for _, _, _, second_sums in matched]
     first_sums, from_corner = [], []
     for at, (held, facts, _, _) in enumerate(matched):
-        if at == quads - 1:
-            far[at], from_second = tie((far[at], from_second))
         sums, corner_sums = match_far(far[at], held, facts)
         first_sums.append(sums)
         from_corner.append(send(corner_sums, 2, 1))
     returned = []
     for at, (_, _, near_sums, _) in enumerate(matched):
+        if at == 0:
+            first_sums[0], from_second = tie((first_sums[0], from_second))
         (sums,) = merge([first_sums[at], from_corner[at]], 1)
         pieces = merge([near_sums, from_second[at], send(sums, 1, 2)], shards)
         returned += [collect(piece, at, d) for d, piece in enumerate(pieces)]

time: 91.2 us -> 88.7 us (0.973)
  waiting for transfers between devices: 24.2 us -> 21.4 us
  starting transfers between devices: 29.4 us -> 30.6 us
    ppermute x10, waiting for transfers between devices: 9.25 us -> 6.2 us  [send(): return lax.ppermute(value, ('query', 'lib'), pairs)]
    ppermute x10, starting transfers between devices: 11.4 us -> 12.6 us  [send(): return lax.ppermute(value, ('query', 'lib'), pairs)]
  transfers between devices with their start and end apart: 20 -> 20, of which waited for: 7 -> 5; matrix products, arithmetic and copies ran while one was open for 0% -> 0% of each run, Pallas kernels for 32% -> 32%
where the time goes in v4:
time: 88.7 us; the launch traced here: 88.4 us
  starting transfers between devices  30.6 us (34%)
  Pallas kernels  29.6 us (33%)
  waiting for transfers between devices  21.4 us (24%)
  local copies, waits for them, and re-layouts  5.83 us (7%)
    ppermute x10, starting transfers between devices, send(): return lax.ppermute(value, ('query', 'lib'), pairs)  12.6 us
    pallas_call x1, Pallas kernels, match_near(): pl.pallas_call(kernel, out_shape=outs * quads, in_specs=[smem, smem] + [p...  11.5 us
    ppermute x4, starting transfers between devices, collect(): lax.ppermute(value, ('query', 'lib'), [(b, a) for a, b in layer_pairs(str...  10.2 us
    ppermute x4, waiting for transfers between devices, swap(): lax.ppermute(value, 'query', [(c, c ^ distance) for c in range(shards)])  9.24 us
    pallas_call x2, Pallas kernels, match_far(): pl.pallas_call(rest_kernel, out_shape=(jax.ShapeDtypeStruct((rows // 2, w...  8.77 us
    pallas_call x1, Pallas kernels, sort_library(): pl.pallas_call(functools.partial(sort_kernel, buckets), out_shape=(jax.Sh...  6.6 us
    ppermute x10, waiting for transfers between devices, send(): return lax.ppermute(value, ('query', 'lib'), pairs)  6.2 us
    ppermute x4, waiting for transfers between devices, collect(): lax.ppermute(value, ('query', 'lib'), [(b, a) for a, b in layer_pairs(str...  5.95 us
  transfers between devices with their start and end apart: 20, of which 5 were waited for; matrix products, arithmetic and copies ran while one was open for 0% of the time, Pallas kernels for 32%

profile of v4, /device:TPU:0, one launch (start us, length us, event | category | flops | bytes accessed | tf_op | source)
XLA Modules:
  0.0 88.4 jit_solution(4724941046879265461)
XLA Ops:
  0.6 0.5 collective-permute-start
  1.2 1.2 %collective-permute-done.1.refs_3_ = s32[32]{0:T(128)S(1)} collective-permute-done((s32[32]{0:T(128)}, s32[32]{0:T(128)S(1)}, u32[]{:S(2)}, u32[]{:S(2)}) %collective-permute-start.1) | collective-permute-done | bytes 160 | tf_op jit(solution)/shard_map/ppermute | solution.py:401
  2.4 0.9 %copy-done = bf16[32,2048]{1,0:T(8,128)(2,1)S(1)} copy-done((bf16[32,2048]{1,0:T(8,128)(2,1)S(1)}, bf16[32,2048]{1,0:T(8,128)(2,1)}, u32[]{:S(2)}) %copy-start) | copy-done | bytes 131096
  3.3 0.7 copy-done.1
  4.0 0.7 collective-permute-start.2
  4.7 2.9 %collective-permute-start.3 = (bf16[64,2176]{1,0:T(8,128)(2,1)S(1)}, bf16[64,2176]{1,0:T(8,128)(2,1)S(1)}, u32[]{:S(2)}, u32[]{:S(2)}) collective-permute-start(bf16[64,2176]{1,0:T(8,128)(2,1)S(1)} %pack.1), channel_id=1, source_target_pairs={{0,4},{1,5},{2,6},{3,7},{4,0},{5,1},{6,2},{7,3},{8,20},{9,21},{10,... | collective-permute-start | bytes 835592 | tf_op jit(solution)/shard_map/ppermute | solution.py:395
  7.7 2.8 %copy-done.2 = bf16[1536,2048]{1,0:T(8,128)(2,1)S(1)} copy-done((bf16[1536,2048]{1,0:T(8,128)(2,1)S(1)}, bf16[1536,2048]{1,0:T(8,128)(2,1)}, u32[]{:S(2)}) %copy-start.2) | copy-done | bytes 6291480
  10.5 0.7 copy-done.3
  11.2 0.7 copy-done.4
  11.8 6.6 %sort_library.1 = (bf16[1536,2176]{1,0:T(8,128)(2,1)}, s32[96,128]{1,0:T(8,128)S(1)}) custom-call(bf16[1536]{0:T(1024)(128)(2,1)S(1)} %copy-done.4, s32[1536]{0:T(1024)S(1)} %copy-done.3, bf16[1536,2048]{1,0:T(8,128)(2,1)S(1)} %copy-done.2), custom_call_target="tpu_custom_call" | custom-call | flops 8053063680 | bytes 12582912 | tf_op jit(solution)/shard_map/sort_library/pallas_call | solution.py:89
  18.4 3.5 %collective-permute-start.9 = (bf16[1536,2176]{1,0:T(8,128)(2,1)}, bf16[1536,2176]{1,0:T(8,128)(2,1)}, u32[]{:S(2)}, u32[]{:S(2)}) collective-permute-start(bf16[1536,2176]{1,0:T(8,128)(2,1)} %get-tuple-element.52.refs_0_), channel_id=1, source_target_pairs={{0,16},{16,0},{1,17},{17,1},{2,18},{18,2},{3,19},{19,3},{4,20},{20... | collective-permute-start | bytes 20054024 | tf_op jit(solution)/shard_map/ppermute | solution.py:401
  22.0 1.5 %collective-permute-start.4 = (bf16[64,2176]{1,0:T(8,128)(2,1)S(1)}, bf16[64,2176]{1,0:T(8,128)(2,1)S(1)}, u32[]{:S(2)}, u32[]{:S(2)}) collective-permute-start(bf16[64,2176]{1,0:T(8,128)(2,1)S(1)} %collective-permute-done.2.refs_2_), channel_id=1, source_target_pairs={{0,2},{1,3},{2,0},{3,1},{4,6},{5,7},{6,4},{7,5},{8,10},{9,11},{10,... | collective-permute-start | bytes 835592 | tf_op jit(solution)/shard_map/ppermute | solution.py:386
  23.5 0.5 collective-permute-start.5
  24.3 8.1 %collective-permute-done.8 = s32[96]{0:T(128)S(1)} collective-permute-done((s32[96]{0:T(128)S(1)}, s32[96]{0:T(128)S(1)}, u32[]{:S(2)}, u32[]{:S(2)}) %collective-permute-start.8) | collective-permute-done | bytes 416 | tf_op jit(solution)/shard_map/ppermute | solution.py:401
  32.4 1.6 %collective-permute-start.7 = (bf16[128,2176]{1,0:T(8,128)(2,1)S(1)}, bf16[128,2176]{1,0:T(8,128)(2,1)S(1)}, u32[]{:S(2)}, u32[]{:S(2)}) collective-permute-start(bf16[128,2176]{1,0:T(8,128)(2,1)S(1)} %pad_maximum_fusion.1), channel_id=1, source_target_pairs={{0,1},{1,0},{2,3},{3,2},{4,5},{5,4},{6,7},{7,6},{8,9},{9,8},{10,11... | collective-permute-start | bytes 1671176 | tf_op jit(solution)/shard_map/ppermute | solution.py:386
  34.0 0.6 collective-permute-start.6
  34.6 11.5 %match_near.1 = (bf16[1280,2176]{1,0:T(8,128)(2,1)S(1)}, f32[8,1280]{1,0:T(8,128)S(1)}, s16[64,2176]{1,0:T(8,128)(2,1)S(1)}, s16[64,2176]{1,0:T(8,128)(2,1)S(1)}...) custom-call(s32[2]{0:T(128)S(1)} %pad_add_fusion.1.quad_ref, ...), custom_call_target="tpu_custom_call" | custom-call | flops 15099494400 | bytes 5570560 | tf_op jit(solution)/shard_map/match_near/pallas_call | solution.py:345
  46.2 1.7 %collective-permute-start.10 = (s16[64,2176]{1,0:T(8,128)(2,1)S(1)}, s16[64,2176]{1,0:T(8,128)(2,1)S(1)}, u32[]{:S(2)}, u32[]{:S(2)}) collective-permute-start(s16[64,2176]{1,0:T(8,128)(2,1)S(1)} %get-tuple-element.56), channel_id=1, source_target_pairs={{0,2},{1,3},{2,0},{3,1},{4,6},{5,7},{6,4},{7,5},{8,10},{9,11},{10,... | collective-permute-start | bytes 835592 | tf_op jit(solution)/shard_map/ppermute | solution.py:386
  48.3 4.4 %match_far.3 = (s16[64,2176]{1,0:T(8,128)(2,1)S(1)}, s16[64,2176]{1,0:T(8,128)(2,1)S(1)}) custom-call(bf16[128,2176]{1,0:T(8,128)(2,1)S(1)} %collective-permute-done.7.far_ref, bf16[1280,2176]{1,0:T(8,128)(2,1)S(1)} %get-tuple-element.74.held, f32[8,1280]{1,0:T(8,128)S(1)} %get-tuple-element.75.facts_ref), custom_call_target="tpu_custom_call" | custom-call | flops 5347737600 | bytes 5570560 | tf_op jit(solution)/shard_map/match_far/pallas_call | solution.py:362
  52.6 1.7 %collective-permute-start.16 = (s16[64,2176]{1,0:T(8,128)(2,1)S(1)}, s16[64,2176]{1,0:T(8,128)(2,1)S(1)}, u32[]{:S(2)}, u32[]{:S(2)}) collective-permute-start(s16[64,2176]{1,0:T(8,128)(2,1)S(1)} %get-tuple-element.77), channel_id=1, source_target_pairs={{0,2},{1,3},{2,0},{3,1},{4,6},{5,7},{6,4},{7,5},{8,10},{9,11},{10,... | collective-permute-start | bytes 835592 | tf_op jit(solution)/shard_map/ppermute | solution.py:386
  54.3 4.4 %match_far.2 = (s16[64,2176]{1,0:T(8,128)(2,1)S(1)}, s16[64,2176]{1,0:T(8,128)(2,1)S(1)}) custom-call(bf16[128,2176]{1,0:T(8,128)(2,1)S(1)} %collective-permute-done.6.far_ref, bf16[1280,2176]{1,0:T(8,128)(2,1)S(1)} %get-tuple-element.63.held, f32[8,1280]{1,0:T(8,128)S(1)} %get-tuple-element.64.facts_ref), custom_call_target="tpu_custom_call" | custom-call | flops 5347737600 | bytes 5570560 | tf_op jit(solution)/shard_map/match_far/pallas_call | solution.py:362
  58.7 0.5 collective-permute-start.12
  59.7 1.6 %collective-permute-start.17 = (s16[64,2176]{1,0:T(8,128)(2,1)S(1)}, s16[64,2176]{1,0:T(8,128)(2,1)S(1)}, u32[]{:S(2)}, u32[]{:S(2)}) collective-permute-start(s16[64,2176]{1,0:T(8,128)(2,1)S(1)} %merge.6), channel_id=1, source_target_pairs={{0,1},{1,0},{2,3},{3,2},{4,5},{5,4},{6,7},{7,6},{8,9},{9,8},{10,11... | collective-permute-start | bytes 835592 | tf_op jit(solution)/shard_map/ppermute | solution.py:386
  61.2 6.1 %collective-permute-done.12.refs_1_ = s16[64,2176]{1,0:T(8,128)(2,1)S(1)} collective-permute-done((s16[64,2176]{1,0:T(8,128)(2,1)S(1)}, s16[64,2176]{1,0:T(8,128)(2,1)S(1)}, u32[]{:S(2)}, u32[]{:S(2)}) %collective-permute-start.12) | collective-permute-done | bytes 278560 | tf_op jit(solution)/shard_map/ppermute | solution.py:386
  67.8 2.6 %collective-permute-start.13 = (s16[64,2176]{1,0:T(8,128)(2,1)S(1)}, s16[64,2176]{1,0:T(8,128)(2,1)S(1)}, u32[]{:S(2)}, u32[]{:S(2)}) collective-permute-start(s16[64,2176]{1,0:T(8,128)(2,1)S(1)} %merge.4), channel_id=1, source_target_pairs={{0,1},{1,0},{2,3},{3,2},{4,5},{5,4},{6,7},{7,6},{8,9},{9,8},{10,11... | collective-permute-start | bytes 835592 | tf_op jit(solution)/shard_map/ppermute | solution.py:386
  70.4 0.5 merge.7
  70.8 2.0 %collective-permute-start.18 = (s16[32,2176]{1,0:T(8,128)(2,1)S(1)}, s16[32,2176]{1,0:T(8,128)(2,1)S(1)}, u32[]{:S(2)}, u32[]{:S(2)}) collective-permute-start(s16[32,2176]{1,0:T(8,128)(2,1)S(1)} %get-tuple-element.78), channel_id=1, source_target_pairs={{4,0},{5,1},{6,2},{7,3},{0,4},{1,5},{2,6},{3,7},{20,8},{21,9},{22,... | collective-permute-start | bytes 417800 | tf_op jit(solution)/shard_map/ppermute | solution.py:398
  72.8 2.4 %collective-permute-start.19 = (s16[32,2176]{1,0:T(8,128)(2,1)S(1)}, s16[32,2176]{1,0:T(8,128)(2,1)S(1)}, u32[]{:S(2)}, u32[]{:S(2)}) collective-permute-start(s16[32,2176]{1,0:T(8,128)(2,1)S(1)} %get-tuple-element.79), channel_id=1, source_target_pairs={{4,16},{5,17},{6,18},{7,19},{0,20},{1,21},{2,22},{3,23},{20,24},{2... | collective-permute-start | bytes 417800 | tf_op jit(solution)/shard_map/ppermute | solution.py:398
  75.7 0.7 collective-permute-start.14
  76.4 5.1 %collective-permute-start.15 = (s16[32,2176]{1,0:T(8,128)(2,1)S(1)}, s16[32,2176]{1,0:T(8,128)(2,1)S(1)}, u32[]{:S(2)}, u32[]{:S(2)}) collective-permute-start(s16[32,2176]{1,0:T(8,128)(2,1)S(1)} %get-tuple-element.70), channel_id=1, source_target_pairs={{0,16},{1,17},{2,18},{3,19},{4,20},{5,21},{6,22},{7,23},{16,24},{1... | collective-permute-start | bytes 417800 | tf_op jit(solution)/shard_map/ppermute | solution.py:398
  81.5 5.9 %collective-permute-done.15.refs_1_ = s16[32,2176]{1,0:T(8,128)(2,1)S(1)} collective-permute-done((s16[32,2176]{1,0:T(8,128)(2,1)S(1)}, s16[32,2176]{1,0:T(8,128)(2,1)S(1)}, u32[]{:S(2)}, u32[]{:S(2)}) %collective-permute-start.15) | collective-permute-done | bytes 139296 | tf_op jit(solution)/shard_map/ppermute | solution.py:398
  87.5 1.0 %finish.1 = (bf16[32,2048]{1,0:T(8,128)(2,1)}, f32[1,32]{1,0:T(1,128)}, f32[1,32]{1,0:T(1,128)}) custom-call(s16[32,2176]{1,0:T(8,128)(2,1)S(1)} %collective-permute-done.14.refs_0_, s16[32,2176]{1,0:T(8,128)(2,1)S(1)} %collective-permute-done.15.refs_1_, s16[32,2176]{1,0:T(8,128)(2,1)S(1)} %collective-permute-done.18.refs_2_, ...), custom_call_target="tpu_custom_call" | custom-call | tf_op jit(solution)/shard_map/finish/pallas_call | solution.py:179
  (33 shorter events, 2.3 us)
Async XLA Ops:
  0.6 1.8 %collective-permute-start = (bf16[32,2048]{1,0:T(8,128)(2,1)}, bf16[32,2048]{1,0:T(8,128)(2,1)S(1)}, u32[]{:S(2)}, u32[]{:S(2)}) collective-permute-start(bf16[32,2048]{1,0:T(8,128)(2,1)} %refs_0_.1), channel_id=1, source_target_pairs={{0,16},{16,0},{1,17},{17,1},{2,18},{18,2},{3,19},{19,3},{4,20},{20... | collective-permute-start | bytes 393224 | tf_op jit(solution)/shard_map/ppermute | solution.py:401
  1.1 1.3 %collective-permute-start.1 = (s32[32]{0:T(128)}, s32[32]{0:T(128)S(1)}, u32[]{:S(2)}, u32[]{:S(2)}) collective-permute-start(s32[32]{0:T(128)} %refs_2_.1), channel_id=1, source_target_pairs={{0,16},{16,0},{1,17},{17,1},{2,18},{18,2},{3,19},{19,3},{4,20},{20... | collective-permute-start | bytes 392 | tf_op jit(solution)/shard_map/ppermute | solution.py:401
  2.4 0.9 %copy-start = (bf16[32,2048]{1,0:T(8,128)(2,1)S(1)}, bf16[32,2048]{1,0:T(8,128)(2,1)}, u32[]{:S(2)}) copy-start(bf16[32,2048]{1,0:T(8,128)(2,1)} %refs_0_.1) | copy-start | bytes 393220
  3.3 0.7 copy-start.1
  4.0 14.4 %collective-permute-start.2 = (bf16[64,2176]{1,0:T(8,128)(2,1)S(1)}, bf16[64,2176]{1,0:T(8,128)(2,1)S(1)}, u32[]{:S(2)}, u32[]{:S(2)}) collective-permute-start(bf16[64,2176]{1,0:T(8,128)(2,1)S(1)} %pack.1), channel_id=1, source_target_pairs={{0,0},{1,1},{2,2},{3,3},{4,4},{5,5},{6,6},{7,7},{8,16},{9,17},{10,... | collective-permute-start | bytes 835592 | tf_op jit(solution)/shard_map/ppermute | solution.py:395
  4.7 13.7 %collective-permute-start.3 = (bf16[64,2176]{1,0:T(8,128)(2,1)S(1)}, bf16[64,2176]{1,0:T(8,128)(2,1)S(1)}, u32[]{:S(2)}, u32[]{:S(2)}) collective-permute-start(bf16[64,2176]{1,0:T(8,128)(2,1)S(1)} %pack.1), channel_id=1, source_target_pairs={{0,4},{1,5},{2,6},{3,7},{4,0},{5,1},{6,2},{7,3},{8,20},{9,21},{10,... | collective-permute-start | bytes 835592 | tf_op jit(solution)/shard_map/ppermute | solution.py:395
  7.7 2.8 %copy-start.2 = (bf16[1536,2048]{1,0:T(8,128)(2,1)S(1)}, bf16[1536,2048]{1,0:T(8,128)(2,1)}, u32[]{:S(2)}) copy-start(bf16[1536,2048]{1,0:T(8,128)(2,1)} %library_ref.1) | copy-start | bytes 18874372
  10.5 0.7 copy-start.3
  11.1 0.7 copy-start.4
  18.4 16.2 %collective-permute-start.9 = (bf16[1536,2176]{1,0:T(8,128)(2,1)}, bf16[1536,2176]{1,0:T(8,128)(2,1)}, u32[]{:S(2)}, u32[]{:S(2)}) collective-permute-start(bf16[1536,2176]{1,0:T(8,128)(2,1)} %get-tuple-element.52.refs_0_), channel_id=1, source_target_pairs={{0,16},{16,0},{1,17},{17,1},{2,18},{18,2},{3,19},{19,3},{4,20},{20... | collective-permute-start | bytes 20054024 | tf_op jit(solution)/shard_map/ppermute | solution.py:401
  22.0 10.4 %collective-permute-start.4 = (bf16[64,2176]{1,0:T(8,128)(2,1)S(1)}, bf16[64,2176]{1,0:T(8,128)(2,1)S(1)}, u32[]{:S(2)}, u32[]{:S(2)}) collective-permute-start(bf16[64,2176]{1,0:T(8,128)(2,1)S(1)} %collective-permute-done.2.refs_2_), channel_id=1, source_target_pairs={{0,2},{1,3},{2,0},{3,1},{4,6},{5,7},{6,4},{7,5},{8,10},{9,11},{10,... | collective-permute-start | bytes 835592 | tf_op jit(solution)/shard_map/ppermute | solution.py:386
  23.5 8.9 %collective-permute-start.5 = (bf16[64,2176]{1,0:T(8,128)(2,1)S(1)}, bf16[64,2176]{1,0:T(8,128)(2,1)S(1)}, u32[]{:S(2)}, u32[]{:S(2)}) collective-permute-start(bf16[64,2176]{1,0:T(8,128)(2,1)S(1)} %collective-permute-done.3.refs_4_), channel_id=1, source_target_pairs={{0,2},{1,3},{2,0},{3,1},{4,6},{5,7},{6,4},{7,5},{8,10},{9,11},{10,... | collective-permute-start | bytes 835592 | tf_op jit(solution)/shard_map/ppermute | solution.py:386
  24.1 8.2 %collective-permute-start.8 = (s32[96]{0:T(128)S(1)}, s32[96]{0:T(128)S(1)}, u32[]{:S(2)}, u32[]{:S(2)}) collective-permute-start(s32[96]{0:T(128)S(1)} %slice_reduce_fusion), channel_id=1, source_target_pairs={{0,16},{16,0},{1,17},{17,1},{2,18},{18,2},{3,19},{19,3},{4,20},{20... | collective-permute-start | bytes 1160 | tf_op jit(solution)/shard_map/ppermute | solution.py:401
  32.4 15.8 %collective-permute-start.7 = (bf16[128,2176]{1,0:T(8,128)(2,1)S(1)}, bf16[128,2176]{1,0:T(8,128)(2,1)S(1)}, u32[]{:S(2)}, u32[]{:S(2)}) collective-permute-start(bf16[128,2176]{1,0:T(8,128)(2,1)S(1)} %pad_maximum_fusion.1), channel_id=1, source_target_pairs={{0,1},{1,0},{2,3},{3,2},{4,5},{5,4},{6,7},{7,6},{8,9},{9,8},{10,11... | collective-permute-start | bytes 1671176 | tf_op jit(solution)/shard_map/ppermute | solution.py:386
  34.0 14.2 %collective-permute-start.6 = (bf16[128,2176]{1,0:T(8,128)(2,1)S(1)}, bf16[128,2176]{1,0:T(8,128)(2,1)S(1)}, u32[]{:S(2)}, u32[]{:S(2)}) collective-permute-start(bf16[128,2176]{1,0:T(8,128)(2,1)S(1)} %pad_maximum_fusion), channel_id=1, source_target_pairs={{0,1},{1,0},{2,3},{3,2},{4,5},{5,4},{6,7},{7,6},{8,9},{9,8},{10,11... | collective-permute-start | bytes 1671176 | tf_op jit(solution)/shard_map/ppermute | solution.py:386
  46.2 15.1 %collective-permute-start.10 = (s16[64,2176]{1,0:T(8,128)(2,1)S(1)}, s16[64,2176]{1,0:T(8,128)(2,1)S(1)}, u32[]{:S(2)}, u32[]{:S(2)}) collective-permute-start(s16[64,2176]{1,0:T(8,128)(2,1)S(1)} %get-tuple-element.56), channel_id=1, source_target_pairs={{0,2},{1,3},{2,0},{3,1},{4,6},{5,7},{6,4},{7,5},{8,10},{9,11},{10,... | collective-permute-start | bytes 835592 | tf_op jit(solution)/shard_map/ppermute | solution.py:386
  47.8 13.4 %collective-permute-start.11 = (s16[64,2176]{1,0:T(8,128)(2,1)S(1)}, s16[64,2176]{1,0:T(8,128)(2,1)S(1)}, u32[]{:S(2)}, u32[]{:S(2)}) collective-permute-start(s16[64,2176]{1,0:T(8,128)(2,1)S(1)} %get-tuple-element.60), channel_id=1, source_target_pairs={{0,2},{1,3},{2,0},{3,1},{4,6},{5,7},{6,4},{7,5},{8,10},{9,11},{10,... | collective-permute-start | bytes 835592 | tf_op jit(solution)/shard_map/ppermute | solution.py:386
  52.6 6.6 %collective-permute-start.16 = (s16[64,2176]{1,0:T(8,128)(2,1)S(1)}, s16[64,2176]{1,0:T(8,128)(2,1)S(1)}, u32[]{:S(2)}, u32[]{:S(2)}) collective-permute-start(s16[64,2176]{1,0:T(8,128)(2,1)S(1)} %get-tuple-element.77), channel_id=1, source_target_pairs={{0,2},{1,3},{2,0},{3,1},{4,6},{5,7},{6,4},{7,5},{8,10},{9,11},{10,... | collective-permute-start | bytes 835592 | tf_op jit(solution)/shard_map/ppermute | solution.py:386
  58.7 8.6 %collective-permute-start.12 = (s16[64,2176]{1,0:T(8,128)(2,1)S(1)}, s16[64,2176]{1,0:T(8,128)(2,1)S(1)}, u32[]{:S(2)}, u32[]{:S(2)}) collective-permute-start(s16[64,2176]{1,0:T(8,128)(2,1)S(1)} %get-tuple-element.68), channel_id=1, source_target_pairs={{0,2},{1,3},{2,0},{3,1},{4,6},{5,7},{6,4},{7,5},{8,10},{9,11},{10,... | collective-permute-start | bytes 835592 | tf_op jit(solution)/shard_map/ppermute | solution.py:386
  59.7 10.7 %collective-permute-start.17 = (s16[64,2176]{1,0:T(8,128)(2,1)S(1)}, s16[64,2176]{1,0:T(8,128)(2,1)S(1)}, u32[]{:S(2)}, u32[]{:S(2)}) collective-permute-start(s16[64,2176]{1,0:T(8,128)(2,1)S(1)} %merge.6), channel_id=1, source_target_pairs={{0,1},{1,0},{2,3},{3,2},{4,5},{5,4},{6,7},{7,6},{8,9},{9,8},{10,11... | collective-permute-start | bytes 835592 | tf_op jit(solution)/shard_map/ppermute | solution.py:386
  67.8 7.5 %collective-permute-start.13 = (s16[64,2176]{1,0:T(8,128)(2,1)S(1)}, s16[64,2176]{1,0:T(8,128)(2,1)S(1)}, u32[]{:S(2)}, u32[]{:S(2)}) collective-permute-start(s16[64,2176]{1,0:T(8,128)(2,1)S(1)} %merge.4), channel_id=1, source_target_pairs={{0,1},{1,0},{2,3},{3,2},{4,5},{5,4},{6,7},{7,6},{8,9},{9,8},{10,11... | collective-permute-start | bytes 835592 | tf_op jit(solution)/shard_map/ppermute | solution.py:386
  70.8 10.7 %collective-permute-start.18 = (s16[32,2176]{1,0:T(8,128)(2,1)S(1)}, s16[32,2176]{1,0:T(8,128)(2,1)S(1)}, u32[]{:S(2)}, u32[]{:S(2)}) collective-permute-start(s16[32,2176]{1,0:T(8,128)(2,1)S(1)} %get-tuple-element.78), channel_id=1, source_target_pairs={{4,0},{5,1},{6,2},{7,3},{0,4},{1,5},{2,6},{3,7},{20,8},{21,9},{22,... | collective-permute-start | bytes 417800 | tf_op jit(solution)/shard_map/ppermute | solution.py:398
  72.8 8.7 %collective-permute-start.19 = (s16[32,2176]{1,0:T(8,128)(2,1)S(1)}, s16[32,2176]{1,0:T(8,128)(2,1)S(1)}, u32[]{:S(2)}, u32[]{:S(2)}) collective-permute-start(s16[32,2176]{1,0:T(8,128)(2,1)S(1)} %get-tuple-element.79), channel_id=1, source_target_pairs={{4,16},{5,17},{6,18},{7,19},{0,20},{1,21},{2,22},{3,23},{20,24},{2... | collective-permute-start | bytes 417800 | tf_op jit(solution)/shard_map/ppermute | solution.py:398
  75.7 5.8 %collective-permute-start.14 = (s16[32,2176]{1,0:T(8,128)(2,1)S(1)}, s16[32,2176]{1,0:T(8,128)(2,1)S(1)}, u32[]{:S(2)}, u32[]{:S(2)}) collective-permute-start(s16[32,2176]{1,0:T(8,128)(2,1)S(1)} %get-tuple-element.69), channel_id=1, source_target_pairs={{0,0},{1,1},{2,2},{3,3},{4,4},{5,5},{6,6},{7,7},{16,8},{17,9},{18,... | collective-permute-start | bytes 417800 | tf_op jit(solution)/shard_map/ppermute | solution.py:398
  76.4 11.1 %collective-permute-start.15 = (s16[32,2176]{1,0:T(8,128)(2,1)S(1)}, s16[32,2176]{1,0:T(8,128)(2,1)S(1)}, u32[]{:S(2)}, u32[]{:S(2)}) collective-permute-start(s16[32,2176]{1,0:T(8,128)(2,1)S(1)} %get-tuple-element.70), channel_id=1, source_target_pairs={{0,16},{1,17},{2,18},{3,19},{4,20},{5,21},{6,22},{7,23},{16,24},{1... | collective-permute-start | bytes 417800 | tf_op jit(solution)/shard_map/ppermute | solution.py:398

commit v5 on v4

--- a/solution.py
+++ b/solution.py
@@ -25,6 +25,10 @@
 MIB = 1 << 20
 
 
+def in_place(*arrays):
+    return [pltpu.with_memory_space_constraint(a, pltpu.HBM) for a in arrays]
+
+
 def split3(value):
     pieces = []
     for _ in range(3):
@@ -34,15 +38,27 @@
     return pieces
 
 
-def sort_kernel(buckets, time_ref, bucket_ref, library_ref, sorted_ref, first_ref, facts_ref):
-    count, bins = library_ref.shape
-    total = time_ref.shape[0]
-
-    @pl.when(pl.program_id(0) == 0)
+def sort_kernel(buckets, time_ref, bucket_ref, library_ref, sorted_ref, first_ref, times, bucket_ids, facts_ref, held, arrived):
+    step = pl.program_id(0)
+    total, bins = held.shape
+    count = sorted_ref.shape[0]
+    small = [
+        pltpu.make_async_copy(time_ref, times, arrived.at[0]),
+        pltpu.make_async_copy(bucket_ref, bucket_ids, arrived.at[1]),
+    ]
+
+    def block(n):
+        rows = pl.ds(pl.multiple_of(n * count, UNIT), count)
+        return pltpu.make_async_copy(library_ref.at[rows, :], held.at[rows, :], arrived.at[2 + n])
+
+    @pl.when(step == 0)
     def _():
-        facts_ref[0:1, :] = time_ref[...].astype(jnp.float32).reshape(1, total)
-        facts_ref[1:2, :] = bucket_ref[...].astype(jnp.float32).reshape(1, total)
-
+        for c in small + [block(n) for n in range(total // count)]:
+            c.start()
+        for c in small:
+            c.wait()
+        facts_ref[0:1, :] = times[...].astype(jnp.float32).reshape(1, total)
+        facts_ref[1:2, :] = bucket_ids[...].astype(jnp.float32).reshape(1, total)
 
     def earlier(n):
         order = [lax.broadcasted_iota(jnp.int32, (n, n), d) for d in range(2)]
@@ -67,7 +83,8 @@
         .astype(jnp.bfloat16)
     )
 
-    entries = library_ref[...]
+    block(step).wait()
+    entries = held[pl.ds(pl.multiple_of(step * count, UNIT), count), :]
     wide = entries.astype(jnp.float32)
     scale = lax.rsqrt(jnp.sum(wide * wide, axis=1, keepdims=True) / bins + EPSILON)
     which = lax.broadcasted_iota(jnp.int32, (LANES, count), 0)
@@ -93,20 +110,22 @@
             jax.ShapeDtypeStruct((blocks * buckets, LANES), jnp.int32),
         ),
         grid=(blocks,),
-        in_specs=[
-            pl.BlockSpec((total,), lambda n: (0,)),
-            pl.BlockSpec((total,), lambda n: (0,)),
-            pl.BlockSpec((count, bins), lambda n: (n, 0)),
-        ],
+        in_specs=[pl.BlockSpec(memory_space=pltpu.HBM)] * 3,
         out_specs=[
             pl.BlockSpec((count, bins + LANES), lambda n: (n, 0)),
             pl.BlockSpec((buckets, LANES), lambda n: (n, 0)),
         ],
-        scratch_shapes=[pltpu.VMEM((8, total), jnp.float32)],
+        scratch_shapes=[
+            pltpu.VMEM((total,), library_time.dtype),
+            pltpu.VMEM((total,), library_bucket.dtype),
+            pltpu.VMEM((8, total), jnp.float32),
+            pltpu.VMEM((total, bins), library.dtype),
+            pltpu.SemaphoreType.DMA((2 + blocks,)),
+        ],
         compiler_params=pltpu.CompilerParams(vmem_limit_bytes=SORT_MIB * MIB),
         cost_estimate=pl.CostEstimate(flops=5 * count * total * bins, bytes_accessed=4 * total * bins, transcendentals=0),
         name="sort_library",
-    )(library_time, library_bucket, library)
+    )(*in_place(library_time, library_bucket, library))
 
 
 def encode(out, rows, vector, k, total, time_sum):

time: 88.7 us -> 88.6 us (level)
  local copies, waits for them, and re-layouts: 5.83 us -> 1.66 us
  starting transfers between devices: 30.6 us -> 33.2 us
  Pallas kernels: 29.6 us -> 31.7 us
    unnamed x10 -> x4, local copies, waits for them, and re-layouts: 5.73 us -> 1.56 us
    pallas_call x1, Pallas kernels: 6.6 us -> 8.45 us  [sort_library(): pl.pallas_call(functools.partial(sort_kernel, buckets), out_shape=(jax.Sh...]
    ppermute x4, starting transfers between devices: 10.2 us -> 12 us  [collect(): lax.ppermute(value, ('query', 'lib'), [(b, a) for a, b in layer_pairs(str...]
  transfers between devices with their start and end apart: 20 -> 20, of which waited for: 5 -> 5; matrix products, arithmetic and copies ran while one was open for 0% -> 0% of each run, Pallas kernels for 32% -> 35%
where the time goes in v5:
time: 88.6 us; the launch traced here: 88.5 us
  starting transfers between devices  33.2 us (37%)
  Pallas kernels  31.7 us (36%)
  waiting for transfers between devices  20.9 us (24%)
  local copies, waits for them, and re-layouts  1.66 us (2%)
    ppermute x10, starting transfers between devices, send(): return lax.ppermute(value, ('query', 'lib'), pairs)  12.9 us
    ppermute x4, starting transfers between devices, collect(): lax.ppermute(value, ('query', 'lib'), [(b, a) for a, b in layer_pairs(str...  12 us
    pallas_call x1, Pallas kernels, match_near(): pl.pallas_call(kernel, out_shape=outs * quads, in_specs=[smem, smem] + [p...  11.7 us
    ppermute x4, waiting for transfers between devices, swap(): lax.ppermute(value, 'query', [(c, c ^ distance) for c in range(shards)])  9.24 us
    pallas_call x2, Pallas kernels, match_far(): pl.pallas_call(rest_kernel, out_shape=(jax.ShapeDtypeStruct((rows // 2, w...  8.76 us
    pallas_call x1, Pallas kernels, sort_library(): pl.pallas_call(functools.partial(sort_kernel, buckets), out_shape=(jax.Sh...  8.45 us
    ppermute x4, waiting for transfers between devices, collect(): lax.ppermute(value, ('query', 'lib'), [(b, a) for a, b in layer_pairs(str...  5.95 us
    ppermute x10, waiting for transfers between devices, send(): return lax.ppermute(value, ('query', 'lib'), pairs)  5.72 us
  transfers between devices with their start and end apart: 20, of which 5 were waited for; matrix products, arithmetic and copies ran while one was open for 0% of the time, Pallas kernels for 35%

profile of v5, /device:TPU:0, one launch (start us, length us, event | category | flops | bytes accessed | tf_op | source)
XLA Modules:
  0.0 88.5 jit_solution(14846169227759246208)
XLA Ops:
  0.6 0.5 collective-permute-start
  1.2 1.2 %collective-permute-done.1.refs_3_ = s32[32]{0:T(128)S(1)} collective-permute-done((s32[32]{0:T(128)}, s32[32]{0:T(128)S(1)}, u32[]{:S(2)}, u32[]{:S(2)}) %collective-permute-start.1) | collective-permute-done | bytes 160 | tf_op jit(solution)/shard_map/ppermute | solution.py:420
  2.4 0.9 %copy-done = bf16[32,2048]{1,0:T(8,128)(2,1)S(1)} copy-done((bf16[32,2048]{1,0:T(8,128)(2,1)S(1)}, bf16[32,2048]{1,0:T(8,128)(2,1)}, u32[]{:S(2)}) %copy-start) | copy-done | bytes 131096
  3.3 0.7 copy-done.1
  4.0 0.7 collective-permute-start.2
  4.7 2.9 %collective-permute-start.3 = (bf16[64,2176]{1,0:T(8,128)(2,1)S(1)}, bf16[64,2176]{1,0:T(8,128)(2,1)S(1)}, u32[]{:S(2)}, u32[]{:S(2)}) collective-permute-start(bf16[64,2176]{1,0:T(8,128)(2,1)S(1)} %pack.1), channel_id=1, source_target_pairs={{0,4},{1,5},{2,6},{3,7},{4,0},{5,1},{6,2},{7,3},{8,20},{9,21},{10,... | collective-permute-start | bytes 835592 | tf_op jit(solution)/shard_map/ppermute | solution.py:414
  7.7 8.4 %sort_library.1 = (bf16[1536,2176]{1,0:T(8,128)(2,1)}, s32[96,128]{1,0:T(8,128)S(1)}) custom-call(bf16[1536]{0:T(1024)(128)(2,1)} %time_ref.1, s32[1536]{0:T(1024)} %bucket_ref.1, bf16[1536,2048]{1,0:T(8,128)(2,1)} %library_ref.1), custom_call_target="tpu_custom_call" | custom-call | flops 8053063680 | bytes 12582912 | tf_op jit(solution)/shard_map/sort_library/pallas_call | solution.py:106
  16.1 4.1 %collective-permute-start.9 = (bf16[1536,2176]{1,0:T(8,128)(2,1)}, bf16[1536,2176]{1,0:T(8,128)(2,1)}, u32[]{:S(2)}, u32[]{:S(2)}) collective-permute-start(bf16[1536,2176]{1,0:T(8,128)(2,1)} %get-tuple-element.52.refs_0_), channel_id=1, source_target_pairs={{0,16},{16,0},{1,17},{17,1},{2,18},{18,2},{3,19},{19,3},{4,20},{20... | collective-permute-start | bytes 20054024 | tf_op jit(solution)/shard_map/ppermute | solution.py:420
  20.2 1.7 %collective-permute-start.4 = (bf16[64,2176]{1,0:T(8,128)(2,1)S(1)}, bf16[64,2176]{1,0:T(8,128)(2,1)S(1)}, u32[]{:S(2)}, u32[]{:S(2)}) collective-permute-start(bf16[64,2176]{1,0:T(8,128)(2,1)S(1)} %collective-permute-done.2.refs_2_), channel_id=1, source_target_pairs={{0,2},{1,3},{2,0},{3,1},{4,6},{5,7},{6,4},{7,5},{8,10},{9,11},{10,... | collective-permute-start | bytes 835592 | tf_op jit(solution)/shard_map/ppermute | solution.py:405
  22.5 8.1 %collective-permute-done.8 = s32[96]{0:T(128)S(1)} collective-permute-done((s32[96]{0:T(128)S(1)}, s32[96]{0:T(128)S(1)}, u32[]{:S(2)}, u32[]{:S(2)}) %collective-permute-start.8) | collective-permute-done | bytes 416 | tf_op jit(solution)/shard_map/ppermute | solution.py:420
  30.7 1.7 %collective-permute-start.7 = (bf16[128,2176]{1,0:T(8,128)(2,1)S(1)}, bf16[128,2176]{1,0:T(8,128)(2,1)S(1)}, u32[]{:S(2)}, u32[]{:S(2)}) collective-permute-start(bf16[128,2176]{1,0:T(8,128)(2,1)S(1)} %pad_maximum_fusion.1), channel_id=1, source_target_pairs={{0,1},{1,0},{2,3},{3,2},{4,5},{5,4},{6,7},{7,6},{8,9},{9,8},{10,11... | collective-permute-start | bytes 1671176 | tf_op jit(solution)/shard_map/ppermute | solution.py:405
  32.4 0.5 collective-permute-start.6
  32.9 11.7 %match_near.1 = (bf16[1280,2176]{1,0:T(8,128)(2,1)S(1)}, f32[8,1280]{1,0:T(8,128)S(1)}, s16[64,2176]{1,0:T(8,128)(2,1)S(1)}, s16[64,2176]{1,0:T(8,128)(2,1)S(1)}...) custom-call(s32[2]{0:T(128)S(1)} %pad_add_fusion.1.quad_ref, ...), custom_call_target="tpu_custom_call" | custom-call | flops 15099494400 | bytes 5570560 | tf_op jit(solution)/shard_map/match_near/pallas_call | solution.py:364
  44.6 1.5 %collective-permute-start.10 = (s16[64,2176]{1,0:T(8,128)(2,1)S(1)}, s16[64,2176]{1,0:T(8,128)(2,1)S(1)}, u32[]{:S(2)}, u32[]{:S(2)}) collective-permute-start(s16[64,2176]{1,0:T(8,128)(2,1)S(1)} %get-tuple-element.56), channel_id=1, source_target_pairs={{0,2},{1,3},{2,0},{3,1},{4,6},{5,7},{6,4},{7,5},{8,10},{9,11},{10,... | collective-permute-start | bytes 835592 | tf_op jit(solution)/shard_map/ppermute | solution.py:405
  46.1 0.6 collective-permute-start.11
  46.7 4.4 %match_far.3 = (s16[64,2176]{1,0:T(8,128)(2,1)S(1)}, s16[64,2176]{1,0:T(8,128)(2,1)S(1)}) custom-call(bf16[128,2176]{1,0:T(8,128)(2,1)S(1)} %collective-permute-done.7.far_ref, bf16[1280,2176]{1,0:T(8,128)(2,1)S(1)} %get-tuple-element.74.held, f32[8,1280]{1,0:T(8,128)S(1)} %get-tuple-element.75.facts_ref), custom_call_target="tpu_custom_call" | custom-call | flops 5347737600 | bytes 5570560 | tf_op jit(solution)/shard_map/match_far/pallas_call | solution.py:381
  51.1 1.5 %collective-permute-start.16 = (s16[64,2176]{1,0:T(8,128)(2,1)S(1)}, s16[64,2176]{1,0:T(8,128)(2,1)S(1)}, u32[]{:S(2)}, u32[]{:S(2)}) collective-permute-start(s16[64,2176]{1,0:T(8,128)(2,1)S(1)} %get-tuple-element.77), channel_id=1, source_target_pairs={{0,2},{1,3},{2,0},{3,1},{4,6},{5,7},{6,4},{7,5},{8,10},{9,11},{10,... | collective-permute-start | bytes 835592 | tf_op jit(solution)/shard_map/ppermute | solution.py:405
  52.6 4.4 %match_far.2 = (s16[64,2176]{1,0:T(8,128)(2,1)S(1)}, s16[64,2176]{1,0:T(8,128)(2,1)S(1)}) custom-call(bf16[128,2176]{1,0:T(8,128)(2,1)S(1)} %collective-permute-done.6.far_ref, bf16[1280,2176]{1,0:T(8,128)(2,1)S(1)} %get-tuple-element.63.held, f32[8,1280]{1,0:T(8,128)S(1)} %get-tuple-element.64.facts_ref), custom_call_target="tpu_custom_call" | custom-call | flops 5347737600 | bytes 5570560 | tf_op jit(solution)/shard_map/match_far/pallas_call | solution.py:381
  57.0 0.6 collective-permute-start.12
  57.7 0.4 merge.6
  58.1 1.7 %collective-permute-start.17 = (s16[64,2176]{1,0:T(8,128)(2,1)S(1)}, s16[64,2176]{1,0:T(8,128)(2,1)S(1)}, u32[]{:S(2)}, u32[]{:S(2)}) collective-permute-start(s16[64,2176]{1,0:T(8,128)(2,1)S(1)} %merge.6), channel_id=1, source_target_pairs={{0,1},{1,0},{2,3},{3,2},{4,5},{5,4},{6,7},{7,6},{8,9},{9,8},{10,11... | collective-permute-start | bytes 835592 | tf_op jit(solution)/shard_map/ppermute | solution.py:405
  59.8 5.6 %collective-permute-done.12.refs_1_ = s16[64,2176]{1,0:T(8,128)(2,1)S(1)} collective-permute-done((s16[64,2176]{1,0:T(8,128)(2,1)S(1)}, s16[64,2176]{1,0:T(8,128)(2,1)S(1)}, u32[]{:S(2)}, u32[]{:S(2)}) %collective-permute-start.12) | collective-permute-done | bytes 278560 | tf_op jit(solution)/shard_map/ppermute | solution.py:405
  65.5 0.4 merge.4
  65.9 2.8 %collective-permute-start.13 = (s16[64,2176]{1,0:T(8,128)(2,1)S(1)}, s16[64,2176]{1,0:T(8,128)(2,1)S(1)}, u32[]{:S(2)}, u32[]{:S(2)}) collective-permute-start(s16[64,2176]{1,0:T(8,128)(2,1)S(1)} %merge.4), channel_id=1, source_target_pairs={{0,1},{1,0},{2,3},{3,2},{4,5},{5,4},{6,7},{7,6},{8,9},{9,8},{10,11... | collective-permute-start | bytes 835592 | tf_op jit(solution)/shard_map/ppermute | solution.py:405
  68.6 0.5 merge.7
  69.1 3.5 %collective-permute-start.18 = (s16[32,2176]{1,0:T(8,128)(2,1)S(1)}, s16[32,2176]{1,0:T(8,128)(2,1)S(1)}, u32[]{:S(2)}, u32[]{:S(2)}) collective-permute-start(s16[32,2176]{1,0:T(8,128)(2,1)S(1)} %get-tuple-element.78), channel_id=1, source_target_pairs={{4,0},{5,1},{6,2},{7,3},{0,4},{1,5},{2,6},{3,7},{20,8},{21,9},{22,... | collective-permute-start | bytes 417800 | tf_op jit(solution)/shard_map/ppermute | solution.py:417
  72.6 2.7 %collective-permute-start.19 = (s16[32,2176]{1,0:T(8,128)(2,1)S(1)}, s16[32,2176]{1,0:T(8,128)(2,1)S(1)}, u32[]{:S(2)}, u32[]{:S(2)}) collective-permute-start(s16[32,2176]{1,0:T(8,128)(2,1)S(1)} %get-tuple-element.79), channel_id=1, source_target_pairs={{4,16},{5,17},{6,18},{7,19},{0,20},{1,21},{2,22},{3,23},{20,24},{2... | collective-permute-start | bytes 417800 | tf_op jit(solution)/shard_map/ppermute | solution.py:417
  75.3 0.5 merge.5
  75.8 0.7 collective-permute-start.14
  76.4 5.1 %collective-permute-start.15 = (s16[32,2176]{1,0:T(8,128)(2,1)S(1)}, s16[32,2176]{1,0:T(8,128)(2,1)S(1)}, u32[]{:S(2)}, u32[]{:S(2)}) collective-permute-start(s16[32,2176]{1,0:T(8,128)(2,1)S(1)} %get-tuple-element.70), channel_id=1, source_target_pairs={{0,16},{1,17},{2,18},{3,19},{4,20},{5,21},{6,22},{7,23},{16,24},{1... | collective-permute-start | bytes 417800 | tf_op jit(solution)/shard_map/ppermute | solution.py:417
  81.6 5.9 %collective-permute-done.15.refs_1_ = s16[32,2176]{1,0:T(8,128)(2,1)S(1)} collective-permute-done((s16[32,2176]{1,0:T(8,128)(2,1)S(1)}, s16[32,2176]{1,0:T(8,128)(2,1)S(1)}, u32[]{:S(2)}, u32[]{:S(2)}) %collective-permute-start.15) | collective-permute-done | bytes 139296 | tf_op jit(solution)/shard_map/ppermute | solution.py:417
  87.5 1.0 %finish.1 = (bf16[32,2048]{1,0:T(8,128)(2,1)}, f32[1,32]{1,0:T(1,128)}, f32[1,32]{1,0:T(1,128)}) custom-call(s16[32,2176]{1,0:T(8,128)(2,1)S(1)} %collective-permute-done.14.refs_0_, s16[32,2176]{1,0:T(8,128)(2,1)S(1)} %collective-permute-done.15.refs_1_, s16[32,2176]{1,0:T(8,128)(2,1)S(1)} %collective-permute-done.18.refs_2_, ...), custom_call_target="tpu_custom_call" | custom-call | tf_op jit(solution)/shard_map/finish/pallas_call | solution.py:198
  (27 shorter events, 1.0 us)
Async XLA Ops:
  0.6 1.8 %collective-permute-start = (bf16[32,2048]{1,0:T(8,128)(2,1)}, bf16[32,2048]{1,0:T(8,128)(2,1)S(1)}, u32[]{:S(2)}, u32[]{:S(2)}) collective-permute-start(bf16[32,2048]{1,0:T(8,128)(2,1)} %refs_0_.1), channel_id=1, source_target_pairs={{0,16},{16,0},{1,17},{17,1},{2,18},{18,2},{3,19},{19,3},{4,20},{20... | collective-permute-start | bytes 393224 | tf_op jit(solution)/shard_map/ppermute | solution.py:420
  1.1 1.3 %collective-permute-start.1 = (s32[32]{0:T(128)}, s32[32]{0:T(128)S(1)}, u32[]{:S(2)}, u32[]{:S(2)}) collective-permute-start(s32[32]{0:T(128)} %refs_2_.1), channel_id=1, source_target_pairs={{0,16},{16,0},{1,17},{17,1},{2,18},{18,2},{3,19},{19,3},{4,20},{20... | collective-permute-start | bytes 392 | tf_op jit(solution)/shard_map/ppermute | solution.py:420
  2.4 0.9 %copy-start = (bf16[32,2048]{1,0:T(8,128)(2,1)S(1)}, bf16[32,2048]{1,0:T(8,128)(2,1)}, u32[]{:S(2)}) copy-start(bf16[32,2048]{1,0:T(8,128)(2,1)} %refs_0_.1) | copy-start | bytes 393220
  3.3 0.7 copy-start.1
  4.0 12.1 %collective-permute-start.2 = (bf16[64,2176]{1,0:T(8,128)(2,1)S(1)}, bf16[64,2176]{1,0:T(8,128)(2,1)S(1)}, u32[]{:S(2)}, u32[]{:S(2)}) collective-permute-start(bf16[64,2176]{1,0:T(8,128)(2,1)S(1)} %pack.1), channel_id=1, source_target_pairs={{0,0},{1,1},{2,2},{3,3},{4,4},{5,5},{6,6},{7,7},{8,16},{9,17},{10,... | collective-permute-start | bytes 835592 | tf_op jit(solution)/shard_map/ppermute | solution.py:414
  4.7 11.4 %collective-permute-start.3 = (bf16[64,2176]{1,0:T(8,128)(2,1)S(1)}, bf16[64,2176]{1,0:T(8,128)(2,1)S(1)}, u32[]{:S(2)}, u32[]{:S(2)}) collective-permute-start(bf16[64,2176]{1,0:T(8,128)(2,1)S(1)} %pack.1), channel_id=1, source_target_pairs={{0,4},{1,5},{2,6},{3,7},{4,0},{5,1},{6,2},{7,3},{8,20},{9,21},{10,... | collective-permute-start | bytes 835592 | tf_op jit(solution)/shard_map/ppermute | solution.py:414
  16.1 16.7 %collective-permute-start.9 = (bf16[1536,2176]{1,0:T(8,128)(2,1)}, bf16[1536,2176]{1,0:T(8,128)(2,1)}, u32[]{:S(2)}, u32[]{:S(2)}) collective-permute-start(bf16[1536,2176]{1,0:T(8,128)(2,1)} %get-tuple-element.52.refs_0_), channel_id=1, source_target_pairs={{0,16},{16,0},{1,17},{17,1},{2,18},{18,2},{3,19},{19,3},{4,20},{20... | collective-permute-start | bytes 20054024 | tf_op jit(solution)/shard_map/ppermute | solution.py:420
  20.2 10.4 %collective-permute-start.4 = (bf16[64,2176]{1,0:T(8,128)(2,1)S(1)}, bf16[64,2176]{1,0:T(8,128)(2,1)S(1)}, u32[]{:S(2)}, u32[]{:S(2)}) collective-permute-start(bf16[64,2176]{1,0:T(8,128)(2,1)S(1)} %collective-permute-done.2.refs_2_), channel_id=1, source_target_pairs={{0,2},{1,3},{2,0},{3,1},{4,6},{5,7},{6,4},{7,5},{8,10},{9,11},{10,... | collective-permute-start | bytes 835592 | tf_op jit(solution)/shard_map/ppermute | solution.py:405
  21.8 8.8 %collective-permute-start.5 = (bf16[64,2176]{1,0:T(8,128)(2,1)S(1)}, bf16[64,2176]{1,0:T(8,128)(2,1)S(1)}, u32[]{:S(2)}, u32[]{:S(2)}) collective-permute-start(bf16[64,2176]{1,0:T(8,128)(2,1)S(1)} %collective-permute-done.3.refs_4_), channel_id=1, source_target_pairs={{0,2},{1,3},{2,0},{3,1},{4,6},{5,7},{6,4},{7,5},{8,10},{9,11},{10,... | collective-permute-start | bytes 835592 | tf_op jit(solution)/shard_map/ppermute | solution.py:405
  22.3 8.2 %collective-permute-start.8 = (s32[96]{0:T(128)S(1)}, s32[96]{0:T(128)S(1)}, u32[]{:S(2)}, u32[]{:S(2)}) collective-permute-start(s32[96]{0:T(128)S(1)} %slice_reduce_fusion), channel_id=1, source_target_pairs={{0,16},{16,0},{1,17},{17,1},{2,18},{18,2},{3,19},{19,3},{4,20},{20... | collective-permute-start | bytes 1160 | tf_op jit(solution)/shard_map/ppermute | solution.py:420
  30.7 16.0 %collective-permute-start.7 = (bf16[128,2176]{1,0:T(8,128)(2,1)S(1)}, bf16[128,2176]{1,0:T(8,128)(2,1)S(1)}, u32[]{:S(2)}, u32[]{:S(2)}) collective-permute-start(bf16[128,2176]{1,0:T(8,128)(2,1)S(1)} %pad_maximum_fusion.1), channel_id=1, source_target_pairs={{0,1},{1,0},{2,3},{3,2},{4,5},{5,4},{6,7},{7,6},{8,9},{9,8},{10,11... | collective-permute-start | bytes 1671176 | tf_op jit(solution)/shard_map/ppermute | solution.py:405
  32.4 14.3 %collective-permute-start.6 = (bf16[128,2176]{1,0:T(8,128)(2,1)S(1)}, bf16[128,2176]{1,0:T(8,128)(2,1)S(1)}, u32[]{:S(2)}, u32[]{:S(2)}) collective-permute-start(bf16[128,2176]{1,0:T(8,128)(2,1)S(1)} %pad_maximum_fusion), channel_id=1, source_target_pairs={{0,1},{1,0},{2,3},{3,2},{4,5},{5,4},{6,7},{7,6},{8,9},{9,8},{10,11... | collective-permute-start | bytes 1671176 | tf_op jit(solution)/shard_map/ppermute | solution.py:405
  44.6 15.2 %collective-permute-start.10 = (s16[64,2176]{1,0:T(8,128)(2,1)S(1)}, s16[64,2176]{1,0:T(8,128)(2,1)S(1)}, u32[]{:S(2)}, u32[]{:S(2)}) collective-permute-start(s16[64,2176]{1,0:T(8,128)(2,1)S(1)} %get-tuple-element.56), channel_id=1, source_target_pairs={{0,2},{1,3},{2,0},{3,1},{4,6},{5,7},{6,4},{7,5},{8,10},{9,11},{10,... | collective-permute-start | bytes 835592 | tf_op jit(solution)/shard_map/ppermute | solution.py:405
  46.1 13.7 %collective-permute-start.11 = (s16[64,2176]{1,0:T(8,128)(2,1)S(1)}, s16[64,2176]{1,0:T(8,128)(2,1)S(1)}, u32[]{:S(2)}, u32[]{:S(2)}) collective-permute-start(s16[64,2176]{1,0:T(8,128)(2,1)S(1)} %get-tuple-element.60), channel_id=1, source_target_pairs={{0,2},{1,3},{2,0},{3,1},{4,6},{5,7},{6,4},{7,5},{8,10},{9,11},{10,... | collective-permute-start | bytes 835592 | tf_op jit(solution)/shard_map/ppermute | solution.py:405
  51.1 6.6 %collective-permute-start.16 = (s16[64,2176]{1,0:T(8,128)(2,1)S(1)}, s16[64,2176]{1,0:T(8,128)(2,1)S(1)}, u32[]{:S(2)}, u32[]{:S(2)}) collective-permute-start(s16[64,2176]{1,0:T(8,128)(2,1)S(1)} %get-tuple-element.77), channel_id=1, source_target_pairs={{0,2},{1,3},{2,0},{3,1},{4,6},{5,7},{6,4},{7,5},{8,10},{9,11},{10,... | collective-permute-start | bytes 835592 | tf_op jit(solution)/shard_map/ppermute | solution.py:405
  57.0 8.5 %collective-permute-start.12 = (s16[64,2176]{1,0:T(8,128)(2,1)S(1)}, s16[64,2176]{1,0:T(8,128)(2,1)S(1)}, u32[]{:S(2)}, u32[]{:S(2)}) collective-permute-start(s16[64,2176]{1,0:T(8,128)(2,1)S(1)} %get-tuple-element.68), channel_id=1, source_target_pairs={{0,2},{1,3},{2,0},{3,1},{4,6},{5,7},{6,4},{7,5},{8,10},{9,11},{10,... | collective-permute-start | bytes 835592 | tf_op jit(solution)/shard_map/ppermute | solution.py:405
  58.1 10.5 %collective-permute-start.17 = (s16[64,2176]{1,0:T(8,128)(2,1)S(1)}, s16[64,2176]{1,0:T(8,128)(2,1)S(1)}, u32[]{:S(2)}, u32[]{:S(2)}) collective-permute-start(s16[64,2176]{1,0:T(8,128)(2,1)S(1)} %merge.6), channel_id=1, source_target_pairs={{0,1},{1,0},{2,3},{3,2},{4,5},{5,4},{6,7},{7,6},{8,9},{9,8},{10,11... | collective-permute-start | bytes 835592 | tf_op jit(solution)/shard_map/ppermute | solution.py:405
  65.9 9.4 %collective-permute-start.13 = (s16[64,2176]{1,0:T(8,128)(2,1)S(1)}, s16[64,2176]{1,0:T(8,128)(2,1)S(1)}, u32[]{:S(2)}, u32[]{:S(2)}) collective-permute-start(s16[64,2176]{1,0:T(8,128)(2,1)S(1)} %merge.4), channel_id=1, source_target_pairs={{0,1},{1,0},{2,3},{3,2},{4,5},{5,4},{6,7},{7,6},{8,9},{9,8},{10,11... | collective-permute-start | bytes 835592 | tf_op jit(solution)/shard_map/ppermute | solution.py:405
  69.1 12.5 %collective-permute-start.18 = (s16[32,2176]{1,0:T(8,128)(2,1)S(1)}, s16[32,2176]{1,0:T(8,128)(2,1)S(1)}, u32[]{:S(2)}, u32[]{:S(2)}) collective-permute-start(s16[32,2176]{1,0:T(8,128)(2,1)S(1)} %get-tuple-element.78), channel_id=1, source_target_pairs={{4,0},{5,1},{6,2},{7,3},{0,4},{1,5},{2,6},{3,7},{20,8},{21,9},{22,... | collective-permute-start | bytes 417800 | tf_op jit(solution)/shard_map/ppermute | solution.py:417
  72.6 9.0 %collective-permute-start.19 = (s16[32,2176]{1,0:T(8,128)(2,1)S(1)}, s16[32,2176]{1,0:T(8,128)(2,1)S(1)}, u32[]{:S(2)}, u32[]{:S(2)}) collective-permute-start(s16[32,2176]{1,0:T(8,128)(2,1)S(1)} %get-tuple-element.79), channel_id=1, source_target_pairs={{4,16},{5,17},{6,18},{7,19},{0,20},{1,21},{2,22},{3,23},{20,24},{2... | collective-permute-start | bytes 417800 | tf_op jit(solution)/shard_map/ppermute | solution.py:417
  75.8 5.8 %collective-permute-start.14 = (s16[32,2176]{1,0:T(8,128)(2,1)S(1)}, s16[32,2176]{1,0:T(8,128)(2,1)S(1)}, u32[]{:S(2)}, u32[]{:S(2)}) collective-permute-start(s16[32,2176]{1,0:T(8,128)(2,1)S(1)} %get-tuple-element.69), channel_id=1, source_target_pairs={{0,0},{1,1},{2,2},{3,3},{4,4},{5,5},{6,6},{7,7},{16,8},{17,9},{18,... | collective-permute-start | bytes 417800 | tf_op jit(solution)/shard_map/ppermute | solution.py:417
  76.4 11.1 %collective-permute-start.15 = (s16[32,2176]{1,0:T(8,128)(2,1)S(1)}, s16[32,2176]{1,0:T(8,128)(2,1)S(1)}, u32[]{:S(2)}, u32[]{:S(2)}) collective-permute-start(s16[32,2176]{1,0:T(8,128)(2,1)S(1)} %get-tuple-element.70), channel_id=1, source_target_pairs={{0,16},{1,17},{2,18},{3,19},{4,20},{5,21},{6,22},{7,23},{16,24},{1... | collective-permute-start | bytes 417800 | tf_op jit(solution)/shard_map/ppermute | solution.py:417
